TPU v7x, 32 devices: a whole 2x2x4 slice. The times are simulated.
32 devices in a mesh: grp: 8 (over z, x), seq: 4 (over y, core).
Axes of the slice: x: 2, y: 2, z: 4, core: 2. Of those that a mesh axis runs over, the one named last changes fastest.
Arguments:
- tokens: bfloat16 [4096, 768], P(('grp', 'seq')), may hold values from -6 to 6
- global_tokens: bfloat16 [512, 768], P('grp'), may hold values from -6 to 6
- neighbours: int32 [4096, 8], P(('grp', 'seq')), may hold values from 0 to 383
- token_ranks: int32 [2, 4096], P(None, ('grp', 'seq')), may hold values from 0 to 511
- membership: int32 [4096], P(('grp', 'seq')), may hold values from 0 to 63
- w_graph: bfloat16 [768, 768], replicated, may hold values from -0.625 to 0.625
- gain_one: float32 [768], replicated, may hold values from 0.5 to 1.5
- shift_one: float32 [768], replicated, may hold values from -1.75 to 1.75
- w_query: bfloat16 [768, 768], replicated, may hold values from -0.21875 to 0.21875
- w_key: bfloat16 [768, 768], replicated, may hold values from -0.21875 to 0.21875
- w_value: bfloat16 [768, 768], replicated, may hold values from -0.21875 to 0.21875
- rich_query: bfloat16 [64, 48], replicated, may hold values from -0.75 to 0.75
- rich_key: bfloat16 [64, 48], replicated, may hold values from -0.75 to 0.75
- w_out: bfloat16 [768, 768], replicated, may hold values from -1.25 to 1.25
- gain_two: float32 [768], replicated, may hold values from 0.5 to 1.5
- shift_two: float32 [768], replicated, may hold values from -1.75 to 1.75
- w_up: bfloat16 [768, 3072], replicated, may hold values from -0.21875 to 0.21875
- bias_up: float32 [3072], replicated, may hold values from -1.75 to 1.75
- w_down: bfloat16 [3072, 768], replicated, may hold values from -0.109375 to 0.109375
- bias_down: float32 [768], replicated, may hold values from -1.75 to 1.75
- cot_tokens: bfloat16 [4096, 768], P(('grp', 'seq')), may hold values from -6 to 6
- cot_global: bfloat16 [512, 768], P('grp'), may hold values from -6 to 6
Outputs:
- out_tokens: bfloat16 [4096, 768], P(('grp', 'seq'))
- out_global: bfloat16 [512, 768], P('grp')
- grad_tokens: float32 [4096, 768], P(('grp', 'seq'))
- grad_global: float32 [512, 768], P('grp')
- grad_w_graph: float32 [768, 768], P('seq')
- grad_gain_one: float32 [768], P('seq')
- grad_shift_one: float32 [768], P('seq')
- grad_w_query: float32 [768, 768], P('seq')
- grad_w_key: float32 [768, 768], P('seq')
- grad_w_value: float32 [768, 768], P('seq')
- grad_rich_query: float32 [64, 48], P('seq')
- grad_rich_key: float32 [64, 48], P('seq')
- grad_w_out: float32 [768, 768], P('seq')
- grad_gain_two: float32 [768], P('seq')
- grad_shift_two: float32 [768], P('seq')
- grad_w_up: float32 [768, 3072], P('seq')
- grad_bias_up: float32 [3072], P('seq')
- grad_w_down: float32 [3072, 768], P('seq')
- grad_bias_down: float32 [768], P('seq')
Inputs may be any that keep to these rules, and one draw needn't show every extreme that they name: neighbours[i, k] = n names position (i // 128) * 128 - 128 + n of i's sequence.
All inputs are finite; a program needn't handle non-finite values.
Results may differ from a plain program's by a relative error of at most 0.019.
Values may be sent and summed in bfloat16 or wider, within the bound.
No kernel may reach another device: no remote copies, remote signals or barrier semaphores. Data moves between devices by JAX's collectives and lax.ppermute only.
A program may use at most 192 MiB of HBM per device.

v0:
```python
import functools
import math

import jax
import jax.numpy as jnp
from jax import lax
from jax.experimental import pallas as pl
from jax.experimental.pallas import tpu as pltpu
from jax.sharding import PartitionSpec as P

D = 768
HEADS = 12
HEAD_DIM = 64
RADIUS = 128
GLOBALS = 64
NEIGH = 8
SEQ_TOKENS = 2048


EPSILON = 1e-05
PRECISE = lax.Precision.HIGHEST
MASKED = -1e30


def with_halo(cells, sides, width):
    for axis, dim in sides:
        count = lax.axis_size(axis)
        ends = count - 1
        head = lax.slice_in_dim(cells, 0, width, axis=dim)
        tail = lax.slice_in_dim(cells, cells.shape[dim] - width, cells.shape[dim], axis=dim)
        cells = jnp.concatenate(
            [
                lax.ppermute(tail, axis, [(i, (i + 1) % count) for i in range(ends)]),
                cells,
                lax.ppermute(head, axis, [((i + 1) % count, i) for i in range(ends)]),
            ],
            axis=dim,
        )
    return cells


def joined(array, axis, combine):
    everything = jax.tree.map(
        lambda part, kind: lax.all_gather(part.astype(kind), axis),
        array,
        (jnp.bfloat16, jnp.bfloat16, jnp.bfloat16),
    )

    def take(k):
        return jax.tree.map(lambda part, own: part[k].astype(own.dtype), everything, array)

    return lax.fori_loop(
        1, lax.axis_size(axis), lambda k, so_far: combine(so_far, take(k)), take(0)
    )


def shifted(block, axis, distance):
    devices = range(lax.axis_size(axis))
    route = [(i - distance, i) for i in devices if i - distance in devices]
    return lax.ppermute(block, axis, route)


def layer_norm(rows_in, gain_in, shift_in):
    row_mean = jnp.mean(rows_in, axis=-1, keepdims=True)
    centred = rows_in - row_mean
    variance = jnp.mean(centred * centred, axis=-1, keepdims=True)
    return centred * lax.rsqrt(variance + EPSILON) * gain_in + shift_in


def rich_part(a_block, b_window, rank_query, rank_key, log_norm):
    combined = None
    for coordinate in range(2):
        order_flag = (rank_query[coordinate][:, None] < rank_key[coordinate][None, :]).astype(
            jnp.float32
        )
        distance = (
            jnp.log1p(
                jnp.abs(rank_query[coordinate][:, None] - rank_key[coordinate][None, :]).astype(
                    jnp.float32
                )
            )
            / log_norm
        )
        order_logit = a_block[:, :, None, coordinate] + b_window[:, None, :, coordinate]
        centre = a_block[:, :, None, 2 + coordinate] + b_window[:, None, :, 2 + coordinate]
        pair_term = (
            order_flag * jax.nn.log_sigmoid(order_logit)
            + (1.0 - order_flag) * jax.nn.log_sigmoid(-order_logit)
            - 0.5 * (distance - centre) ** 2
        )
        combined = pair_term if combined is None else combined + pair_term
    return combined


def product(left, right):
    return jnp.dot(left, right, preferred_element_type=jnp.float32)


def product_left(left, right):
    return jnp.einsum("ta,tb->ab", left, right, preferred_element_type=jnp.float32)


def product_right(left, right):
    return jnp.einsum("tb,ab->ta", left, right, preferred_element_type=jnp.float32)


def local(
    tokens,
    global_tokens,
    neighbours,
    token_ranks,
    membership,
    w_graph,
    gain_one,
    shift_one,
    w_query,
    w_key,
    w_value,
    rich_query,
    rich_key,
    w_out,
    gain_two,
    shift_two,
    w_up,
    bias_up,
    w_down,
    bias_down,
    cot_tokens,
    cot_global,
):
    tok_count = tokens.shape[0]
    seq_count = lax.axis_size("seq")
    seq_index = lax.axis_index("seq")
    seq_len = min(SEQ_TOKENS, tok_count * seq_count)
    span = seq_len // tok_count
    group_seqs = global_tokens.shape[0] // GLOBALS
    seq_slot = seq_index // span
    seq_local = seq_index % span
    slot_flag = (jnp.arange(group_seqs, dtype=jnp.int32) == seq_slot).astype(jnp.float32)
    log_norm = math.log(1.0 + seq_len)
    score_scale = 1.0 / math.sqrt(HEAD_DIM)
    block_rows = min(512, tok_count)
    window = block_rows + 2 * RADIUS
    ext_count = tok_count + 2 * RADIUS
    first_flag = (seq_index == 0).astype(jnp.float32)
    own_pos = seq_local * tok_count + jnp.arange(tok_count, dtype=jnp.int32)
    ext_pos = seq_local * tok_count - RADIUS + jnp.arange(ext_count, dtype=jnp.int32)
    key_valid = (ext_pos >= 0) & (ext_pos < seq_len)

    def own_slot(array_in):
        return lax.dynamic_index_in_dim(array_in, seq_slot, 0, keepdims=False)

    def to_slots(array_in):
        return slot_flag.reshape((group_seqs,) + (1,) * array_in.ndim) * array_in[None]

    token_ext = with_halo(tokens, (("seq", 0),), RADIUS)
    token_ext = jnp.where(key_valid[:, None], token_ext, jnp.zeros_like(token_ext))
    flat_index = neighbours.reshape(-1)
    gathered = (
        jnp.take(token_ext, flat_index, axis=0).astype(jnp.float32).reshape(tok_count, NEIGH, D)
    )
    agg_low = jnp.mean(gathered, axis=1).astype(jnp.bfloat16)
    graph_pre = product(agg_low, w_graph)
    graph_out, graph_back = jax.vjp(jax.nn.gelu, graph_pre)
    super_rows = tokens.astype(jnp.float32) + graph_out
    normed_full, norm_back = jax.vjp(layer_norm, super_rows, gain_one, shift_one)
    normed = normed_full.astype(jnp.bfloat16)
    glob_in = global_tokens.astype(jnp.float32)
    glob_normed_full, glob_norm_back = jax.vjp(layer_norm, glob_in, gain_one, shift_one)
    glob_normed = glob_normed_full.astype(jnp.bfloat16)
    query = product(normed, w_query).astype(jnp.bfloat16)
    key_own = product(normed, w_key).astype(jnp.bfloat16)
    value_own = product(normed, w_value).astype(jnp.bfloat16)
    glob_query = (
        product(glob_normed, w_query)
        .astype(jnp.bfloat16)
        .reshape(group_seqs, GLOBALS, HEADS, HEAD_DIM)
    )
    glob_key = (
        product(glob_normed, w_key)
        .astype(jnp.bfloat16)
        .reshape(group_seqs, GLOBALS, HEADS, HEAD_DIM)
    )
    glob_value = (
        product(glob_normed, w_value)
        .astype(jnp.bfloat16)
        .reshape(group_seqs, GLOBALS, HEADS, HEAD_DIM)
    )
    glob_query_own = own_slot(glob_query)
    glob_key_own = own_slot(glob_key)
    glob_value_own = own_slot(glob_value)
    kv_ext = with_halo(jnp.concatenate([key_own, value_own], axis=1), (("seq", 0),), RADIUS)
    key_ext = kv_ext[:, :D].reshape(ext_count, HEADS, HEAD_DIM)
    value_ext = kv_ext[:, D:].reshape(ext_count, HEADS, HEAD_DIM)
    rank_ext = with_halo(token_ranks, (("seq", 1),), RADIUS)
    rich_q3 = rich_query.reshape(HEAD_DIM, HEADS, 4)
    rich_k3 = rich_key.reshape(HEAD_DIM, HEADS, 4)
    query_heads = query.reshape(tok_count, HEADS, HEAD_DIM)
    a_rows = jnp.einsum("the,ehc->htc", query_heads, rich_q3, preferred_element_type=jnp.float32)
    b_ext = jnp.einsum("the,ehc->htc", key_ext, rich_k3, preferred_element_type=jnp.float32)

    def block_scores():

        def rich_scores(left_rows, right_rows):
            return rich_part(left_rows, right_rows, token_ranks, rank_ext, log_norm)

        rich_vals, rich_back = jax.vjp(rich_scores, a_rows, b_ext)
        raw_scores = (
            jnp.einsum("qhe,khe->hqk", query_heads, key_ext, preferred_element_type=jnp.float32)
            * score_scale
        )
        pos_gap = own_pos[:, None] - ext_pos[None, :]
        key_mask = (jnp.abs(pos_gap) <= RADIUS) & key_valid[None, :]
        scores = jnp.where(key_mask[None], raw_scores + rich_vals, MASKED)
        glob_scores = (
            jnp.einsum(
                "qhe,ghe->hqg", query_heads, glob_key_own, preferred_element_type=jnp.float32
            )
            * score_scale
        )
        return (scores, glob_scores, rich_back, query_heads, key_ext)

    scored = block_scores()
    scores = scored[0]
    glob_scores = scored[1]
    row_top = jnp.maximum(jnp.max(scores, axis=-1), jnp.max(glob_scores, axis=-1))
    row_denom = jnp.sum(jnp.exp(scores - row_top[..., None]), axis=-1) + jnp.sum(
        jnp.exp(glob_scores - row_top[..., None]), axis=-1
    )
    log_total = row_top + jnp.log(row_denom)
    prob_rows = jnp.exp(scores - log_total[..., None]).astype(jnp.bfloat16)
    glob_probs = jnp.exp(glob_scores - log_total[..., None]).astype(jnp.bfloat16)
    attn_block = jnp.einsum(
        "hqk,khe->qhe", prob_rows, value_ext, preferred_element_type=jnp.float32
    ) + jnp.einsum("hqg,ghe->qhe", glob_probs, glob_value_own, preferred_element_type=jnp.float32)
    attn_parts = attn_block.reshape(block_rows, D)
    attn_rows = attn_parts.astype(jnp.bfloat16)
    member_mask = membership[None, :] == jnp.arange(GLOBALS, dtype=jnp.int32)[:, None]
    key_heads = key_ext[RADIUS : RADIUS + tok_count]
    value_heads = value_ext[RADIUS : RADIUS + tok_count]
    member_raw = (
        jnp.einsum("ghe,the->ght", glob_query_own, key_heads, preferred_element_type=jnp.float32)
        * score_scale
    )
    member_scores = jnp.where(member_mask[:, None, :], member_raw, MASKED)
    local_top = jnp.max(member_scores, axis=-1)
    member_exp = jnp.where(
        member_mask[:, None, :], jnp.exp(member_scores - local_top[..., None]), 0.0
    )
    local_sum = jnp.sum(member_exp, axis=-1)
    local_acc = jnp.einsum(
        "ght,the->ghe", member_exp, value_heads.astype(jnp.float32), precision=PRECISE
    )
    slot_top = jnp.where(slot_flag[:, None, None] > 0.5, local_top[None], MASKED)
    slot_sum = to_slots(local_sum)
    slot_acc = to_slots(local_acc)

    def combine_softmax(first_part, second_part):
        top_one, sum_one, acc_one = first_part
        top_two, sum_two, acc_two = second_part
        top_both = jnp.maximum(top_one, top_two)
        scale_one = jnp.exp(top_one - top_both)
        scale_two = jnp.exp(top_two - top_both)
        return (
            top_both,
            sum_one * scale_one + sum_two * scale_two,
            acc_one * scale_one[..., None] + acc_two * scale_two[..., None],
        )

    merged_top, merged_sum, merged_acc = joined(
        (slot_top, slot_sum, slot_acc), "seq", combine_softmax
    )
    self_scores = (
        jnp.einsum("sghe,skhe->sghk", glob_query, glob_key, preferred_element_type=jnp.float32)
        * score_scale
    )
    glob_top = jnp.maximum(merged_top, jnp.max(self_scores, axis=-1))
    self_exp = jnp.exp(self_scores - glob_top[..., None])
    merged_scale = jnp.exp(merged_top - glob_top)
    glob_denom = merged_sum * merged_scale + jnp.sum(self_exp, axis=-1)
    glob_lse = glob_top + jnp.log(glob_denom)
    glob_att_f = (
        merged_acc * merged_scale[..., None]
        + jnp.einsum("sghk,skhe->sghe", self_exp, glob_value.astype(jnp.float32), precision=PRECISE)
    ) / glob_denom[..., None]
    glob_attn = glob_att_f.reshape(group_seqs * GLOBALS, D).astype(jnp.bfloat16)
    y_one = super_rows + product(attn_rows, w_out)
    glob_y_one = glob_in + product(glob_attn, w_out)

    def feed_forward(rows_in):
        normed_two_full, back_two = jax.vjp(layer_norm, rows_in, gain_two, shift_two)
        normed_two = normed_two_full.astype(jnp.bfloat16)
        hidden_pre = product(normed_two, w_up) + bias_up
        hidden_full, gelu_back = jax.vjp(jax.nn.gelu, hidden_pre)
        hidden = hidden_full.astype(jnp.bfloat16)
        result = rows_in + product(hidden, w_down) + bias_down
        return (result, normed_two, hidden, back_two, gelu_back)

    def feed_back(cotangent, normed_two, hidden, back_two, gelu_back):
        cot_full = cotangent.astype(jnp.float32)
        grad_down = product_left(hidden, cotangent)
        grad_bias_d = jnp.sum(cot_full, axis=0)
        d_hidden = product_right(cotangent, w_down)
        d_pre = gelu_back(d_hidden)[0].astype(jnp.bfloat16)
        grad_up = product_left(normed_two, d_pre)
        grad_bias_u = jnp.sum(d_pre.astype(jnp.float32), axis=0)
        d_normed_two = product_right(d_pre, w_up)
        d_rows, grad_gain, grad_shift = back_two(d_normed_two)
        return (
            cot_full + d_rows,
            (grad_gain, grad_shift, grad_up, grad_bias_u, grad_down, grad_bias_d),
        )

    long_ff = feed_forward(y_one)
    glob_ff = feed_forward(glob_y_one)
    out_tokens = long_ff[0].astype(jnp.bfloat16)
    out_global = glob_ff[0].astype(jnp.bfloat16)
    d_y_one, long_mlp = feed_back(cot_tokens, long_ff[1], long_ff[2], long_ff[3], long_ff[4])
    glob_d_y_one, glob_mlp = feed_back(cot_global, glob_ff[1], glob_ff[2], glob_ff[3], glob_ff[4])
    mlp_grads = [
        local_part + first_flag * glob_part for local_part, glob_part in zip(long_mlp, glob_mlp)
    ]
    d_proj = d_y_one.astype(jnp.bfloat16)
    glob_d_proj = glob_d_y_one.astype(jnp.bfloat16)
    grad_out = product_left(attn_rows, d_proj) + first_flag * product_left(glob_attn, glob_d_proj)
    d_attn = product_right(d_proj, w_out).astype(jnp.bfloat16).reshape(tok_count, HEADS, HEAD_DIM)
    glob_d_attn = (
        product_right(glob_d_proj, w_out)
        .astype(jnp.bfloat16)
        .reshape(group_seqs, GLOBALS, HEADS, HEAD_DIM)
    )
    glob_d_attn_own = own_slot(glob_d_attn)
    rich_q3_full = rich_q3.astype(jnp.float32)
    rich_k3_full = rich_k3.astype(jnp.float32)
    d_key_ext = jnp.zeros((ext_count, HEADS, HEAD_DIM), jnp.float32)
    d_value_ext = jnp.zeros((ext_count, HEADS, HEAD_DIM), jnp.float32)
    scores, glob_scores, rich_back, q_part, key_win = block_scores()
    prob_full = jnp.exp(scores - log_total[..., None])
    glob_prob_full = jnp.exp(glob_scores - log_total[..., None])
    d_probs = jnp.einsum("qhe,khe->hqk", d_attn, value_ext, preferred_element_type=jnp.float32)
    glob_d_probs = jnp.einsum(
        "qhe,ghe->hqg", d_attn, glob_value_own, preferred_element_type=jnp.float32
    )
    row_delta = jnp.sum(prob_full * d_probs, axis=-1) + jnp.sum(
        glob_prob_full * glob_d_probs, axis=-1
    )
    d_scores = (prob_full * (d_probs - row_delta[..., None])).astype(jnp.bfloat16)
    glob_d_scores = (glob_prob_full * (glob_d_probs - row_delta[..., None])).astype(jnp.bfloat16)
    query_rich_grad, key_rich_grad = rich_back(d_scores.astype(jnp.float32))
    query_grad = (
        jnp.einsum("hqk,khe->qhe", d_scores, key_win, preferred_element_type=jnp.float32)
        + jnp.einsum(
            "hqg,ghe->qhe", glob_d_scores, glob_key_own, preferred_element_type=jnp.float32
        )
    ) * score_scale + jnp.einsum("hqc,ehc->qhe", query_rich_grad, rich_q3_full, precision=PRECISE)
    key_win_grad = jnp.einsum(
        "hqk,qhe->khe", d_scores, q_part, preferred_element_type=jnp.float32
    ) * score_scale + jnp.einsum("hkc,ehc->khe", key_rich_grad, rich_k3_full, precision=PRECISE)
    value_win_grad = jnp.einsum(
        "hqk,qhe->khe", prob_full.astype(jnp.bfloat16), d_attn, preferred_element_type=jnp.float32
    )
    d_key_ext = d_key_ext.at[0:window].add(key_win_grad)
    d_value_ext = d_value_ext.at[0:window].add(value_win_grad)
    glob_key_grad = (
        jnp.einsum("hqg,qhe->ghe", glob_d_scores, q_part, preferred_element_type=jnp.float32)
        * score_scale
    )
    glob_value_grad = jnp.einsum(
        "hqg,qhe->ghe",
        glob_prob_full.astype(jnp.bfloat16),
        d_attn,
        preferred_element_type=jnp.float32,
    )
    grad_rich_q = jnp.einsum(
        "qhe,hqc->ehc", q_part.astype(jnp.float32), query_rich_grad, precision=PRECISE
    )
    grad_rich_k = jnp.einsum(
        "khe,hkc->ehc", key_win.astype(jnp.float32), key_rich_grad, precision=PRECISE
    )
    query_grads = query_grad.reshape(block_rows, D)
    glob_delta = jnp.sum(glob_d_attn.astype(jnp.float32) * glob_att_f, axis=-1)
    glob_delta_own = own_slot(glob_delta)
    glob_lse_own = own_slot(glob_lse)
    member_probs = jnp.where(
        member_mask[:, None, :], jnp.exp(member_scores - glob_lse_own[..., None]), 0.0
    )
    member_d_probs = jnp.einsum(
        "ghe,the->ght", glob_d_attn_own, value_heads, preferred_element_type=jnp.float32
    )
    member_d_scores = (member_probs * (member_d_probs - glob_delta_own[..., None])).astype(
        jnp.bfloat16
    )
    glob_query_part = (
        jnp.einsum("ght,the->ghe", member_d_scores, key_heads, preferred_element_type=jnp.float32)
        * score_scale
    )
    own_key_extra = (
        jnp.einsum(
            "ght,ghe->the", member_d_scores, glob_query_own, preferred_element_type=jnp.float32
        )
        * score_scale
    )
    own_value_extra = jnp.einsum(
        "ght,ghe->the", member_probs, glob_d_attn_own.astype(jnp.float32), precision=PRECISE
    )
    d_key_ext = d_key_ext.at[RADIUS : RADIUS + tok_count].add(own_key_extra)
    d_value_ext = d_value_ext.at[RADIUS : RADIUS + tok_count].add(own_value_extra)
    grad_rims = jnp.concatenate(
        [d_key_ext.reshape(ext_count, D), d_value_ext.reshape(ext_count, D)], axis=1
    )
    from_above = shifted(grad_rims[:RADIUS].astype(jnp.bfloat16), "seq", -1).astype(jnp.float32)
    from_below = shifted(grad_rims[tok_count + RADIUS :].astype(jnp.bfloat16), "seq", 1).astype(
        jnp.float32
    )
    kv_grad = grad_rims[RADIUS : RADIUS + tok_count]
    kv_grad = kv_grad.at[:RADIUS].add(from_below).at[tok_count - RADIUS :].add(from_above)
    summed_query, summed_key, summed_value = (
        lax.psum(to_slots(glob_query_part).astype(jnp.bfloat16), "seq").astype(jnp.float32),
        lax.psum(to_slots(glob_key_grad).astype(jnp.bfloat16), "seq").astype(jnp.float32),
        lax.psum(to_slots(glob_value_grad).astype(jnp.bfloat16), "seq").astype(jnp.float32),
    )
    self_probs = jnp.exp(self_scores - glob_lse[..., None])
    self_d_probs = jnp.einsum(
        "sghe,skhe->sghk", glob_d_attn, glob_value, preferred_element_type=jnp.float32
    )
    self_d_scores = (self_probs * (self_d_probs - glob_delta[..., None])).astype(jnp.bfloat16)
    glob_rows_total = group_seqs * GLOBALS
    glob_d_query = (
        (
            summed_query
            + jnp.einsum(
                "sghk,skhe->sghe", self_d_scores, glob_key, preferred_element_type=jnp.float32
            )
            * score_scale
        )
        .astype(jnp.bfloat16)
        .reshape(glob_rows_total, D)
    )
    glob_d_key = (
        (
            summed_key
            + jnp.einsum(
                "sghk,sghe->skhe", self_d_scores, glob_query, preferred_element_type=jnp.float32
            )
            * score_scale
        )
        .astype(jnp.bfloat16)
        .reshape(glob_rows_total, D)
    )
    glob_d_value = (
        (
            summed_value
            + jnp.einsum(
                "sghk,sghe->skhe", self_probs, glob_d_attn.astype(jnp.float32), precision=PRECISE
            )
        )
        .astype(jnp.bfloat16)
        .reshape(glob_rows_total, D)
    )
    d_query = query_grads.astype(jnp.bfloat16)
    d_key = kv_grad[:, :D].astype(jnp.bfloat16)
    d_value = kv_grad[:, D:].astype(jnp.bfloat16)
    grad_query = product_left(normed, d_query) + first_flag * product_left(
        glob_normed, glob_d_query
    )
    grad_key = product_left(normed, d_key) + first_flag * product_left(glob_normed, glob_d_key)
    grad_value = product_left(normed, d_value) + first_flag * product_left(
        glob_normed, glob_d_value
    )
    d_normed = (
        product_right(d_query, w_query)
        + product_right(d_key, w_key)
        + product_right(d_value, w_value)
    )
    glob_d_normed = (
        product_right(glob_d_query, w_query)
        + product_right(glob_d_key, w_key)
        + product_right(glob_d_value, w_value)
    )
    d_super_norm, grad_gain_one, grad_shift_one = norm_back(d_normed)
    d_super = d_y_one + d_super_norm
    glob_d_norm, glob_gain_one, glob_shift_one = glob_norm_back(glob_d_normed)
    grad_global = glob_d_y_one + glob_d_norm
    grad_gain_one = grad_gain_one + first_flag * glob_gain_one
    grad_shift_one = grad_shift_one + first_flag * glob_shift_one
    d_graph_pre = graph_back(d_super)[0].astype(jnp.bfloat16)
    grad_graph = product_left(agg_low, d_graph_pre)
    d_agg = product_right(d_graph_pre, w_graph) / NEIGH
    d_token_ext = (
        jnp.zeros((ext_count, D), jnp.float32).at[flat_index].add(jnp.repeat(d_agg, NEIGH, axis=0))
    )
    d_token_ext = jnp.where(key_valid[:, None], d_token_ext, 0.0)
    token_above = shifted(d_token_ext[:RADIUS].astype(jnp.bfloat16), "seq", -1).astype(jnp.float32)
    token_below = shifted(d_token_ext[tok_count + RADIUS :].astype(jnp.bfloat16), "seq", 1).astype(
        jnp.float32
    )
    own_grad = (
        d_token_ext[RADIUS : RADIUS + tok_count]
        .at[:RADIUS]
        .add(token_below)
        .at[tok_count - RADIUS :]
        .add(token_above)
    )
    grad_tokens = d_super + own_grad
    weight_grads = (
        grad_graph,
        grad_gain_one,
        grad_shift_one,
        grad_query,
        grad_key,
        grad_value,
        grad_rich_q.reshape(HEAD_DIM, 4 * HEADS),
        grad_rich_k.reshape(HEAD_DIM, 4 * HEADS),
        grad_out,
        mlp_grads[0],
        mlp_grads[1],
        mlp_grads[2],
        mlp_grads[3],
        mlp_grads[4],
        mlp_grads[5],
    )
    pieces = [weight_grad.reshape(seq_count, -1) for weight_grad in weight_grads]
    packed = jnp.concatenate(pieces, axis=1)
    group_count = lax.axis_size("grp")
    received = lax.all_to_all(
        packed.astype(jnp.bfloat16), "seq", split_axis=0, concat_axis=0, tiled=True
    ).astype(packed.dtype)
    group_total = jnp.sum(received, axis=0).reshape(group_count, -1)
    crossed = lax.all_to_all(
        group_total.astype(jnp.bfloat16), "grp", split_axis=0, concat_axis=0, tiled=True
    ).astype(group_total.dtype)
    final_part = jnp.sum(crossed, axis=0)
    flat_sum = lax.all_gather(final_part.astype(jnp.bfloat16), "grp", axis=0, tiled=True).astype(
        final_part.dtype
    )
    results = []
    offset = 0
    for weight_grad in weight_grads:
        part_len = weight_grad.size // seq_count
        results.append(
            flat_sum[offset : offset + part_len].reshape(
                (weight_grad.shape[0] // seq_count,) + weight_grad.shape[1:]
            )
        )
        offset = offset + part_len
    return (
        out_tokens,
        out_global,
        grad_tokens,
        grad_global,
        results[0],
        results[1],
        results[2],
        results[3],
        results[4],
        results[5],
        results[6],
        results[7],
        results[8],
        results[9],
        results[10],
        results[11],
        results[12],
        results[13],
        results[14],
    )


SEQ_WAYS = 4
GRP_WAYS = 8
OWN_HEADS = HEADS // SEQ_WAYS
OWN = D // SEQ_WAYS
FF = 3072
FF_OWN = FF // SEQ_WAYS
TOK = 128
ROWS = SEQ_WAYS * TOK
ALL = ROWS + GLOBALS
GLOB_OWN = GLOBALS // SEQ_WAYS
CHUNK = TOK + GLOB_OWN
PIECE = OWN // GRP_WAYS
BAND = SEQ_WAYS * PIECE
WIN = TOK + 2 * RADIUS
PAD = ROWS + 2 * RADIUS
BF = jnp.bfloat16
F32 = jnp.float32
GELU_SCALE = math.sqrt(2.0 / math.pi)
GELU_CUBE = 0.044715
LOG_NORM = math.log(1.0 + ROWS)
SCORE_SCALE = 1.0 / math.sqrt(HEAD_DIM)
CORE_SWAP = [(0, 1), (1, 0), (2, 3), (3, 2)]
Y_SWAP = [(0, 2), (2, 0), (1, 3), (3, 1)]
X_SWAP = [(g, g ^ 1) for g in range(GRP_WAYS)]
Z_NEAR = [(g, g ^ 2) for g in range(GRP_WAYS)]
Z_FAR = [(g, g ^ 4) for g in range(GRP_WAYS)]
HALF_TOK = ROWS // 2
HALF_GLOB = GLOBALS // 2
HALF = HALF_TOK + HALF_GLOB
SEND = CHUNK + 32
CODED = D + 128
WIDE = 640
GRAPH_ROWS = 32
X_PAIRS = ((0, 1), (2, 3), (4, 5), (6, 7))
KERNEL_COST = 60_000_000_000
RICH = OWN_HEADS * 2 * 4


def nn(left, right):
    return lax.dot_general(left, right, (((1,), (0,)), ((), ())), preferred_element_type=F32)


def nt(left, right):
    return lax.dot_general(left, right, (((1,), (1,)), ((), ())), preferred_element_type=F32)


def tn(left, right):
    return lax.dot_general(left, right, (((0,), (0,)), ((), ())), preferred_element_type=F32)


def load(source, target, sem):
    copy = pltpu.make_async_copy(source, target, sem)
    copy.start()
    return copy


def pick(stacked, index):
    return lax.dynamic_index_in_dim(stacked, index, 0, keepdims=False)


def tie(*values):
    return lax.optimization_barrier(values)


def reach_seq(block):
    return lax.ppermute(block, "seq", CORE_SWAP), lax.ppermute(block, "seq", Y_SWAP)


def gather_seq(block):
    beside, across = reach_seq(block)
    return [block, beside, across, lax.ppermute(across, "seq", CORE_SWAP)]


def turn_core(chunks):
    me = lax.axis_index("seq")
    return lax.ppermute(jnp.stack([pick(chunks, me ^ 1), pick(chunks, me ^ 3)]), "seq", CORE_SWAP)


def turn_y(chunks, came):
    return jnp.stack([pick(chunks, lax.axis_index("seq") ^ 2), came[1]])


def turned(chunks, came, far):
    mine = pick(chunks, lax.axis_index("seq"))
    return jnp.concatenate([mine, came[0], far[0], far[1]], axis=0)


def added(kept, came):
    return (kept.astype(F32) + came.astype(F32)).astype(BF)


def swap_x(sent):
    return lax.ppermute(sent, "grp", X_SWAP)


def swap_near(sent):
    return lax.ppermute(sent, "grp", Z_NEAR)


def swap_far(sent):
    return lax.ppermute(sent, "grp", Z_FAR)


def halves(kept, came, bit):
    grid = added(kept, came).reshape((-1, 2) + kept.shape[1:])
    mine = lax.dynamic_index_in_dim(grid, bit, 1, keepdims=False)
    return mine, lax.dynamic_index_in_dim(grid, 1 - bit, 1, keepdims=False)


def row_stats(rows_in):
    centred = rows_in - jnp.mean(rows_in, axis=-1, keepdims=True)
    scale = lax.rsqrt(jnp.mean(centred * centred, axis=-1, keepdims=True) + EPSILON)
    return centred * scale, scale


def norm_back(cotangent, gain, rows_in):
    hat, scale = row_stats(rows_in)
    scaled = cotangent * gain
    back = scale * (
        scaled
        - jnp.mean(scaled, axis=-1, keepdims=True)
        - hat * jnp.mean(scaled * hat, axis=-1, keepdims=True)
    )
    return (
        back,
        jnp.sum(cotangent * hat, axis=0, keepdims=True),
        jnp.sum(cotangent, axis=0, keepdims=True),
    )


def gelu_parts(pre):
    square = pre * pre
    bent = jnp.tanh(GELU_SCALE * pre * (1.0 + GELU_CUBE * square))
    half = 0.5 * (1.0 + bent)
    slope = half + 0.5 * pre * (1.0 - bent * bent) * (
        GELU_SCALE * (1.0 + 3.0 * GELU_CUBE * square)
    )
    return pre * half, slope


def counts_of(neigh, first, width):
    spots = (lax.broadcasted_iota(jnp.int32, (neigh.shape[0], width), 1) + first).astype(F32)
    total = jnp.zeros((neigh.shape[0], width), F32)
    for k in range(NEIGH):
        total = total + jnp.where(neigh[:, k : k + 1] == spots, 1.0, 0.0)
    return total.astype(BF)


def as_row(ref):
    return ref[...].reshape(1, ref.shape[0])


def own_window(me):
    return pl.ds(pl.multiple_of(lax.div(3 * me, 2) * 128, 128), 256)


def own_part(wide, me):
    return jnp.where(me % 2 == 0, wide[:, :OWN], wide[:, 256 - OWN :])


def rich_rows(rich, me, h):
    lane = lax.broadcasted_iota(jnp.int32, (8, 4 * HEADS), 1)
    term = lax.broadcasted_iota(jnp.int32, (8, 4 * HEADS), 0)
    chosen = (lane == 4 * (OWN_HEADS * me + h) + term) & (term < 4)
    return nn(jnp.where(chosen, 1.0, 0.0).astype(BF), rich)


def rich_columns(rich, me, h):
    row = lax.broadcasted_iota(jnp.int32, (4 * HEADS, 128), 0)
    term = lax.broadcasted_iota(jnp.int32, (4 * HEADS, 128), 1)
    chosen = (row == 4 * (OWN_HEADS * me + h) + term) & (term < 4)
    return tn(rich, jnp.where(chosen, 1.0, 0.0).astype(BF))


def code_kernel(
    tok_any, neigh_any, rank_any, member_any, out_ref, tok_ref, neigh_ref, rank_ref, member_ref, sems
):
    pairs = (tok_any, tok_ref), (neigh_any, neigh_ref), (rank_any, rank_ref), (member_any, member_ref)
    copies = [load(source, target, sems.at[i]) for i, (source, target) in enumerate(pairs)]
    for copy in copies:
        copy.wait()
    out_ref[:, :D] = tok_ref[...]
    ints = jnp.concatenate(
        [neigh_ref[...], rank_ref[...], member_ref[...], jnp.zeros((TOK - 11, TOK), jnp.int32)], axis=0
    )
    ints = ints.astype(F32).T
    high = jnp.floor(ints * (1.0 / 256.0))
    low = ints - 256.0 * high
    out_ref[:, D:] = jnp.concatenate([low[:, :16], high[:, :16], low[:, 32:]], axis=1).astype(BF)


def decoded(coded):
    coded = coded.astype(F32)
    return coded + 256.0 * jnp.concatenate([coded[:, 16:], coded[:, :16]], axis=1)


def share_out(chunk_of, bit, pairs, kept_ref, sent_ref):
    for i, pair in enumerate(pairs):
        first, second = (chunk_of(g) for g in pair)
        kept_ref[i] = jnp.where(bit == 0, first, second)
        sent_ref[i] = jnp.where(bit == 0, second, first)


def row_pieces(ref, g):
    return [ref[OWN * p + PIECE * g : OWN * p + PIECE * (g + 1)] for p in range(SEQ_WAYS)]


def pair_terms(meta_col, meta_row, before_ref, distance_ref):
    for c in range(2):
        gap = meta_col[:, 8 + c : 9 + c] - meta_row[8 + c : 9 + c]
        before_ref[c] = jnp.where(gap < 0.0, 1.0, -1.0)
        distance_ref[c] = jnp.log(1.0 + jnp.abs(gap)) * (1.0 / LOG_NORM)


def attend_kernel(
    tok_a, tok_b, tok_c, tok_d, glob_ref, gain_ref, shift_ref, rich_q_ref, rich_k_ref,
    w_graph_any, w_query_any, w_key_any, w_value_any,
    both_ref, member_ref, glob_att_ref, meta_row_ref,
    agg_any, pre_any, super_any, normed_any, qkv_any, prob_any,
    agg_ref, pre_ref, super_ref, normed_ref, qkv_ref, prob_ref,
    padded, w_graph_ref, w_project_ref, keys, values, key_rich, meta_pad, before_ref, distance_ref,
    rich_left, far_ref, heads_out, attn_ref, meta_col_ref, sems, prob_sems,
):
    me = lax.axis_index("seq")
    graph_copy = load(w_graph_any, w_graph_ref, sems.at[0])
    project_copies = [
        load(weight.at[:, own_window(me)], w_project_ref.at[i], sems.at[1 + i])
        for i, weight in enumerate((w_query_any, w_key_any, w_value_any))
    ]
    padded[:RADIUS] = jnp.zeros((RADIUS, D), BF)
    padded[RADIUS + ROWS :] = jnp.zeros((RADIUS, D), BF)
    starts = [pl.multiple_of((me ^ k) * TOK, TOK) for k in range(SEQ_WAYS)]
    for start, tok in zip(starts, (tok_a, tok_b, tok_c, tok_d)):
        padded[pl.ds(start + RADIUS, TOK)] = tok[:, :D]
    for start, tok in zip(starts, (tok_a, tok_b, tok_c, tok_d)):
        floats = decoded(tok[:, D:])
        meta_col_ref[pl.ds(start, TOK)] = floats
        meta_row_ref[:, pl.ds(start, TOK)] = floats.T[:16]
        counts = counts_of(floats, 0, WIN)
        mean = nn(counts, padded[pl.ds(start, WIN)]) * (1.0 / NEIGH)
        agg_ref[pl.ds(start, TOK)] = mean.astype(BF)
    gain, shift = as_row(gain_ref), as_row(shift_ref)
    graph_copy.wait()
    for low in range(0, ROWS, 256):
        rows = slice(low, low + 256)
        pre = nn(agg_ref[rows], w_graph_ref[...])
        pre_ref[rows] = pre
        tokens = padded[RADIUS + low : RADIUS + low + 256].astype(F32)
        super_rows = tokens + gelu_parts(pre)[0]
        super_ref[rows] = super_rows
        normed_ref[rows] = (row_stats(super_rows)[0] * gain + shift).astype(BF)
    glob_hat = row_stats(glob_ref[...].astype(F32))[0]
    normed_ref[ROWS:] = (glob_hat * gain + shift).astype(BF)
    kept = [
        load(source, target, sems.at[4 + i])
        for i, (source, target) in enumerate((
            (agg_ref.at[:, own_window(me)], agg_any), (pre_ref, pre_any), (super_ref, super_any), (normed_ref, normed_any),
        ))
    ]
    normed = normed_ref[...]
    for part in range(3):
        project_copies[part].wait()
        projected = nn(normed, own_part(w_project_ref[part], me)).astype(BF)
        for h in range(OWN_HEADS):
            qkv_ref[part * OWN_HEADS + h] = projected[:, h * HEAD_DIM : (h + 1) * HEAD_DIM]
    kept.append(load(qkv_ref, qkv_any, sems.at[8]))
    rich_q, rich_k = rich_q_ref[...], rich_k_ref[...]
    spread_keys(qkv_ref, keys, values)
    meta_pad[...] = jnp.zeros((16, PAD), F32)
    meta_pad[:, RADIUS : RADIUS + ROWS] = meta_row_ref[...]

    def prepare(h, carry):
        key_rich[h] = nt(rich_rows(rich_k, me, h).astype(BF), keys[h])
        rich_left[h] = rich_columns(rich_q, me, h).astype(BF)
        return carry

    lax.fori_loop(0, OWN_HEADS, prepare, 0)

    def prob_copy(b):
        rows = pl.ds(pl.multiple_of(b * TOK, TOK), TOK)
        return pltpu.make_async_copy(prob_ref.at[:, rows], prob_any.at[:, rows], prob_sems.at[b])

    def block(b, carry):
        start = pl.multiple_of(b * TOK, TOK)
        rows = pl.ds(start, TOK)
        window = pl.ds(start, WIN)
        pair_terms(meta_col_ref[rows], meta_pad[:, window], before_ref, distance_ref)
        q_spot = lax.broadcasted_iota(jnp.int32, (TOK, WIN), 0)
        k_spot = lax.broadcasted_iota(jnp.int32, (TOK, WIN), 1)
        ahead = k_spot - q_spot
        place = k_spot + (start - RADIUS)
        mask = (ahead >= 0) & (ahead <= 2 * RADIUS) & (place >= 0) & (place < ROWS)
        far_ref[...] = jnp.where(mask, 0.0, MASKED)

        def head(h, inner):
            query = qkv_ref[h, rows]
            query_rich = nn(query, rich_left[h])
            right = key_rich[h, :, window]
            scores = nt(query, keys[h, window]) * SCORE_SCALE + far_ref[...]
            spread = None
            for c in range(2):
                logit = (query_rich[:, c : c + 1] + right[c : c + 1]) * before_ref[c]
                off = distance_ref[c] - (query_rich[:, 2 + c : 3 + c] + right[2 + c : 3 + c])
                scores = scores + (jnp.minimum(logit, 0.0) - 0.5 * off * off)
                grown = 1.0 + jnp.exp(-jnp.abs(logit))
                spread = grown if spread is None else spread * grown
            scores = scores - jnp.log(spread)
            glob_scores = nt(query, qkv_ref[OWN_HEADS + h, ROWS:]) * SCORE_SCALE
            top = jnp.maximum(
                jnp.max(scores, axis=-1, keepdims=True), jnp.max(glob_scores, axis=-1, keepdims=True)
            )
            prob = jnp.exp(scores - top)
            glob_prob = jnp.exp(glob_scores - top)
            total = jnp.sum(prob, axis=-1, keepdims=True) + jnp.sum(
                glob_prob, axis=-1, keepdims=True
            )
            inverse = 1.0 / total
            prob = prob * inverse
            glob_prob = glob_prob * inverse
            prob_ref[h, rows, :WIN] = prob
            prob_ref[h, rows, WIN : WIN + GLOBALS] = glob_prob
            mixed = nn(prob.astype(BF), values[h, window]) + nn(
                glob_prob.astype(BF), qkv_ref[2 * OWN_HEADS + h, ROWS:]
            )
            heads_out[h, rows] = mixed.astype(BF)
            return inner

        lax.fori_loop(0, OWN_HEADS, head, 0, unroll=True)
        prob_copy(b).start()
        return carry

    lax.fori_loop(0, SEQ_WAYS, block, 0)
    slot = lax.broadcasted_iota(jnp.int32, (GLOBALS, ROWS), 0).astype(F32)
    member = meta_row_ref[10:11] == slot

    def glob_head(h, carry):
        query = qkv_ref[h, ROWS:]
        scores = nt(query, qkv_ref[OWN_HEADS + h, :ROWS]) * SCORE_SCALE
        scores = jnp.where(member, scores, MASKED)
        own = nt(query, qkv_ref[OWN_HEADS + h, ROWS:]) * SCORE_SCALE
        top = jnp.maximum(
            jnp.max(scores, axis=-1, keepdims=True), jnp.max(own, axis=-1, keepdims=True)
        )
        prob = jnp.exp(scores - top)
        own_prob = jnp.exp(own - top)
        total = jnp.sum(prob, axis=-1, keepdims=True) + jnp.sum(own_prob, axis=-1, keepdims=True)
        inverse = 1.0 / total
        prob = prob * inverse
        own_prob = own_prob * inverse
        member_ref[h, :, :ROWS] = prob
        member_ref[h, :, ROWS : ROWS + GLOBALS] = own_prob
        mixed = nn(prob.astype(BF), qkv_ref[2 * OWN_HEADS + h, :ROWS]) + nn(
            own_prob.astype(BF), qkv_ref[2 * OWN_HEADS + h, ROWS:]
        )
        glob_att_ref[h] = mixed
        heads_out[h, ROWS:] = mixed.astype(BF)
        return carry

    lax.fori_loop(0, OWN_HEADS, glob_head, 0)
    for h in range(OWN_HEADS):
        attn_ref[:, h * HEAD_DIM : (h + 1) * HEAD_DIM] = heads_out[h]
    for half in range(2):
        span = slice(OWN * half, OWN * (half + 1))
        low, glob_low = HALF_TOK * half, ROWS + HALF_GLOB * half
        both_ref[:HALF_TOK, span] = attn_ref[low : low + HALF_TOK]
        both_ref[HALF_TOK:, span] = attn_ref[glob_low : glob_low + HALF_GLOB]
    for copy in kept:
        copy.wait()
    for b in range(SEQ_WAYS):
        prob_copy(b).wait()


def meta_columns(meta_row):
    return jnp.concatenate([meta_row, jnp.zeros((TOK - 16, TOK), F32)], axis=0).T


def spread_keys(qkv_ref, keys, values):
    edge = jnp.zeros((OWN_HEADS, RADIUS, HEAD_DIM), BF)
    for held, first in ((keys, OWN_HEADS), (values, 2 * OWN_HEADS)):
        held[:, :RADIUS] = edge
        held[:, RADIUS + ROWS :] = edge
        held[:, RADIUS : RADIUS + ROWS] = qkv_ref[first : first + OWN_HEADS, :ROWS]


def own_feed_kernel(
    att_a, att_b, att_c, att_d, gain_ref, shift_ref, bias_up_ref, bias_down_ref, cot_ref,
    super_any, glob_any, cot_glob_any, w_out_any, w_up_any, w_down_any,
    out_ref, send_ref,
    att_refs, glob_att_refs, super_ref, glob_ref, cot_glob_ref, w_out_ref, w_up_ref, w_down_ref,
    bias_ref, out_sum, back_sum, sems,
):
    me = lax.axis_index("seq")
    half = lax.div(me, 2)
    inner = lax.rem(me, 2)
    tok_rows = pl.ds(pl.multiple_of(inner * TOK, TOK), TOK)
    glob_rows = pl.ds(pl.multiple_of(HALF_TOK + inner * GLOB_OWN, GLOB_OWN), GLOB_OWN)
    own_tok = pl.ds(pl.multiple_of(me * TOK, TOK), TOK)
    own_glob = pl.ds(pl.multiple_of(me * GLOB_OWN, GLOB_OWN), GLOB_OWN)
    first = []
    for k, att in enumerate((att_a, att_b, att_c, att_d)):
        first.append(load(att.at[tok_rows], att_refs.at[k], sems.at[k]))
        first.append(load(att.at[glob_rows], glob_att_refs.at[k], sems.at[4 + k]))
    first.append(load(super_any.at[own_tok], super_ref, sems.at[8]))
    first.append(load(glob_any.at[own_glob], glob_ref, sems.at[9]))
    first.append(load(cot_glob_any.at[own_glob], cot_glob_ref, sems.at[10]))
    first.append(load(w_out_any, w_out_ref, sems.at[11]))

    def up_copy(j):
        span = pl.ds(pl.multiple_of(j * FF_OWN, FF_OWN), FF_OWN)
        return pltpu.make_async_copy(w_up_any.at[:, span], w_up_ref.at[j], sems.at[12 + j])

    def down_copy(j):
        span = pl.ds(pl.multiple_of(j * FF_OWN, FF_OWN), FF_OWN)
        return pltpu.make_async_copy(w_down_any.at[span], w_down_ref.at[j], sems.at[16 + j])

    for j in range(SEQ_WAYS):
        up_copy(j).start()
        down_copy(j).start()
    for copy in first:
        copy.wait()
    y_rows = jnp.concatenate([super_ref[...], glob_ref[...].astype(F32)], axis=0)
    for k in range(SEQ_WAYS):
        wide = jnp.concatenate([att_refs[k], glob_att_refs[k]], axis=0)
        mixed = jnp.where(half == 0, wide[:, :OWN], wide[:, OWN:])
        y_rows = y_rows + nn(mixed, w_out_ref[pl.ds(pl.multiple_of((me ^ k) * OWN, OWN), OWN)])
    gain = as_row(gain_ref)
    hat, scale = row_stats(y_rows)
    normed = (hat * gain + as_row(shift_ref)).astype(BF)
    cot = jnp.concatenate([cot_ref[...], cot_glob_ref[...]], axis=0)
    bias = as_row(bias_up_ref)
    for j in range(SEQ_WAYS):
        bias_ref[j : j + 1] = bias[:, FF_OWN * j : FF_OWN * (j + 1)]
    out_sum[...] = y_rows + as_row(bias_down_ref)
    back_sum[...] = jnp.zeros((CHUNK, D), F32)

    def units(j, carry):
        up_copy(j).wait()
        hidden, slope = gelu_parts(nn(normed, w_up_ref[j]) + bias_ref[pl.ds(j, 1)])
        down_copy(j).wait()
        d_pre = (nt(cot, w_down_ref[j]) * slope).astype(BF)
        back_sum[...] += nt(d_pre, w_up_ref[j])
        out_sum[...] += nn(hidden.astype(BF), w_down_ref[j])
        return carry

    lax.fori_loop(0, SEQ_WAYS, units, 0)
    out, back = out_sum[...], back_sum[...]
    out_ref[...] = out[:TOK].astype(BF)
    scaled = back * gain
    cot = cot.astype(F32)
    d_rows = cot + scale * (
        scaled
        - jnp.mean(scaled, axis=-1, keepdims=True)
        - hat * jnp.mean(scaled * hat, axis=-1, keepdims=True)
    )
    sums = [back * hat, back, cot]
    sums = [jnp.sum(rows, axis=0, keepdims=True) for rows in sums]
    send_ref[:CHUNK] = d_rows.astype(BF)
    send_ref[CHUNK : CHUNK + GLOB_OWN] = out[TOK:].astype(BF)
    sums = jnp.concatenate(sums + [jnp.zeros((13, D), F32)], axis=0)
    send_ref[CHUNK + GLOB_OWN :] = sums.astype(BF)


def feed_rows_kernel(
    att_a, att_b, att_c, att_d, cot_a, cot_b, cot_c, cot_d, cot_glob_ref, glob_ref, gain_ref,
    shift_ref, bias_ref, super_any, w_out_any, w_up_any,
    kept_ref, sent_ref, normed_ref, slope_ref, cot_ref,
    super_ref, w_out_ref, w_up_ref, hidden_ref, grad, sems,
):
    me, x = lax.axis_index("seq"), lax.rem(lax.axis_index("grp"), 2)
    mine = pl.multiple_of(me * FF_OWN, FF_OWN)
    copies = [
        load(super_any, super_ref, sems.at[0]),
        load(w_out_any, w_out_ref, sems.at[1]),
        load(w_up_any.at[:, pl.ds(mine, FF_OWN)], w_up_ref, sems.at[2]),
    ]
    for k, cot in enumerate((cot_a, cot_b, cot_c, cot_d)):
        b = me ^ k
        at = lax.div(b, 2) * HALF + lax.rem(b, 2) * TOK
        cot_ref[pl.ds(pl.multiple_of(at, 32), TOK)] = cot[...]
    for half in range(2):
        cot_ref[HALF * half + HALF_TOK : HALF * (half + 1)] = cot_glob_ref[
            HALF_GLOB * half : HALF_GLOB * (half + 1)
        ]
    gain, shift = as_row(gain_ref), as_row(shift_ref)
    bias = as_row(bias_ref)
    bias = [bias[:, FF_OWN * j : FF_OWN * (j + 1)] for j in range(SEQ_WAYS)]
    bias = jnp.where(me < 2, jnp.where(me == 0, bias[0], bias[1]), jnp.where(me == 2, bias[2], bias[3]))
    for copy in copies:
        copy.wait()
    for half in range(2):
        rows = slice(HALF * half, HALF * (half + 1))
        glob_rows = glob_ref[HALF_GLOB * half : HALF_GLOB * (half + 1)].astype(F32)
        y_rows = jnp.concatenate([super_ref[HALF_TOK * half : HALF_TOK * (half + 1)], glob_rows], axis=0)
        for k, att in enumerate((att_a, att_b, att_c, att_d)):
            w_rows = w_out_ref[pl.ds(pl.multiple_of((me ^ k) * OWN, OWN), OWN)]
            y_rows = y_rows + nn(att[:, OWN * half : OWN * (half + 1)], w_rows)
        normed = (row_stats(y_rows)[0] * gain + shift).astype(BF)
        normed_ref[rows] = normed
        hidden, slope = gelu_parts(nn(normed, w_up_ref[...]) + bias)
        hidden_ref[rows] = hidden.astype(BF)
        slope_ref[rows] = slope
    grad[...] = tn(hidden_ref[...], cot_ref[...])
    share_out(lambda g: grad[BAND * g : BAND * (g + 1)].astype(BF), x, X_PAIRS, kept_ref, sent_ref)


def feed_back_kernel(
    normed_ref, slope_ref, cot_ref, w_down_any,
    kept_ref, sent_ref, d_bias_ref, w_down_ref, d_pre_ref, grad, sems,
):
    me = lax.axis_index("seq")
    x = lax.rem(lax.axis_index("grp"), 2)
    mine = pl.ds(pl.multiple_of(me * FF_OWN, FF_OWN), FF_OWN)
    load(w_down_any.at[mine], w_down_ref, sems.at[0]).wait()
    d_bias = jnp.zeros((1, FF_OWN), F32)
    for half in range(2):
        rows = slice(HALF * half, HALF * (half + 1))
        d_pre = (nt(cot_ref[rows], w_down_ref[...]) * slope_ref[rows]).astype(BF)
        d_pre_ref[rows] = d_pre
        d_bias = d_bias + jnp.sum(d_pre.astype(F32), axis=0, keepdims=True)
    d_bias_ref[...] = d_bias
    grad[...] = tn(normed_ref[...], d_pre_ref[...])
    share_out(
        lambda g: jnp.concatenate(row_pieces(grad, g), axis=0).astype(BF), x, X_PAIRS, kept_ref, sent_ref
    )


def project_grad_kernel(normed_ref, d_qkv_ref, attn_ref, d_proj_ref, kept_ref, sent_ref, grad, grad_out):
    x = lax.rem(lax.axis_index("grp"), 2)
    grad[...] = tn(normed_ref[...], d_qkv_ref[:, : 3 * OWN])
    total = None
    for half in range(2):
        columns = slice(OWN * half, OWN * (half + 1))
        first, glob_first = HALF_TOK * half, ROWS + HALF_GLOB * half
        term = tn(attn_ref[:HALF_TOK, columns], d_proj_ref[first : first + HALF_TOK])
        term = term + tn(attn_ref[HALF_TOK:, columns], d_proj_ref[glob_first : glob_first + HALF_GLOB])
        total = term if total is None else total + term
    grad_out[...] = total

    def chunk(g):
        out_rows = grad_out[PIECE * g : PIECE * (g + 1)]
        left = jnp.concatenate(row_pieces(grad, g), axis=0)
        right = [out_rows[:, OWN * p : OWN * (p + 1)] for p in range(SEQ_WAYS)]
        return jnp.concatenate([left, jnp.concatenate(right, axis=0)], axis=1).astype(BF)

    share_out(chunk, x, X_PAIRS, kept_ref, sent_ref)


def back_kernel(
    back_a, back_b, back_c, back_d, glob_att_ref, meta_row_ref, rich_q_ref,
    rich_k_ref, w_out_any, qkv_any, prob_any, member_any,
    d_proj_ref, d_qkv_ref, vec_ref, out_global_ref,
    w_out_ref, qkv_ref, prob_ref, member_ref, keys, values, key_rich, meta_pad, before_ref, distance_ref,
    rich_left, d_att, d_keys, d_values, d_key_rich, d_query_rich, rich_qt, rich_kt, d_glob, parts, rich,
    sems, prob_sems,
):
    me = lax.axis_index("seq")
    own_rows = pl.ds(pl.multiple_of(me * OWN, OWN), OWN)
    w_copy = load(w_out_any.at[own_rows], w_out_ref, sems.at[0])
    qkv_copy = load(qkv_any, qkv_ref, sems.at[1])

    def prob_copy(b):
        rows = pl.ds(pl.multiple_of(b * TOK, TOK), TOK)
        return pltpu.make_async_copy(prob_any.at[:, rows], prob_ref.at[:, rows], prob_sems.at[b])

    for b in range(SEQ_WAYS):
        prob_copy(b).start()
    member_copy = load(member_any, member_ref, sems.at[2])
    sums = None
    for k, back in enumerate((back_a, back_b, back_c, back_d)):
        at = me ^ k
        d_proj_ref[pl.ds(pl.multiple_of(at * TOK, TOK), TOK)] = back[:TOK]
        d_proj_ref[pl.ds(pl.multiple_of(ROWS + at * GLOB_OWN, GLOB_OWN), GLOB_OWN)] = back[TOK:CHUNK]
        out_global_ref[pl.ds(pl.multiple_of(at * GLOB_OWN, GLOB_OWN), GLOB_OWN)] = back[
            CHUNK : CHUNK + GLOB_OWN
        ]
        part = back[CHUNK + GLOB_OWN :].astype(F32)
        sums = part if sums is None else sums + part
    vec_ref[...] = sums[:8]
    w_copy.wait()
    projected = nt(d_proj_ref[...], w_out_ref[...]).astype(BF)
    for h in range(OWN_HEADS):
        d_att[h] = projected[:, h * HEAD_DIM : (h + 1) * HEAD_DIM]
    meta_pad[...] = jnp.zeros((16, PAD), F32)
    meta_pad[:, RADIUS : RADIUS + ROWS] = meta_row_ref[...]
    qkv_copy.wait()
    spread_keys(qkv_ref, keys, values)
    rich_q, rich_k = rich_q_ref[...], rich_k_ref[...]

    def prepare(h, carry):
        rich_left[h] = rich_columns(rich_q, me, h).astype(BF)
        rich_qt[h] = rich_rows(rich_q, me, h)
        rich_kt[h] = rich_rows(rich_k, me, h)
        key_rich[h] = nt(rich_kt[h].astype(BF), keys[h])
        return carry

    lax.fori_loop(0, OWN_HEADS, prepare, 0)
    d_keys[...] = jnp.zeros((OWN_HEADS, PAD, HEAD_DIM), F32)
    d_values[...] = jnp.zeros((OWN_HEADS, PAD, HEAD_DIM), F32)
    d_key_rich[...] = jnp.zeros((OWN_HEADS, 8, PAD), F32)
    d_glob[...] = jnp.zeros((2 * OWN_HEADS, GLOBALS, HEAD_DIM), F32)

    def block(b, carry):
        start = pl.multiple_of(b * TOK, TOK)
        rows = pl.ds(start, TOK)
        window = pl.ds(start, WIN)
        pair_terms(meta_columns(meta_row_ref[:, rows]), meta_pad[:, window], before_ref, distance_ref)
        prob_copy(b).wait()

        def head(h, inner):
            query = qkv_ref[h, rows]
            d_out = d_att[h, rows]
            prob = prob_ref[h, rows, :WIN]
            glob_prob = prob_ref[h, rows, WIN : WIN + GLOBALS]
            d_prob = nt(d_out, values[h, window])
            d_glob_prob = nt(d_out, qkv_ref[2 * OWN_HEADS + h, ROWS:])
            delta = jnp.sum(prob * d_prob, axis=-1, keepdims=True) + jnp.sum(
                glob_prob * d_glob_prob, axis=-1, keepdims=True
            )
            d_scores = prob * (d_prob - delta)
            d_low = d_scores.astype(BF)
            d_glob_low = (glob_prob * (d_glob_prob - delta)).astype(BF)
            query_rich = nn(query, rich_left[h])
            right = key_rich[h, :, window]
            lefts, belows = [None] * 4, [None] * 4
            for c in range(2):
                logit = query_rich[:, c : c + 1] + right[c : c + 1]
                pulled = d_scores * (0.5 * before_ref[c] - 0.5 * jnp.tanh(0.5 * logit))
                off = distance_ref[c] - (query_rich[:, 2 + c : 3 + c] + right[2 + c : 3 + c])
                off = d_scores * off
                lefts[c] = jnp.sum(pulled, axis=-1, keepdims=True)
                lefts[2 + c] = jnp.sum(off, axis=-1, keepdims=True)
                belows[c] = jnp.sum(pulled, axis=0, keepdims=True)
                belows[2 + c] = jnp.sum(off, axis=0, keepdims=True)
            d_key_rich[h, :, window] += jnp.concatenate(belows + [jnp.zeros((4, WIN), F32)], axis=0)
            lane = lax.broadcasted_iota(jnp.int32, (TOK, 8), 1)
            d_left = jnp.zeros((TOK, 8), F32)
            d_query = (
                nn(d_low, keys[h, window]) + nn(d_glob_low, qkv_ref[OWN_HEADS + h, ROWS:])
            ) * SCORE_SCALE
            for c, column in enumerate(lefts):
                d_left = jnp.where(lane == c, column, d_left)
                d_query = d_query + column * rich_qt[h, c : c + 1]
            d_query_rich[h, rows] = d_left
            parts[h, rows] = d_query.astype(BF)
            d_keys[h, window] += tn(d_low, query) * SCORE_SCALE
            d_values[h, window] += tn(prob.astype(BF), d_out)
            d_glob[h] += tn(d_glob_low, query) * SCORE_SCALE
            d_glob[OWN_HEADS + h] += tn(glob_prob.astype(BF), d_out)
            return inner

        lax.fori_loop(0, OWN_HEADS, head, 0, unroll=True)
        return carry

    lax.fori_loop(0, SEQ_WAYS, block, 0)
    member_copy.wait()

    def glob_head(h, carry):
        query = qkv_ref[h, ROWS:]
        key_rows = qkv_ref[OWN_HEADS + h, :ROWS]
        value_rows = qkv_ref[2 * OWN_HEADS + h, :ROWS]
        glob_key = qkv_ref[OWN_HEADS + h, ROWS:]
        glob_value = qkv_ref[2 * OWN_HEADS + h, ROWS:]
        d_out = d_att[h, ROWS:]
        delta = jnp.sum(d_out.astype(F32) * glob_att_ref[h], axis=-1, keepdims=True)
        prob = member_ref[h, :, :ROWS]
        own_prob = member_ref[h, :, ROWS : ROWS + GLOBALS]
        d_low = (prob * (nt(d_out, value_rows) - delta)).astype(BF)
        d_own = (own_prob * (nt(d_out, glob_value) - delta)).astype(BF)
        d_query = (nn(d_low, key_rows) + nn(d_own, glob_key)) * SCORE_SCALE
        parts[h, ROWS:] = d_query.astype(BF)
        parts[OWN_HEADS + h, ROWS:] = (d_glob[h] + tn(d_own, query) * SCORE_SCALE).astype(BF)
        parts[2 * OWN_HEADS + h, ROWS:] = (
            d_glob[OWN_HEADS + h] + tn(own_prob.astype(BF), d_out)
        ).astype(BF)
        d_right = d_key_rich[h, :, RADIUS : RADIUS + ROWS]
        d_key = d_keys[h, RADIUS : RADIUS + ROWS] + tn(d_low, query) * SCORE_SCALE
        d_key = d_key + lax.dot_general(
            d_right, rich_kt[h], (((0,), (0,)), ((), ())), precision=PRECISE,
            preferred_element_type=F32,
        )
        d_value = d_values[h, RADIUS : RADIUS + ROWS] + tn(prob.astype(BF), d_out)
        parts[OWN_HEADS + h, :ROWS] = d_key.astype(BF)
        parts[2 * OWN_HEADS + h, :ROWS] = d_value.astype(BF)
        rich[pl.ds(pl.multiple_of(8 * h, 8), 8)] = jnp.concatenate(
            [tn(d_query_rich[h].astype(BF), qkv_ref[h, :ROWS])[:4], nn(d_right.astype(BF), key_rows)[:4]],
            axis=0,
        )
        return carry

    lax.fori_loop(0, OWN_HEADS, glob_head, 0)
    for i in range(3 * OWN_HEADS):
        d_qkv_ref[:, i * HEAD_DIM : (i + 1) * HEAD_DIM] = parts[i]
    rich[RICH:] = jnp.zeros((32 - RICH, HEAD_DIM), F32)
    d_qkv_ref[:, 3 * OWN :] = jnp.zeros((ALL, WIDE - 3 * OWN), BF)
    d_qkv_ref[:32, 3 * OWN :] = rich[...].astype(BF)


def norm_kernel(
    dqkv_a, dqkv_b, dqkv_c, dqkv_d, glob_ref, d_proj_ref, gain_ref, vec_two_ref, d_bias_up_ref,
    w_query_any, w_key_any, w_value_any, super_any, pre_any, agg_any,
    grad_glob_ref, kept_ref, sent_ref, d_own_ref, d_pre,
    w_query_ref, w_key_ref, w_value_ref, super_ref, pre_ref, agg_ref, d_super, d_qkv, d_norm, rich, sems,
):
    me, x = lax.axis_index("seq"), lax.rem(lax.axis_index("grp"), 2)
    weight_copies = [
        load(source, target, sems.at[i])
        for i, (source, target) in enumerate((
            (w_query_any, w_query_ref), (w_key_any, w_key_ref), (w_value_any, w_value_ref),
        ))
    ]
    row_copies = [load(super_any, super_ref, sems.at[3]), load(pre_any, pre_ref, sems.at[4])]
    agg_copy = load(agg_any, agg_ref, sems.at[5])
    for k, part in enumerate((dqkv_a, dqkv_b, dqkv_c, dqkv_d)):
        d_qkv[me ^ k] = part[...]
        rich[me ^ k] = part[:32, 3 * OWN :].astype(F32)
    total = None
    for i, weight in enumerate((w_query_ref, w_key_ref, w_value_ref)):
        weight_copies[i].wait()
        for p in range(SEQ_WAYS):
            term = nt(d_qkv[p, :, OWN * i : OWN * (i + 1)], weight[:, OWN * p : OWN * (p + 1)])
            total = term if total is None else total + term
    d_norm[...] = total
    for copy in row_copies:
        copy.wait()
    gain = as_row(gain_ref)
    d_gain = jnp.zeros((1, D), F32)
    d_shift = jnp.zeros((1, D), F32)
    for low in range(0, ALL, 192):
        rows = slice(low, low + 192)
        inner = min(192, ROWS - low)
        if inner == 192:
            rows_in = super_ref[rows]
        else:
            rows_in = jnp.concatenate([super_ref[low:], glob_ref[...].astype(F32)], axis=0)
        back, gain_part, shift_part = norm_back(d_norm[rows], gain, rows_in)
        d_gain = d_gain + gain_part
        d_shift = d_shift + shift_part
        back = back + d_proj_ref[rows].astype(F32)
        d_super[rows] = back
        long = slice(low, low + inner)
        slope = gelu_parts(pre_ref[long])[1]
        d_pre[long] = (back[:inner] * slope).astype(BF)
    grad_glob_ref[...] = d_super[ROWS:]
    d_own_ref[...] = d_super[pl.ds(pl.multiple_of(me * TOK, TOK), TOK)]
    agg_copy.wait()
    grad = tn(own_part(agg_ref[...], me), d_pre[...])
    extra = jnp.concatenate(
        [vec_two_ref[0:3], d_bias_up_ref[...], d_gain, d_shift, jnp.zeros((1, D), F32)], axis=0
    )

    def chunk(g):
        pieces = [rich[g // 2, 12 * (g % 2) + i : 12 * (g % 2) + i + 1] for i in range(12)]
        rows = [grad[PIECE * g : PIECE * (g + 1)], jnp.concatenate(pieces, axis=1), extra]
        return jnp.concatenate(rows, axis=0).astype(BF)

    share_out(chunk, x, X_PAIRS, kept_ref, sent_ref)


def tokens_kernel(d_own_ref, d_pre, meta_row_ref, w_graph_any, grad_tok_ref, w_graph_ref, sems):
    me = lax.axis_index("seq")
    copy = load(w_graph_any, w_graph_ref, sems.at[0])
    counts = []
    for shift in (-1, 0, 1):
        rows = pl.ds(pl.multiple_of(jnp.clip(me - shift, 0, SEQ_WAYS - 1) * TOK, TOK), TOK)
        counts.append(counts_of(meta_columns(meta_row_ref[:, rows]), (shift + 1) * TOK, TOK))
    copy.wait()
    total = d_own_ref[...]
    for shift, count in zip((-1, 0, 1), counts):
        b = me - shift
        fits = (b >= 0) & (b < SEQ_WAYS)
        rows = pl.ds(pl.multiple_of(jnp.clip(b, 0, SEQ_WAYS - 1) * TOK, TOK), TOK)
        d_agg = (nt(d_pre[rows], w_graph_ref[...]) * (1.0 / NEIGH)).astype(BF)
        total = total + jnp.where(fits, tn(count, d_agg), 0.0)
    grad_tok_ref[...] = total


DISTANCES = (0, 4, 2, 6)


def down_out_kernel(held, came, out_ref):
    for i, distance in enumerate(DISTANCES):
        for flip, pieces in enumerate((held, came)):
            g = lax.axis_index("grp") ^ (distance + flip)
            out_ref[pl.ds(pl.multiple_of(BAND * g, BAND), BAND)] = pieces[i].astype(F32)


def up_out_kernel(held, came, out_ref):
    for i, distance in enumerate(DISTANCES):
        for flip, pieces in enumerate((held, came)):
            g = lax.axis_index("grp") ^ (distance + flip)
            piece = pieces[i].astype(F32)
            rows = pl.ds(pl.multiple_of(PIECE * g, 8), PIECE)
            for k in range(SEQ_WAYS):
                columns = pl.ds(pl.multiple_of((lax.axis_index("seq") ^ k) * D, D), D)
                out_ref[rows, columns] = piece[PIECE * k : PIECE * (k + 1)]


def project_out_kernel(held, came, query_ref, key_ref, value_ref, out_ref, pieces):
    for i, distance in enumerate(DISTANCES):
        for flip, blocks in enumerate((held, came)):
            g = lax.axis_index("grp") ^ (distance + flip)
            rows = pl.ds(pl.multiple_of(PIECE * g, 8), PIECE)
            piece = blocks[i].astype(F32)
            for k in range(SEQ_WAYS):
                pieces[lax.axis_index("seq") ^ k] = piece[PIECE * k : PIECE * (k + 1), : 3 * OWN]
            for j, ref in enumerate((query_ref, key_ref, value_ref)):
                parts = [pieces[p, :, OWN * j : OWN * (j + 1)] for p in range(SEQ_WAYS)]
                ref[rows] = jnp.concatenate(parts, axis=1)
            parts = [piece[PIECE * p : PIECE * (p + 1), 3 * OWN :] for p in range(SEQ_WAYS)]
            out_ref[rows] = jnp.concatenate(parts, axis=1)


def graph_out_kernel(
    held, came, graph_ref, gain_one_ref, shift_one_ref, gain_two_ref, shift_two_ref, bias_up_ref,
    bias_down_ref, rich_q_ref, rich_k_ref, vectors,
):
    me = lax.axis_index("seq")
    for i, distance in enumerate(DISTANCES):
        for flip, blocks in enumerate((held, came)):
            g = lax.axis_index("grp") ^ (distance + flip)
            rows = pl.ds(pl.multiple_of(PIECE * g, 8), PIECE)
            piece = blocks[i].astype(F32)
            graph_ref[rows] = piece[:PIECE]
            for j in range(12):
                vectors[g, j : j + 1] = piece[PIECE : PIECE + 1, HEAD_DIM * j : HEAD_DIM * (j + 1)]
            vectors[g, 12:16] = jnp.zeros((4, HEAD_DIM), F32)
    sums = held[0, PIECE : PIECE + 8].astype(F32)
    lane = lax.broadcasted_iota(jnp.int32, (D, 256), 0)
    spot = lax.broadcasted_iota(jnp.int32, (D, 256), 1)
    own = jnp.where((lane == OWN * me + spot) & (spot < OWN), 1.0, 0.0).astype(BF)
    own = nn(sums.astype(BF), own)[:, :OWN]
    for ref, row in (
        (gain_two_ref, 1), (shift_two_ref, 2), (bias_down_ref, 3), (gain_one_ref, 5), (shift_one_ref, 6),
    ):
        ref[...] = own[row : row + 1].reshape(OWN)
    bias_up_ref[...] = sums[4:5].reshape(FF_OWN)
    lane = lax.broadcasted_iota(jnp.int32, (HEAD_DIM, 128), 0)
    spot = lax.broadcasted_iota(jnp.int32, (HEAD_DIM, 128), 1)
    part = HEAD_DIM // SEQ_WAYS
    own = jnp.where((lane == part * me + spot) & (spot < part), 1.0, 0.0).astype(BF)
    own = nn(vectors[...].reshape(16 * GRP_WAYS, HEAD_DIM).astype(BF), own).astype(BF)
    row = lax.broadcasted_iota(jnp.int32, (16 * GRP_WAYS, 128), 0)
    place = 12 * lax.div(row, 16) + lax.rem(row, 16)
    column = lax.broadcasted_iota(jnp.int32, (16 * GRP_WAYS, 128), 1)
    for side, ref in enumerate((rich_q_ref, rich_k_ref)):
        wanted = 8 * lax.div(column, 4) + 4 * side + lax.rem(column, 4)
        chosen = (place == wanted) & (lax.rem(row, 16) < 12) & (column < 4 * HEADS)
        turned_rich = tn(own, jnp.where(chosen, 1.0, 0.0).astype(BF))
        ref[...] = turned_rich[:part, : 4 * HEADS]


def call(kernel, ins, outs, scratch=(), apart=0, outs_apart=0, room=50):
    vmem, any_space = pl.BlockSpec(memory_space=pltpu.VMEM), pl.BlockSpec(memory_space=pltpu.HBM)
    return pl.pallas_call(
        kernel,
        out_shape=[jax.ShapeDtypeStruct(shape, kind) for shape, kind in outs],
        in_specs=[vmem] * (len(ins) - apart) + [any_space] * apart,
        out_specs=[vmem] * (len(outs) - outs_apart) + [any_space] * outs_apart,
        scratch_shapes=[pltpu.VMEM(*s) if isinstance(s, tuple) else s for s in scratch],
        compiler_params=pltpu.CompilerParams(vmem_limit_bytes=room * 1024 * 1024),
        cost_estimate=pl.CostEstimate(flops=KERNEL_COST, bytes_accessed=0, transcendentals=0),
    )(*ins)


def split_heads(
    tokens, global_tokens, neighbours, token_ranks, membership, w_graph, gain_one, shift_one,
    w_query, w_key, w_value, rich_query, rich_key, w_out, gain_two, shift_two, w_up, bias_up,
    w_down, bias_down, cot_tokens, cot_global,
):
    me = lax.axis_index("seq")
    grp = lax.axis_index("grp")
    x, z_low, z_high = grp % 2, (grp // 2) % 2, grp // 4
    (coded,) = call(
        code_kernel,
        [tokens, neighbours.T, token_ranks, membership.reshape(1, TOK)],
        [((TOK, CODED), BF)],
        [((TOK, D), BF), ((NEIGH, TOK), jnp.int32), ((2, TOK), jnp.int32), ((1, TOK), jnp.int32),
         pltpu.SemaphoreType.DMA((4,))],
        apart=4, room=60,
    )
    beside, across = reach_seq(coded)
    cot_tokens, across = tie(cot_tokens, across)
    tok_blocks = [coded, beside, across, lax.ppermute(across, "seq", CORE_SWAP)]
    cot_beside, cot_across = reach_seq(cot_tokens)
    rich_query, rich_key = rich_query.T, rich_key.T

    weights_shape = (D, D), BF
    stored = [
        ((ROWS, D), BF), ((ROWS, D), F32), ((ROWS, D), F32), ((ALL, D), BF),
        ((3 * OWN_HEADS, ALL, HEAD_DIM), BF), ((OWN_HEADS, ROWS, 512), F32),
    ]
    kept_agg = (ROWS, 256), BF
    heads_scratch = [
        ((OWN_HEADS, PAD, HEAD_DIM), BF), ((OWN_HEADS, PAD, HEAD_DIM), BF),
        ((OWN_HEADS, 8, PAD), F32), ((16, PAD), F32), ((2, TOK, WIN), F32), ((2, TOK, WIN), F32),
        ((OWN_HEADS, HEAD_DIM, 128), BF),
    ]
    (
        both, member_prob, glob_att, meta_row, agg, graph_pre, super_rows, normed, qkv,
        prob,
    ) = call(
        attend_kernel,
        [*tok_blocks, global_tokens, gain_one, shift_one, rich_query, rich_key, w_graph, w_query,
         w_key, w_value],
        [((HALF, 2 * OWN), BF), ((OWN_HEADS, GLOBALS, 640), F32),
         ((OWN_HEADS, GLOBALS, HEAD_DIM), F32), ((16, ROWS), F32), kept_agg, *stored[1:]],
        [*stored, ((PAD, D), BF), weights_shape, ((3, D, 256), BF), *heads_scratch,
         ((TOK, WIN), F32), ((OWN_HEADS, ALL, HEAD_DIM), BF), ((ALL, OWN), BF),
         ((ROWS, 128), F32), pltpu.SemaphoreType.DMA((9,)), pltpu.SemaphoreType.DMA((SEQ_WAYS,))],
        apart=4, outs_apart=6,
    )
    both, cot_beside, cot_across = tie(both, cot_beside, cot_across)
    att_blocks = gather_seq(both)
    cot_blocks = [cot_tokens, cot_beside, cot_across, lax.ppermute(cot_across, "seq", CORE_SWAP)]
    out_tokens, back = call(
        own_feed_kernel,
        [*att_blocks, gain_two, shift_two, bias_up, bias_down, cot_tokens, super_rows,
         global_tokens, cot_global, w_out, w_up, w_down],
        [((TOK, D), BF), ((SEND, D), BF)],
        [((SEQ_WAYS, TOK, 2 * OWN), BF), ((SEQ_WAYS, GLOB_OWN, 2 * OWN), BF), ((TOK, D), F32),
         ((GLOB_OWN, D), BF), ((GLOB_OWN, D), BF), weights_shape, ((SEQ_WAYS, D, FF_OWN), BF),
         ((SEQ_WAYS, FF_OWN, D), BF), ((SEQ_WAYS, FF_OWN), F32), ((CHUNK, D), F32), ((CHUNK, D), F32),
         pltpu.SemaphoreType.DMA((20,))],
        apart=6,
    )
    beside, across = reach_seq(back)
    late_gain, back = tie(gain_two, back)
    down_kept, down_sent, normed_two, slope, cot_all = call(
        feed_rows_kernel,
        [*att_blocks, *cot_blocks, cot_global, global_tokens, late_gain, shift_two,
         bias_up, super_rows, w_out, w_up],
        [((4, BAND, D), BF), ((4, BAND, D), BF), ((ALL, D), BF), ((ALL, FF_OWN), F32), ((ALL, D), BF)],
        [((ROWS, D), F32), weights_shape, ((D, FF_OWN), BF), ((ALL, FF_OWN), BF), ((D, D), F32),
         pltpu.SemaphoreType.DMA((3,))],
        apart=3,
    )
    down_came = swap_x(down_sent)
    across, down_kept = tie(across, down_kept)
    diagonal = lax.ppermute(across, "seq", CORE_SWAP)
    normed_two, across = tie(normed_two, across)
    up_kept, up_sent, d_bias_up = call(
        feed_back_kernel,
        [normed_two, slope, cot_all, w_down],
        [((4, BAND, D), BF), ((4, BAND, D), BF), ((1, FF_OWN), F32)],
        [((FF_OWN, D), BF), ((ALL, FF_OWN), BF), ((D, D), F32), pltpu.SemaphoreType.DMA((1,))],
        apart=1,
    )
    up_came = swap_x(up_sent)
    late_row, up_kept = tie(meta_row, up_kept)

    d_proj, d_qkv, vec_two, out_global = call(
        back_kernel,
        [back, beside, across, diagonal, glob_att, late_row, rich_query, rich_key,
         w_out, qkv, prob, member_prob],
        [((ALL, D), BF), ((ALL, WIDE), BF), ((8, D), F32), ((GLOBALS, D), BF)],
        [((OWN, D), BF), stored[4], stored[5], ((OWN_HEADS, GLOBALS, 640), F32), *heads_scratch,
         ((OWN_HEADS, ALL, HEAD_DIM), BF), ((OWN_HEADS, PAD, HEAD_DIM), F32),
         ((OWN_HEADS, PAD, HEAD_DIM), F32), ((OWN_HEADS, 8, PAD), F32), ((OWN_HEADS, ROWS, 8), F32),
         ((OWN_HEADS, 8, HEAD_DIM), F32), ((OWN_HEADS, 8, HEAD_DIM), F32),
         ((2 * OWN_HEADS, GLOBALS, HEAD_DIM), F32), ((3 * OWN_HEADS, ALL, HEAD_DIM), BF),
         ((32, HEAD_DIM), F32), pltpu.SemaphoreType.DMA((3,)), pltpu.SemaphoreType.DMA((SEQ_WAYS,))],
        apart=4,
    )
    beside, across = reach_seq(d_qkv)
    held = {"d_qkv": d_qkv, "down": down_kept, "up": up_kept}
    latest = ["d_qkv"]

    def due(value):
        value, held[latest[0]] = tie(value, held[latest[0]])
        return value

    def hold(key, value):
        held[key] = value
        latest[0] = key
        return value

    def halve(key, came, bit):
        kept, sent = halves(held[key], due(came), bit)
        hold(key, kept)
        return sent

    def total(key, came):
        return hold(key, added(held[key], due(came)))

    def join(key, came):
        return hold(key, jnp.concatenate([held[key], due(came)], axis=0))

    down_came = swap_near(halve("down", down_came, z_low))
    proj_kept, proj_sent = call(
        project_grad_kernel,
        [due(normed), d_qkv, both, d_proj],
        [((4, BAND, D), BF)] * 2,
        [((D, 3 * OWN), F32), ((OWN, D), F32)],
    )
    hold("proj", proj_kept)
    proj_came = swap_x(proj_sent)
    down_came = swap_far(halve("down", down_came, z_high))
    up_came = swap_near(halve("up", up_came, z_low))
    across = hold("across", due(across))
    diagonal = lax.ppermute(across, "seq", CORE_SWAP)
    down_came = swap_far(total("down", down_came))
    up_came = swap_far(halve("up", up_came, z_high))
    proj_came = swap_near(halve("proj", proj_came, z_low))

    grad_global, graph_kept, graph_sent, d_own, d_pre = call(
        norm_kernel,
        [d_qkv, beside, held["across"], diagonal, global_tokens, d_proj, gain_one, due(vec_two), d_bias_up,
         w_query, w_key, w_value, super_rows, graph_pre, agg],
        [((GLOBALS, D), F32), ((4, GRAPH_ROWS, D), BF), ((4, GRAPH_ROWS, D), BF), ((TOK, D), F32),
         ((ROWS, D), BF)],
        [*[weights_shape] * 3, ((ROWS, D), F32), ((ROWS, D), F32), ((ROWS, 256), BF), ((ALL, D), F32),
         ((SEQ_WAYS, ALL, WIDE), BF), ((ALL, D), F32), ((SEQ_WAYS, 32, HEAD_DIM), F32),
         pltpu.SemaphoreType.DMA((6,))],
        apart=6,
    )
    hold("graph", graph_kept)
    graph_came = swap_x(graph_sent)
    up_mine = total("up", up_came).reshape(SEQ_WAYS, PIECE, D)
    up_core = turn_core(up_mine)
    proj_came = swap_far(halve("proj", proj_came, z_high))
    down_came = swap_near(join("down", down_came))
    up_core = due(up_core)
    up_far = lax.ppermute(turn_y(up_mine, up_core), "seq", Y_SWAP)
    hold("up_core", up_core)
    (grad_tokens,) = call(
        tokens_kernel, [due(d_own), d_pre, meta_row, w_graph], [((TOK, D), F32)],
        [weights_shape, pltpu.SemaphoreType.DMA((1,))], apart=1,
    )
    hold("tokens", grad_tokens)
    up_came = swap_far(hold("up", turned(up_mine, held["up_core"], due(up_far))[None]))
    proj_sum = total("proj", proj_came)
    proj_core = turn_core(proj_sum[0, :, : 3 * OWN].reshape(SEQ_WAYS, PIECE, 3 * OWN))
    down_came = swap_x(join("down", down_came))
    graph_came = swap_near(halve("graph", graph_came, z_low))
    proj_core = due(proj_core)
    proj_mine = held["proj"][0, :, : 3 * OWN].reshape(SEQ_WAYS, PIECE, 3 * OWN)
    proj_far = lax.ppermute(turn_y(proj_mine, proj_core), "seq", Y_SWAP)
    hold("proj_core", proj_core)
    up_came = swap_near(join("up", up_came))
    proj_turned = turned(proj_mine, held["proj_core"], due(proj_far))
    proj_turned = jnp.concatenate([proj_turned, held["proj"][0, :, 3 * OWN :]], axis=1)[None]
    proj_came = swap_far(hold("proj", proj_turned))
    up_came = swap_x(join("up", up_came))
    proj_came = swap_near(join("proj", proj_came))
    graph_came = swap_far(halve("graph", graph_came, z_high))
    graph_came = swap_far(total("graph", graph_came))
    (g_down,) = call(down_out_kernel, [held["down"], due(down_came)], [((FF_OWN, D), F32)])
    hold("g_down", g_down)
    graph_came = swap_near(join("graph", graph_came))
    proj_came = swap_x(join("proj", proj_came))
    (g_up,) = call(up_out_kernel, [held["up"], due(up_came)], [((OWN, FF), F32)])
    hold("g_up", g_up)
    graph_came = swap_x(join("graph", graph_came))
    g_query, g_key, g_value, g_out = call(
        project_out_kernel,
        [held["proj"], due(proj_came)],
        [((OWN, D), F32)] * 4,
        [((SEQ_WAYS, PIECE, 3 * OWN), F32)],
    )
    hold("g_query", g_query)
    (
        g_graph, g_gain_one, g_shift_one, g_gain_two, g_shift_two, g_bias_up, g_bias_down, g_rich_q,
        g_rich_k,
    ) = call(
        graph_out_kernel,
        [held["graph"], due(graph_came)],
        [((OWN, D), F32), *[((OWN,), F32)] * 4, ((FF_OWN,), F32), ((OWN,), F32),
         *[((HEAD_DIM // SEQ_WAYS, 4 * HEADS), F32)] * 2],
        [((GRP_WAYS, 16, HEAD_DIM), F32)],
    )
    grad_tokens, g_down, g_up, g_query = (held[key] for key in ("tokens", "g_down", "g_up", "g_query"))
    return (
        out_tokens, out_global, grad_tokens, grad_global,
        g_graph, g_gain_one, g_shift_one, g_query, g_key, g_value, g_rich_q, g_rich_k,
        g_out, g_gain_two, g_shift_two, g_up, g_bias_up, g_down, g_bias_down,
    )


def layer(*arrays):
    tokens, global_tokens = arrays[:2]
    ways = (lax.axis_size("seq"), lax.axis_size("grp"))
    if ways == (SEQ_WAYS, GRP_WAYS) and tokens.shape[0] == TOK and global_tokens.shape[0] == GLOBALS:
        return split_heads(*arrays)
    return local(*arrays)


def solution(mesh):
    return jax.shard_map(
        layer,
        mesh=mesh,
        in_specs=(
            P(("grp", "seq"), None),
            P("grp", None),
            P(("grp", "seq"), None),
            P(None, ("grp", "seq")),
            P(("grp", "seq")),
            P(),
            P(),
            P(),
            P(),
            P(),
            P(),
            P(),
            P(),
            P(),
            P(),
            P(),
            P(),
            P(),
            P(),
            P(),
            P(("grp", "seq"), None),
            P("grp", None),
        ),
        out_specs=(
            P(("grp", "seq"), None),
            P("grp", None),
            P(("grp", "seq"), None),
            P("grp", None),
            P("seq", None),
            P("seq"),
            P("seq"),
            P("seq", None),
            P("seq", None),
            P("seq", None),
            P("seq", None),
            P("seq", None),
            P("seq", None),
            P("seq"),
            P("seq"),
            P("seq", None),
            P("seq"),
            P("seq", None),
            P("seq"),
        ),
        check_vma=False,
    )
```

profile of v0, /device:TPU:0, one launch (start us, length us, event | category | flops | bytes accessed | tf_op | source)
XLA Modules:
  0.0 189.7 jit_solution(14594950128543719549)
XLA Ops:
  0.7 2.0 %shard_map.357.tok_a = bf16[128,896]{1,0:T(8,128)(2,1)} custom-call(bf16[128,768]{1,0:T(8,128)(2,1)} %tok_any.1, s32[8,128]{1,0:T(8,128)} %bitcast.72, s32[2,128]{1,0:T(2,128)} %rank_any.1, s32[1,128]{1,0:T(1,128)} %bitcast.73), custom_call_target="tpu_custom_call" | custom-call | flops 60000002048 | tf_op jit(solution)/shard_map/pallas_call | solution.py:1422
  2.7 3.0 %collective-permute-start.1 = (bf16[128,896]{1,0:T(8,128)(2,1)}, bf16[128,896]{1,0:T(8,128)(2,1)S(1)}, u32[]{:S(2)}, u32[]{:S(2)}) collective-permute-start(bf16[128,896]{1,0:T(8,128)(2,1)} %shard_map.357.tok_a), channel_id=1, source_target_pairs={{0,2},{2,0},{1,3},{3,1},{4,6},{6,4},{5,7},{7,5},{8,10},{10,8},{9,1... | collective-permute-start | bytes 688136 | tf_op jit(solution)/shard_map/ppermute | solution.py:634
  5.7 5.8 %collective-permute-done.1.tok_c = bf16[128,896]{1,0:T(8,128)(2,1)S(1)} collective-permute-done((bf16[128,896]{1,0:T(8,128)(2,1)}, bf16[128,896]{1,0:T(8,128)(2,1)S(1)}, u32[]{:S(2)}, u32[]{:S(2)}) %collective-permute-start.1) | collective-permute-done | bytes 229408 | tf_op jit(solution)/shard_map/ppermute | solution.py:634
  12.1 1.7 collective-permute-start.4
  14.8 17.6 %shard_map.358 = (bf16[288,384]{1,0:T(8,128)(2,1)S(1)}, f32[3,64,640]{2,1,0:T(8,128)S(1)}, f32[3,64,64]{2,1,0:T(8,128)S(1)}, f32[16,512]{1,0:T(8,128)S(1)}, bf16...) custom-call(bf16[128,896]{1,0:T(8,128)(2,1)S(1)} %copy-done.2, ...), custom_call_target="tpu_custom_call" | custom-call | flops 60000002048 | tf_op jit(solution)/shard_map/pallas_call | solution.py:1422
  35.0 6.1 %collective-permute-done.6.att_c = bf16[288,384]{1,0:T(8,128)(2,1)S(1)} collective-permute-done((bf16[288,384]{1,0:T(8,128)(2,1)S(1)}, bf16[288,384]{1,0:T(8,128)(2,1)S(1)}, u32[]{:S(2)}, u32[]{:S(2)}) %collective-permute-start.6) | collective-permute-done | bytes 221216 | tf_op jit(solution)/shard_map/ppermute | solution.py:634
  41.6 1.0 collective-permute-done.7.att_d
  42.6 9.8 %shard_map.359 = (bf16[128,768]{1,0:T(8,128)(2,1)}, bf16[176,768]{1,0:T(8,128)(2,1)S(1)}) custom-call(bf16[288,384]{1,0:T(8,128)(2,1)S(1)} %get-tuple-element.140.att_a.attn_ref, bf16[288,384]{1,0:T(8,128)(2,1)S(1)} %collective-permute-done.5.att_b, bf16[288,384]{1,0:T(8,128)(2,1)S(1)} %collective-permute-done.6.att_c, ...), custom_call_target="tpu_custom_call" | custom-call | flops 60000002048 | tf_op jit(solution)/shard_map/pallas_call | solution.py:1422
  52.4 1.4 collective-permute-start.10
  53.9 6.7 %shard_map.360 = (bf16[4,96,768]{2,1,0:T(8,128)(2,1)S(1)}, bf16[4,96,768]{2,1,0:T(8,128)(2,1)S(1)}, bf16[576,768]{1,0:T(8,128)(2,1)S(1)}, f32[576,768]{1,0:T(8,128)}, bf16[576,768]{1,0:T(8,128)(2,1)}) custom-call(bf16[288,384]{1,0:T(8,128)(2,1)S(1)} %get-tuple-element.140.att_a.attn_ref, bf16[288,384]{1,0:T(8,128)(2,1)S(1)} %collective-permute-done.5.att_b, ...), custom_call_target="tpu_custom_call" | custom-call | flops 60000002048 | tf_op jit(solution)/shard_map/pallas_call | solution.py:1422
  60.6 1.6 collective-permute-start.12
  62.3 1.2 copy-done.18
  63.5 4.6 %shard_map.361 = (bf16[4,96,768]{2,1,0:T(8,128)(2,1)S(1)}, bf16[4,96,768]{2,1,0:T(8,128)(2,1)S(1)}, f32[1,768]{1,0:T(1,128)S(1)}) custom-call(bf16[576,768]{1,0:T(8,128)(2,1)S(1)} %get-tuple-element.154.normed_ref, f32[576,768]{1,0:T(8,128)} %get-tuple-element.155.slope_ref, bf16[576,768]{1,0:T(8,128)(2,1)S(1)} %copy-done.18, bf16[3072,768]{1,0:T(8,128)(2,1)} %w_down_any.3), custom_call_target="tpu_custom_call" | custom-call | flops 60000002048 | tf_op jit(solution)/shard_map/pallas_call | solution.py:1422
  68.8 15.1 %shard_map.362 = (bf16[576,768]{1,0:T(8,128)(2,1)S(1)}, bf16[576,640]{1,0:T(8,128)(2,1)S(1)}, f32[8,768]{1,0:T(8,128)S(1)}, bf16[64,768]{1,0:T(8,128)(2,1)}) custom-call(bf16[176,768]{1,0:T(8,128)(2,1)S(1)} %get-tuple-element.144.back_a, bf16[176,768]{1,0:T(8,128)(2,1)S(1)} %collective-permute-done.8.back_b, ...), custom_call_target="tpu_custom_call" | custom-call | flops 60000002048 | tf_op jit(solution)/shard_map/pallas_call | solution.py:1422
  83.8 1.1 collective-permute-start.14
  85.1 1.6 collective-permute-start.16
  86.8 1.5 shard_map.363
  88.3 5.7 %collective-permute-done.16 = bf16[2,96,768]{2,1,0:T(8,128)(2,1)S(1)} collective-permute-done((bf16[2,96,768]{2,1,0:T(8,128)(2,1)S(1)}, bf16[2,96,768]{2,1,0:T(8,128)(2,1)S(1)}, u32[]{:S(2)}, u32[]{:S(2)}) %collective-permute-start.16) | collective-permute-done | bytes 294944 | tf_op jit(solution)/shard_map/ppermute | solution.py:665
  94.8 2.6 %collective-permute-start.18 = (bf16[1,96,768]{2,1,0:T(8,128)(2,1)}, bf16[1,96,768]{2,1,0:T(8,128)(2,1)}, u32[]{:S(2)}, u32[]{:S(2)}) collective-permute-start(bf16[1,96,768]{2,1,0:T(8,128)(2,1)} %get-tuple-element.265), channel_id=1, source_target_pairs={{0,16},{4,20},{8,24},{12,28},{16,0},{20,4},{24,8},{28,12},{1,17},{... | collective-permute-start | bytes 442376 | tf_op jit(solution)/shard_map/ppermute | solution.py:669
  98.3 1.6 collective-permute-start.17
  100.8 1.5 collective-permute-done.14.dqkv_c
  102.3 1.7 collective-permute-done.18
  105.0 1.1 collective-permute-start.23
  106.1 3.8 %collective-permute-done.17 = bf16[2,96,768]{2,1,0:T(8,128)(2,1)S(1)} collective-permute-done((bf16[2,96,768]{2,1,0:T(8,128)(2,1)}, bf16[2,96,768]{2,1,0:T(8,128)(2,1)S(1)}, u32[]{:S(2)}, u32[]{:S(2)}) %collective-permute-start.17) | collective-permute-done | bytes 294944 | tf_op jit(solution)/shard_map/ppermute | solution.py:665
  110.0 5.6 %collective-permute-done.13 = bf16[4,96,768]{2,1,0:T(8,128)(2,1)S(1)} collective-permute-done((bf16[4,96,768]{2,1,0:T(8,128)(2,1)S(1)}, bf16[4,96,768]{2,1,0:T(8,128)(2,1)S(1)}, u32[]{:S(2)}, u32[]{:S(2)}) %collective-permute-start.13) | collective-permute-done | bytes 589856 | tf_op jit(solution)/shard_map/ppermute | solution.py:661
  116.8 10.0 %shard_map.364 = (f32[64,768]{1,0:T(8,128)}, bf16[4,32,768]{2,1,0:T(8,128)(2,1)S(1)}, bf16[4,32,768]{2,1,0:T(8,128)(2,1)S(1)}, f32[128,768]{1,0:T(8,128)S(1)}, bf16[512,768]{1,0:T(8,128)(2,1)}) custom-call(bf16[576,640]{1,0:T(8,128)(2,1)S(1)} %get-tuple-element.166.d_qkv_ref.dqkv_a, bf16[576,640]{1,0:T(8,128)(2,1)S(1)} %collective-permute-done.20.dqkv_b, ...), custom_call_target="tpu_custom_call" | custom-call | flops 60000002048 | tf_op jit(solution)/shard_map/pallas_call | solution.py:1422
  128.1 1.7 collective-permute-start.28
  129.8 1.6 collective-permute-start.27
  132.4 1.4 collective-permute-start.25
  133.8 3.5 %shard_map.365 = f32[128,768]{1,0:T(8,128)} custom-call(f32[128,768]{1,0:T(8,128)S(1)} %get-tuple-element.199.d_own_ref, bf16[512,768]{1,0:T(8,128)(2,1)S(1)} %copy-done.21, f32[16,512]{1,0:T(8,128)S(1)} %get-tuple-element.158.meta_row_ref, bf16[768,768]{1,0:T(8,128)(2,1)S(1)} %copy-done.1), custom_call_target="tpu_custom_call" | custom-call | flops 60000002048 | tf_op jit(solution)/shard_map/pallas_call | solution.py:1422
  138.7 4.6 %collective-permute-done.27 = bf16[2,96,768]{2,1,0:T(8,128)(2,1)S(1)} collective-permute-done((bf16[2,96,768]{2,1,0:T(8,128)(2,1)S(1)}, bf16[2,96,768]{2,1,0:T(8,128)(2,1)S(1)}, u32[]{:S(2)}, u32[]{:S(2)}) %collective-permute-start.27) | collective-permute-done | bytes 294944 | tf_op jit(solution)/shard_map/ppermute | solution.py:665
  143.3 1.5 collective-permute-start.36
  145.0 1.6 collective-permute-start.33
  146.7 2.0 %collective-permute-start.29 = (bf16[2,32,768]{2,1,0:T(8,128)(2,1)S(1)}, bf16[2,32,768]{2,1,0:T(8,128)(2,1)S(1)}, u32[]{:S(2)}, u32[]{:S(2)}) collective-permute-start(bf16[2,32,768]{2,1,0:T(8,128)(2,1)S(1)} %get-tuple-element.268), channel_id=1, source_target_pairs={{0,8},{4,12},{8,0},{12,4},{16,24},{20,28},{24,16},{28,20},{1,9},{5... | collective-permute-start | bytes 294920 | tf_op jit(solution)/shard_map/ppermute | solution.py:665
  149.4 1.0 collective-permute-start.34
  150.4 8.3 %collective-permute-done.32 = bf16[2,96,768]{2,1,0:T(8,128)(2,1)S(1)} collective-permute-done((bf16[2,96,768]{2,1,0:T(8,128)(2,1)S(1)}, bf16[2,96,768]{2,1,0:T(8,128)(2,1)S(1)}, u32[]{:S(2)}, u32[]{:S(2)}) %collective-permute-start.32) | collective-permute-done | bytes 294944 | tf_op jit(solution)/shard_map/ppermute | solution.py:665
  159.1 2.3 %collective-permute-start.35 = (bf16[2,96,768]{2,1,0:T(8,128)(2,1)S(1)}, bf16[2,96,768]{2,1,0:T(8,128)(2,1)S(1)}, u32[]{:S(2)}, u32[]{:S(2)}) collective-permute-start(bf16[2,96,768]{2,1,0:T(8,128)(2,1)S(1)} %constant_dynamic-update-slice_fusion.8), channel_id=1, source_target_pairs={{0,8},{4,12},{8,0},{12,4},{16,24},{20,28},{24,16},{28,20},{1,9},{5... | collective-permute-start | bytes 884744 | tf_op jit(solution)/shard_map/ppermute | solution.py:665
  161.4 1.2 collective-permute-start.37
  162.6 4.0 %collective-permute-done.37 = bf16[1,32,768]{2,1,0:T(8,128)(2,1)S(1)} collective-permute-done((bf16[1,32,768]{2,1,0:T(8,128)(2,1)S(1)}, bf16[1,32,768]{2,1,0:T(8,128)(2,1)S(1)}, u32[]{:S(2)}, u32[]{:S(2)}) %collective-permute-start.37) | collective-permute-done | bytes 49184 | tf_op jit(solution)/shard_map/ppermute | solution.py:669
  166.7 3.4 %collective-permute-start.38 = (bf16[1,32,768]{2,1,0:T(8,128)(2,1)S(1)}, bf16[1,32,768]{2,1,0:T(8,128)(2,1)S(1)}, u32[]{:S(2)}, u32[]{:S(2)}) collective-permute-start(bf16[1,32,768]{2,1,0:T(8,128)(2,1)S(1)} %add_convert_fusion.11), channel_id=1, source_target_pairs={{0,16},{4,20},{8,24},{12,28},{16,0},{20,4},{24,8},{28,12},{1,17},{... | collective-permute-start | bytes 147464 | tf_op jit(solution)/shard_map/ppermute | solution.py:669
  170.1 1.6 shard_map.366
  172.3 2.3 %collective-permute-start.40 = (bf16[2,32,768]{2,1,0:T(8,128)(2,1)S(1)}, bf16[2,32,768]{2,1,0:T(8,128)(2,1)S(1)}, u32[]{:S(2)}, u32[]{:S(2)}) collective-permute-start(bf16[2,32,768]{2,1,0:T(8,128)(2,1)S(1)} %constant_dynamic-update-slice_fusion.10), channel_id=1, source_target_pairs={{0,8},{4,12},{8,0},{12,4},{16,24},{20,28},{24,16},{28,20},{1,9},{5... | collective-permute-start | bytes 294920 | tf_op jit(solution)/shard_map/ppermute | solution.py:665
  174.6 1.1 collective-permute-start.39
  175.7 1.6 shard_map.367
  177.3 1.0 collective-permute-start.42
  178.3 8.2 %collective-permute-done.39.came = bf16[4,96,768]{2,1,0:T(8,128)(2,1)S(1)} collective-permute-done((bf16[4,96,768]{2,1,0:T(8,128)(2,1)S(1)}, bf16[4,96,768]{2,1,0:T(8,128)(2,1)S(1)}, u32[]{:S(2)}, u32[]{:S(2)}) %collective-permute-start.39) | collective-permute-done | bytes 589856 | tf_op jit(solution)/shard_map/ppermute | solution.py:661
  186.6 2.0 %shard_map.368 = (f32[192,768]{1,0:T(8,128)}, f32[192,768]{1,0:T(8,128)}, f32[192,768]{1,0:T(8,128)}, f32[192,768]{1,0:T(8,128)}) custom-call(bf16[4,96,768]{2,1,0:T(8,128)(2,1)S(1)} %constant_dynamic-update-slice_fusion.12.held, bf16[4,96,768]{2,1,0:T(8,128)(2,1)S(1)} %collective-permute-done.39.came), custom_call_target="tpu_custom_call" | custom-call | flops 60000002048 | tf_op jit(solution)/shard_map/pallas_call | solution.py:1422
  188.7 1.1 shard_map.369
  (153 shorter events, 16.0 us)
Async XLA Ops:
  2.7 8.8 %collective-permute-start.1 = (bf16[128,896]{1,0:T(8,128)(2,1)}, bf16[128,896]{1,0:T(8,128)(2,1)S(1)}, u32[]{:S(2)}, u32[]{:S(2)}) collective-permute-start(bf16[128,896]{1,0:T(8,128)(2,1)} %shard_map.357.tok_a), channel_id=1, source_target_pairs={{0,2},{2,0},{1,3},{3,1},{4,6},{6,4},{5,7},{7,5},{8,10},{10,8},{9,1... | collective-permute-start | bytes 688136 | tf_op jit(solution)/shard_map/ppermute | solution.py:634
  5.7 8.1 %collective-permute-start = (bf16[128,896]{1,0:T(8,128)(2,1)}, bf16[128,896]{1,0:T(8,128)(2,1)S(1)}, u32[]{:S(2)}, u32[]{:S(2)}) collective-permute-start(bf16[128,896]{1,0:T(8,128)(2,1)} %shard_map.357.tok_a), channel_id=1, source_target_pairs={{0,1},{1,0},{2,3},{3,2},{4,5},{5,4},{6,7},{7,6},{8,9},{9,8},{10,11... | collective-permute-start | bytes 688136 | tf_op jit(solution)/shard_map/ppermute | solution.py:634
  11.5 2.3 %collective-permute-start.2 = (bf16[128,896]{1,0:T(8,128)(2,1)S(1)}, bf16[128,896]{1,0:T(8,128)(2,1)S(1)}, u32[]{:S(2)}, u32[]{:S(2)}) collective-permute-start(bf16[128,896]{1,0:T(8,128)(2,1)S(1)} %collective-permute-done.1.tok_c), channel_id=1, source_target_pairs={{0,1},{1,0},{2,3},{3,2},{4,5},{5,4},{6,7},{7,6},{8,9},{9,8},{10,11... | collective-permute-start | bytes 688136 | tf_op jit(solution)/shard_map/ppermute | solution.py:1451
  11.5 22.5 %collective-permute-start.3 = (bf16[128,768]{1,0:T(8,128)(2,1)S(1)}, bf16[128,768]{1,0:T(8,128)(2,1)S(1)}, u32[]{:S(2)}, u32[]{:S(2)}) collective-permute-start(bf16[128,768]{1,0:T(8,128)(2,1)S(1)} %copy-done.3), channel_id=1, source_target_pairs={{0,1},{1,0},{2,3},{3,2},{4,5},{5,4},{6,7},{7,6},{8,9},{9,8},{10,11... | collective-permute-start | bytes 589832 | tf_op jit(solution)/shard_map/ppermute | solution.py:634
  12.1 22.0 %collective-permute-start.4 = (bf16[128,768]{1,0:T(8,128)(2,1)S(1)}, bf16[128,768]{1,0:T(8,128)(2,1)S(1)}, u32[]{:S(2)}, u32[]{:S(2)}) collective-permute-start(bf16[128,768]{1,0:T(8,128)(2,1)S(1)} %copy-done.3), channel_id=1, source_target_pairs={{0,2},{2,0},{1,3},{3,1},{4,6},{6,4},{5,7},{7,5},{8,10},{10,8},{9,1... | collective-permute-start | bytes 589832 | tf_op jit(solution)/shard_map/ppermute | solution.py:634
  14.8 27.8 %copy-start.4 = (bf16[64,768]{1,0:T(8,128)(2,1)S(1)}, bf16[64,768]{1,0:T(8,128)(2,1)}, u32[]{:S(2)}) copy-start(bf16[64,768]{1,0:T(8,128)(2,1)} %cot_glob_ref.1) | copy-start | bytes 294916
  14.8 27.8 %copy-start.7 = (f32[3072]{0:T(1024)S(1)}, f32[3072]{0:T(1024)}, u32[]{:S(2)}) copy-start(f32[3072]{0:T(1024)} %bias_ref.1) | copy-start | bytes 36868
  14.8 27.8 %copy-start.12 = (f32[768]{0:T(1024)S(1)}, f32[768]{0:T(1024)}, u32[]{:S(2)}) copy-start(f32[768]{0:T(1024)} %bias_down_ref.1) | copy-start | bytes 9220
  14.8 27.8 %copy-start.13 = (f32[768]{0:T(1024)S(1)}, f32[768]{0:T(1024)}, u32[]{:S(2)}) copy-start(f32[768]{0:T(1024)} %gain_ref.5) | copy-start | bytes 9220
  14.8 27.8 %copy-start.14 = (f32[768]{0:T(1024)S(1)}, f32[768]{0:T(1024)}, u32[]{:S(2)}) copy-start(f32[768]{0:T(1024)} %shift_ref.5) | copy-start | bytes 9220
  34.0 7.1 %collective-permute-start.6 = (bf16[288,384]{1,0:T(8,128)(2,1)S(1)}, bf16[288,384]{1,0:T(8,128)(2,1)S(1)}, u32[]{:S(2)}, u32[]{:S(2)}) collective-permute-start(bf16[288,384]{1,0:T(8,128)(2,1)S(1)} %get-tuple-element.140.att_a.attn_ref), channel_id=1, source_target_pairs={{0,2},{2,0},{1,3},{3,1},{4,6},{6,4},{5,7},{7,5},{8,10},{10,8},{9,1... | collective-permute-start | bytes 663560 | tf_op jit(solution)/shard_map/ppermute | solution.py:634
  35.0 6.6 %collective-permute-start.5 = (bf16[288,384]{1,0:T(8,128)(2,1)S(1)}, bf16[288,384]{1,0:T(8,128)(2,1)S(1)}, u32[]{:S(2)}, u32[]{:S(2)}) collective-permute-start(bf16[288,384]{1,0:T(8,128)(2,1)S(1)} %get-tuple-element.140.att_a.attn_ref), channel_id=1, source_target_pairs={{0,1},{1,0},{2,3},{3,2},{4,5},{5,4},{6,7},{7,6},{8,9},{9,8},{10,11... | collective-permute-start | bytes 663560 | tf_op jit(solution)/shard_map/ppermute | solution.py:634
  41.1 1.5 collective-permute-start.7
  41.1 12.8 %collective-permute-start.9 = (bf16[128,768]{1,0:T(8,128)(2,1)S(1)}, bf16[128,768]{1,0:T(8,128)(2,1)S(1)}, u32[]{:S(2)}, u32[]{:S(2)}) collective-permute-start(bf16[128,768]{1,0:T(8,128)(2,1)S(1)} %collective-permute-done.4.cot_c), channel_id=1, source_target_pairs={{0,1},{1,0},{2,3},{3,2},{4,5},{5,4},{6,7},{7,6},{8,9},{9,8},{10,11... | collective-permute-start | bytes 589832 | tf_op jit(solution)/shard_map/ppermute | solution.py:1482
  52.4 9.7 %collective-permute-start.10 = (bf16[176,768]{1,0:T(8,128)(2,1)S(1)}, bf16[176,768]{1,0:T(8,128)(2,1)S(1)}, u32[]{:S(2)}, u32[]{:S(2)}) collective-permute-start(bf16[176,768]{1,0:T(8,128)(2,1)S(1)} %get-tuple-element.144.back_a), channel_id=1, source_target_pairs={{0,2},{2,0},{1,3},{3,1},{4,6},{6,4},{5,7},{7,5},{8,10},{10,8},{9,1... | collective-permute-start | bytes 811016 | tf_op jit(solution)/shard_map/ppermute | solution.py:634
  53.9 14.9 %collective-permute-start.8 = (bf16[176,768]{1,0:T(8,128)(2,1)S(1)}, bf16[176,768]{1,0:T(8,128)(2,1)S(1)}, u32[]{:S(2)}, u32[]{:S(2)}) collective-permute-start(bf16[176,768]{1,0:T(8,128)(2,1)S(1)} %get-tuple-element.144.back_a), channel_id=1, source_target_pairs={{0,1},{1,0},{2,3},{3,2},{4,5},{5,4},{6,7},{7,6},{8,9},{9,8},{10,11... | collective-permute-start | bytes 811016 | tf_op jit(solution)/shard_map/ppermute | solution.py:634
  60.6 24.4 %collective-permute-start.12 = (bf16[4,96,768]{2,1,0:T(8,128)(2,1)S(1)}, bf16[4,96,768]{2,1,0:T(8,128)(2,1)S(1)}, u32[]{:S(2)}, u32[]{:S(2)}) collective-permute-start(bf16[4,96,768]{2,1,0:T(8,128)(2,1)S(1)} %get-tuple-element.165), channel_id=1, source_target_pairs={{0,4},{4,0},{8,12},{12,8},{16,20},{20,16},{24,28},{28,24},{1,5},{5... | collective-permute-start | bytes 1769480 | tf_op jit(solution)/shard_map/ppermute | solution.py:661
  62.1 6.6 %collective-permute-start.11 = (bf16[176,768]{1,0:T(8,128)(2,1)S(1)}, bf16[176,768]{1,0:T(8,128)(2,1)S(1)}, u32[]{:S(2)}, u32[]{:S(2)}) collective-permute-start(bf16[176,768]{1,0:T(8,128)(2,1)S(1)} %collective-permute-done.10.back_c), channel_id=1, source_target_pairs={{0,1},{1,0},{2,3},{3,2},{4,5},{5,4},{6,7},{7,6},{8,9},{9,8},{10,11... | collective-permute-start | bytes 811016 | tf_op jit(solution)/shard_map/ppermute | solution.py:1507
  68.2 26.7 %collective-permute-start.15 = (bf16[4,96,768]{2,1,0:T(8,128)(2,1)S(1)}, bf16[4,96,768]{2,1,0:T(8,128)(2,1)S(1)}, u32[]{:S(2)}, u32[]{:S(2)}) collective-permute-start(bf16[4,96,768]{2,1,0:T(8,128)(2,1)S(1)} %get-tuple-element.172), channel_id=1, source_target_pairs={{0,4},{4,0},{8,12},{12,8},{16,20},{20,16},{24,28},{28,24},{1,5},{5... | collective-permute-start | bytes 1769480 | tf_op jit(solution)/shard_map/ppermute | solution.py:661
  83.8 18.5 %collective-permute-start.14 = (bf16[576,640]{1,0:T(8,128)(2,1)S(1)}, bf16[576,640]{1,0:T(8,128)(2,1)S(1)}, u32[]{:S(2)}, u32[]{:S(2)}) collective-permute-start(bf16[576,640]{1,0:T(8,128)(2,1)S(1)} %get-tuple-element.166.d_qkv_ref.dqkv_a), channel_id=1, source_target_pairs={{0,2},{2,0},{1,3},{3,1},{4,6},{6,4},{5,7},{7,5},{8,10},{10,8},{9,1... | collective-permute-start | bytes 2211848 | tf_op jit(solution)/shard_map/ppermute | solution.py:634
  85.1 8.9 %collective-permute-start.16 = (bf16[2,96,768]{2,1,0:T(8,128)(2,1)S(1)}, bf16[2,96,768]{2,1,0:T(8,128)(2,1)S(1)}, u32[]{:S(2)}, u32[]{:S(2)}) collective-permute-start(bf16[2,96,768]{2,1,0:T(8,128)(2,1)S(1)} %get-tuple-element.260), channel_id=1, source_target_pairs={{0,8},{4,12},{8,0},{12,4},{16,24},{20,28},{24,16},{28,20},{1,9},{5... | collective-permute-start | bytes 884744 | tf_op jit(solution)/shard_map/ppermute | solution.py:665
  94.8 9.2 %collective-permute-start.18 = (bf16[1,96,768]{2,1,0:T(8,128)(2,1)}, bf16[1,96,768]{2,1,0:T(8,128)(2,1)}, u32[]{:S(2)}, u32[]{:S(2)}) collective-permute-start(bf16[1,96,768]{2,1,0:T(8,128)(2,1)} %get-tuple-element.265), channel_id=1, source_target_pairs={{0,16},{4,20},{8,24},{12,28},{16,0},{20,4},{24,8},{28,12},{1,17},{... | collective-permute-start | bytes 442376 | tf_op jit(solution)/shard_map/ppermute | solution.py:669
  98.3 11.6 %collective-permute-start.17 = (bf16[2,96,768]{2,1,0:T(8,128)(2,1)}, bf16[2,96,768]{2,1,0:T(8,128)(2,1)S(1)}, u32[]{:S(2)}, u32[]{:S(2)}) collective-permute-start(bf16[2,96,768]{2,1,0:T(8,128)(2,1)} %get-tuple-element.258), channel_id=1, source_target_pairs={{0,8},{4,12},{8,0},{12,4},{16,24},{20,28},{24,16},{28,20},{1,9},{5... | collective-permute-start | bytes 884744 | tf_op jit(solution)/shard_map/ppermute | solution.py:665
  99.9 16.9 %collective-permute-start.20 = (bf16[576,640]{1,0:T(8,128)(2,1)S(1)}, bf16[576,640]{1,0:T(8,128)(2,1)S(1)}, u32[]{:S(2)}, u32[]{:S(2)}) collective-permute-start(bf16[576,640]{1,0:T(8,128)(2,1)S(1)} %get-tuple-element.166.d_qkv_ref.dqkv_a), channel_id=1, source_target_pairs={{0,1},{1,0},{2,3},{3,2},{4,5},{5,4},{6,7},{7,6},{8,9},{9,8},{10,11... | collective-permute-start | bytes 2211848 | tf_op jit(solution)/shard_map/ppermute | solution.py:634
  99.9 15.7 %collective-permute-start.13 = (bf16[4,96,768]{2,1,0:T(8,128)(2,1)S(1)}, bf16[4,96,768]{2,1,0:T(8,128)(2,1)S(1)}, u32[]{:S(2)}, u32[]{:S(2)}) collective-permute-start(bf16[4,96,768]{2,1,0:T(8,128)(2,1)S(1)} %get-tuple-element.170), channel_id=1, source_target_pairs={{0,4},{4,0},{8,12},{12,8},{16,20},{20,16},{24,28},{28,24},{1,5},{5... | collective-permute-start | bytes 1769480 | tf_op jit(solution)/shard_map/ppermute | solution.py:661
  102.3 14.4 %collective-permute-start.21 = (bf16[576,640]{1,0:T(8,128)(2,1)S(1)}, bf16[576,640]{1,0:T(8,128)(2,1)S(1)}, u32[]{:S(2)}, u32[]{:S(2)}) collective-permute-start(bf16[576,640]{1,0:T(8,128)(2,1)S(1)} %collective-permute-done.14.dqkv_c), channel_id=1, source_target_pairs={{0,1},{1,0},{2,3},{3,2},{4,5},{5,4},{6,7},{7,6},{8,9},{9,8},{10,11... | collective-permute-start | bytes 2211848 | tf_op jit(solution)/shard_map/ppermute | solution.py:1568
  105.0 22.9 %collective-permute-start.23 = (bf16[1,96,768]{2,1,0:T(8,128)(2,1)S(1)}, bf16[1,96,768]{2,1,0:T(8,128)(2,1)S(1)}, u32[]{:S(2)}, u32[]{:S(2)}) collective-permute-start(bf16[1,96,768]{2,1,0:T(8,128)(2,1)S(1)} %add_convert_fusion.9), channel_id=1, source_target_pairs={{0,16},{4,20},{8,24},{12,28},{16,0},{20,4},{24,8},{28,12},{1,17},{... | collective-permute-start | bytes 442376 | tf_op jit(solution)/shard_map/ppermute | solution.py:669
  115.9 10.9 %collective-permute-start.19 = (bf16[1,96,768]{2,1,0:T(8,128)(2,1)S(1)}, bf16[1,96,768]{2,1,0:T(8,128)(2,1)S(1)}, u32[]{:S(2)}, u32[]{:S(2)}) collective-permute-start(bf16[1,96,768]{2,1,0:T(8,128)(2,1)S(1)} %get-tuple-element.264), channel_id=1, source_target_pairs={{0,16},{4,20},{8,24},{12,28},{16,0},{20,4},{24,8},{28,12},{1,17},{... | collective-permute-start | bytes 442376 | tf_op jit(solution)/shard_map/ppermute | solution.py:669
  116.3 11.5 %collective-permute-start.24 = (bf16[2,96,768]{2,1,0:T(8,128)(2,1)S(1)}, bf16[2,96,768]{2,1,0:T(8,128)(2,1)S(1)}, u32[]{:S(2)}, u32[]{:S(2)}) collective-permute-start(bf16[2,96,768]{2,1,0:T(8,128)(2,1)S(1)} %get-tuple-element.255), channel_id=1, source_target_pairs={{0,8},{4,12},{8,0},{12,4},{16,24},{20,28},{24,16},{28,20},{1,9},{5... | collective-permute-start | bytes 884744 | tf_op jit(solution)/shard_map/ppermute | solution.py:665
  128.0 4.4 %collective-permute-start.22 = (bf16[2,24,768]{2,1,0:T(8,128)(2,1)S(1)}, bf16[2,24,768]{2,1,0:T(8,128)(2,1)S(1)}, u32[]{:S(2)}, u32[]{:S(2)}) collective-permute-start(bf16[2,24,768]{2,1,0:T(8,128)(2,1)S(1)} %pad_maximum_fusion), channel_id=1, source_target_pairs={{0,1},{1,0},{2,3},{3,2},{4,5},{5,4},{6,7},{7,6},{8,9},{9,8},{10,11... | collective-permute-start | bytes 221192 | tf_op jit(solution)/shard_map/ppermute | solution.py:644
  128.1 10.4 %collective-permute-start.28 = (bf16[1,96,768]{2,1,0:T(8,128)(2,1)S(1)}, bf16[1,96,768]{2,1,0:T(8,128)(2,1)S(1)}, u32[]{:S(2)}, u32[]{:S(2)}) collective-permute-start(bf16[1,96,768]{2,1,0:T(8,128)(2,1)S(1)} %get-tuple-element.261), channel_id=1, source_target_pairs={{0,16},{4,20},{8,24},{12,28},{16,0},{20,4},{24,8},{28,12},{1,17},{... | collective-permute-start | bytes 442376 | tf_op jit(solution)/shard_map/ppermute | solution.py:669
  129.8 13.5 %collective-permute-start.27 = (bf16[2,96,768]{2,1,0:T(8,128)(2,1)S(1)}, bf16[2,96,768]{2,1,0:T(8,128)(2,1)S(1)}, u32[]{:S(2)}, u32[]{:S(2)}) collective-permute-start(bf16[2,96,768]{2,1,0:T(8,128)(2,1)S(1)} %constant_dynamic-update-slice_fusion), channel_id=1, source_target_pairs={{0,8},{4,12},{8,0},{12,4},{16,24},{20,28},{24,16},{28,20},{1,9},{5... | collective-permute-start | bytes 884744 | tf_op jit(solution)/shard_map/ppermute | solution.py:665
  131.5 13.3 %collective-permute-start.26 = (bf16[4,32,768]{2,1,0:T(8,128)(2,1)S(1)}, bf16[4,32,768]{2,1,0:T(8,128)(2,1)S(1)}, u32[]{:S(2)}, u32[]{:S(2)}) collective-permute-start(bf16[4,32,768]{2,1,0:T(8,128)(2,1)S(1)} %get-tuple-element.204), channel_id=1, source_target_pairs={{0,4},{4,0},{8,12},{12,8},{16,20},{20,16},{24,28},{28,24},{1,5},{5... | collective-permute-start | bytes 589832 | tf_op jit(solution)/shard_map/ppermute | solution.py:661
  132.4 5.0 %collective-permute-start.25 = (bf16[2,24,768]{2,1,0:T(8,128)(2,1)S(1)}, bf16[2,24,768]{2,1,0:T(8,128)(2,1)S(1)}, u32[]{:S(2)}, u32[]{:S(2)}) collective-permute-start(bf16[2,24,768]{2,1,0:T(8,128)(2,1)S(1)} %pad_maximum_fusion.1), channel_id=1, source_target_pairs={{0,2},{2,0},{1,3},{3,1},{4,6},{6,4},{5,7},{7,5},{8,10},{10,8},{9,1... | collective-permute-start | bytes 221192 | tf_op jit(solution)/shard_map/ppermute | solution.py:1591
  137.4 9.2 %collective-permute-start.30 = (bf16[1,96,768]{2,1,0:T(8,128)(2,1)S(1)}, bf16[1,96,768]{2,1,0:T(8,128)(2,1)S(1)}, u32[]{:S(2)}, u32[]{:S(2)}) collective-permute-start(bf16[1,96,768]{2,1,0:T(8,128)(2,1)S(1)} %maximum_bitcast_fusion), channel_id=1, source_target_pairs={{0,16},{4,20},{8,24},{12,28},{16,0},{20,4},{24,8},{28,12},{1,17},{... | collective-permute-start | bytes 442376 | tf_op jit(solution)/shard_map/ppermute | solution.py:669
  138.6 6.3 %collective-permute-start.31 = (bf16[2,24,576]{2,1,0:T(8,128)(2,1)S(1)}, bf16[2,24,576]{2,1,0:T(8,128)(2,1)S(1)}, u32[]{:S(2)}, u32[]{:S(2)}) collective-permute-start(bf16[2,24,576]{2,1,0:T(8,128)(2,1)S(1)} %pad_maximum_fusion.2), channel_id=1, source_target_pairs={{0,1},{1,0},{2,3},{3,2},{4,5},{5,4},{6,7},{7,6},{8,9},{9,8},{10,11... | collective-permute-start | bytes 165896 | tf_op jit(solution)/shard_map/ppermute | solution.py:644
  143.3 26.8 %collective-permute-start.36 = (bf16[4,96,768]{2,1,0:T(8,128)(2,1)S(1)}, bf16[4,96,768]{2,1,0:T(8,128)(2,1)S(1)}, u32[]{:S(2)}, u32[]{:S(2)}) collective-permute-start(bf16[4,96,768]{2,1,0:T(8,128)(2,1)S(1)} %constant_dynamic-update-slice_fusion.2.held), channel_id=1, source_target_pairs={{0,4},{4,0},{8,12},{12,8},{16,20},{20,16},{24,28},{28,24},{1,5},{5... | collective-permute-start | bytes 1769480 | tf_op jit(solution)/shard_map/ppermute | solution.py:661
  145.0 4.3 %collective-permute-start.33 = (bf16[2,24,576]{2,1,0:T(8,128)(2,1)S(1)}, bf16[2,24,576]{2,1,0:T(8,128)(2,1)S(1)}, u32[]{:S(2)}, u32[]{:S(2)}) collective-permute-start(bf16[2,24,576]{2,1,0:T(8,128)(2,1)S(1)} %pad_maximum_fusion.3), channel_id=1, source_target_pairs={{0,2},{2,0},{1,3},{3,1},{4,6},{6,4},{5,7},{7,5},{8,10},{10,8},{9,1... | collective-permute-start | bytes 165896 | tf_op jit(solution)/shard_map/ppermute | solution.py:1605
  146.7 12.0 %collective-permute-start.32 = (bf16[2,96,768]{2,1,0:T(8,128)(2,1)S(1)}, bf16[2,96,768]{2,1,0:T(8,128)(2,1)S(1)}, u32[]{:S(2)}, u32[]{:S(2)}) collective-permute-start(bf16[2,96,768]{2,1,0:T(8,128)(2,1)S(1)} %constant_dynamic-update-slice_fusion.4), channel_id=1, source_target_pairs={{0,8},{4,12},{8,0},{12,4},{16,24},{20,28},{24,16},{28,20},{1,9},{5... | collective-permute-start | bytes 884744 | tf_op jit(solution)/shard_map/ppermute | solution.py:665
  146.7 14.6 %collective-permute-start.29 = (bf16[2,32,768]{2,1,0:T(8,128)(2,1)S(1)}, bf16[2,32,768]{2,1,0:T(8,128)(2,1)S(1)}, u32[]{:S(2)}, u32[]{:S(2)}) collective-permute-start(bf16[2,32,768]{2,1,0:T(8,128)(2,1)S(1)} %get-tuple-element.268), channel_id=1, source_target_pairs={{0,8},{4,12},{8,0},{12,4},{16,24},{20,28},{24,16},{28,20},{1,9},{5... | collective-permute-start | bytes 294920 | tf_op jit(solution)/shard_map/ppermute | solution.py:665
  149.4 9.7 %collective-permute-start.34 = (bf16[1,96,768]{2,1,0:T(8,128)(2,1)S(1)}, bf16[1,96,768]{2,1,0:T(8,128)(2,1)S(1)}, u32[]{:S(2)}, u32[]{:S(2)}) collective-permute-start(bf16[1,96,768]{2,1,0:T(8,128)(2,1)S(1)} %maximum_bitcast_fusion.1), channel_id=1, source_target_pairs={{0,16},{4,20},{8,24},{12,28},{16,0},{20,4},{24,8},{28,12},{1,17},{... | collective-permute-start | bytes 442376 | tf_op jit(solution)/shard_map/ppermute | solution.py:669
  158.7 17.1 %collective-permute-start.41 = (bf16[4,96,768]{2,1,0:T(8,128)(2,1)S(1)}, bf16[4,96,768]{2,1,0:T(8,128)(2,1)S(1)}, u32[]{:S(2)}, u32[]{:S(2)}) collective-permute-start(bf16[4,96,768]{2,1,0:T(8,128)(2,1)S(1)} %constant_dynamic-update-slice_fusion.6.held), channel_id=1, source_target_pairs={{0,4},{4,0},{8,12},{12,8},{16,20},{20,16},{24,28},{28,24},{1,5},{5... | collective-permute-start | bytes 1769480 | tf_op jit(solution)/shard_map/ppermute | solution.py:661
  159.1 15.5 %collective-permute-start.35 = (bf16[2,96,768]{2,1,0:T(8,128)(2,1)S(1)}, bf16[2,96,768]{2,1,0:T(8,128)(2,1)S(1)}, u32[]{:S(2)}, u32[]{:S(2)}) collective-permute-start(bf16[2,96,768]{2,1,0:T(8,128)(2,1)S(1)} %constant_dynamic-update-slice_fusion.8), channel_id=1, source_target_pairs={{0,8},{4,12},{8,0},{12,4},{16,24},{20,28},{24,16},{28,20},{1,9},{5... | collective-permute-start | bytes 884744 | tf_op jit(solution)/shard_map/ppermute | solution.py:665
  161.4 5.3 %collective-permute-start.37 = (bf16[1,32,768]{2,1,0:T(8,128)(2,1)S(1)}, bf16[1,32,768]{2,1,0:T(8,128)(2,1)S(1)}, u32[]{:S(2)}, u32[]{:S(2)}) collective-permute-start(bf16[1,32,768]{2,1,0:T(8,128)(2,1)S(1)} %get-tuple-element.278), channel_id=1, source_target_pairs={{0,16},{4,20},{8,24},{12,28},{16,0},{20,4},{24,8},{28,12},{1,17},{... | collective-permute-start | bytes 147464 | tf_op jit(solution)/shard_map/ppermute | solution.py:669
  166.7 5.6 %collective-permute-start.38 = (bf16[1,32,768]{2,1,0:T(8,128)(2,1)S(1)}, bf16[1,32,768]{2,1,0:T(8,128)(2,1)S(1)}, u32[]{:S(2)}, u32[]{:S(2)}) collective-permute-start(bf16[1,32,768]{2,1,0:T(8,128)(2,1)S(1)} %add_convert_fusion.11), channel_id=1, source_target_pairs={{0,16},{4,20},{8,24},{12,28},{16,0},{20,4},{24,8},{28,12},{1,17},{... | collective-permute-start | bytes 147464 | tf_op jit(solution)/shard_map/ppermute | solution.py:669
  172.3 5.0 %collective-permute-start.40 = (bf16[2,32,768]{2,1,0:T(8,128)(2,1)S(1)}, bf16[2,32,768]{2,1,0:T(8,128)(2,1)S(1)}, u32[]{:S(2)}, u32[]{:S(2)}) collective-permute-start(bf16[2,32,768]{2,1,0:T(8,128)(2,1)S(1)} %constant_dynamic-update-slice_fusion.10), channel_id=1, source_target_pairs={{0,8},{4,12},{8,0},{12,4},{16,24},{20,28},{24,16},{28,20},{1,9},{5... | collective-permute-start | bytes 294920 | tf_op jit(solution)/shard_map/ppermute | solution.py:665
  174.6 12.0 %collective-permute-start.39 = (bf16[4,96,768]{2,1,0:T(8,128)(2,1)S(1)}, bf16[4,96,768]{2,1,0:T(8,128)(2,1)S(1)}, u32[]{:S(2)}, u32[]{:S(2)}) collective-permute-start(bf16[4,96,768]{2,1,0:T(8,128)(2,1)S(1)} %constant_dynamic-update-slice_fusion.12.held), channel_id=1, source_target_pairs={{0,4},{4,0},{8,12},{12,8},{16,20},{20,16},{24,28},{28,24},{1,5},{5... | collective-permute-start | bytes 1769480 | tf_op jit(solution)/shard_map/ppermute | solution.py:661
  177.3 11.4 %collective-permute-start.42 = (bf16[4,32,768]{2,1,0:T(8,128)(2,1)S(1)}, bf16[4,32,768]{2,1,0:T(8,128)(2,1)S(1)}, u32[]{:S(2)}, u32[]{:S(2)}) collective-permute-start(bf16[4,32,768]{2,1,0:T(8,128)(2,1)S(1)} %constant_dynamic-update-slice_fusion.14.held), channel_id=1, source_target_pairs={{0,4},{4,0},{8,12},{12,8},{16,20},{20,16},{24,28},{28,24},{1,5},{5... | collective-permute-start | bytes 589832 | tf_op jit(solution)/shard_map/ppermute | solution.py:661
  (19 other events, 136.1 us)
where the time goes:
time: 190 us
  Pallas kernels  76.9 us (40%)
  waiting for transfers between devices  59.2 us (31%)
  starting transfers between devices  44.4 us (23%)
  local copies, waits for them, and re-layouts  5.89 us (3%)
  other arithmetic  1.91 us (1%)
    pallas_call x13, Pallas kernels, call(): pl.pallas_call(kernel, out_shape=[jax.ShapeDtypeStruct(shape, kind) for s...  76.9 us
    ppermute x8, waiting for transfers between devices, swap_near(): return lax.ppermute(sent, 'grp', Z_NEAR)  23.4 us
    ppermute x8, waiting for transfers between devices, swap_x(): return lax.ppermute(sent, 'grp', X_SWAP)  13.9 us
    ppermute x5, waiting for transfers between devices, reach_seq(): lax.ppermute(block, 'seq', Y_SWAP)  13.4 us
    ppermute x8, starting transfers between devices, swap_near(): return lax.ppermute(sent, 'grp', Z_NEAR)  11.9 us
    ppermute x8, starting transfers between devices, swap_far(): return lax.ppermute(sent, 'grp', Z_FAR)  11.8 us
    ppermute x5, starting transfers between devices, reach_seq(): lax.ppermute(block, 'seq', Y_SWAP)  8.23 us
    ppermute x8, starting transfers between devices, swap_x(): return lax.ppermute(sent, 'grp', X_SWAP)  8.03 us
  transfers between devices with their start and end apart: 43, of which 17 were waited for; matrix products, arithmetic and copies ran while one was open for 2% of the time, Pallas kernels for 39%

commit v1 on v0

--- a/solution.py
+++ b/solution.py
@@ -596,7 +596,6 @@
 HALF_GLOB = GLOBALS // 2
 HALF = HALF_TOK + HALF_GLOB
 SEND = CHUNK + 32
-CODED = D + 128
 WIDE = 640
 GRAPH_ROWS = 32
 X_PAIRS = ((0, 1), (2, 3), (4, 5), (6, 7))
@@ -706,6 +705,13 @@
     return pre * half, slope
 
 
+def ints_kernel(neigh_ref, rank_ref, member_ref, out_ref):
+    out_ref[:NEIGH] = neigh_ref[...]
+    out_ref[NEIGH:] = jnp.concatenate(
+        [rank_ref[...], member_ref[...], jnp.zeros((16 - NEIGH - 3, TOK), jnp.int32)], axis=0
+    )
+
+
 def counts_of(neigh, first, width):
     spots = (lax.broadcasted_iota(jnp.int32, (neigh.shape[0], width), 1) + first).astype(F32)
     total = jnp.zeros((neigh.shape[0], width), F32)
@@ -740,28 +746,6 @@
     return tn(rich, jnp.where(chosen, 1.0, 0.0).astype(BF))
 
 
-def code_kernel(
-    tok_any, neigh_any, rank_any, member_any, out_ref, tok_ref, neigh_ref, rank_ref, member_ref, sems
-):
-    pairs = (tok_any, tok_ref), (neigh_any, neigh_ref), (rank_any, rank_ref), (member_any, member_ref)
-    copies = [load(source, target, sems.at[i]) for i, (source, target) in enumerate(pairs)]
-    for copy in copies:
-        copy.wait()
-    out_ref[:, :D] = tok_ref[...]
-    ints = jnp.concatenate(
-        [neigh_ref[...], rank_ref[...], member_ref[...], jnp.zeros((TOK - 11, TOK), jnp.int32)], axis=0
-    )
-    ints = ints.astype(F32).T
-    high = jnp.floor(ints * (1.0 / 256.0))
-    low = ints - 256.0 * high
-    out_ref[:, D:] = jnp.concatenate([low[:, :16], high[:, :16], low[:, 32:]], axis=1).astype(BF)
-
-
-def decoded(coded):
-    coded = coded.astype(F32)
-    return coded + 256.0 * jnp.concatenate([coded[:, 16:], coded[:, :16]], axis=1)
-
-
 def share_out(chunk_of, bit, pairs, kept_ref, sent_ref):
     for i, pair in enumerate(pairs):
         first, second = (chunk_of(g) for g in pair)
@@ -781,8 +765,8 @@
 
 
 def attend_kernel(
-    tok_a, tok_b, tok_c, tok_d, glob_ref, gain_ref, shift_ref, rich_q_ref, rich_k_ref,
-    w_graph_any, w_query_any, w_key_any, w_value_any,
+    tok_a, tok_b, tok_c, tok_d, int_a, int_b, int_c, int_d, glob_ref, gain_ref, shift_ref, rich_q_ref,
+    rich_k_ref,    w_graph_any, w_query_any, w_key_any, w_value_any,
     both_ref, member_ref, glob_att_ref, meta_row_ref,
     agg_any, pre_any, super_any, normed_any, qkv_any, prob_any,
     agg_ref, pre_ref, super_ref, normed_ref, qkv_ref, prob_ref,
@@ -799,11 +783,12 @@
     padded[RADIUS + ROWS :] = jnp.zeros((RADIUS, D), BF)
     starts = [pl.multiple_of((me ^ k) * TOK, TOK) for k in range(SEQ_WAYS)]
     for start, tok in zip(starts, (tok_a, tok_b, tok_c, tok_d)):
-        padded[pl.ds(start + RADIUS, TOK)] = tok[:, :D]
-    for start, tok in zip(starts, (tok_a, tok_b, tok_c, tok_d)):
-        floats = decoded(tok[:, D:])
+        padded[pl.ds(start + RADIUS, TOK)] = tok[...]
+    for start, ints in zip(starts, (int_a, int_b, int_c, int_d)):
+        rows = ints[...].astype(F32)
+        meta_row_ref[:, pl.ds(start, TOK)] = rows
+        floats = meta_columns(rows)
         meta_col_ref[pl.ds(start, TOK)] = floats
-        meta_row_ref[:, pl.ds(start, TOK)] = floats.T[:16]
         counts = counts_of(floats, 0, WIN)
         mean = nn(counts, padded[pl.ds(start, WIN)]) * (1.0 / NEIGH)
         agg_ref[pl.ds(start, TOK)] = mean.astype(BF)
@@ -981,11 +966,12 @@
         span = pl.ds(pl.multiple_of(j * FF_OWN, FF_OWN), FF_OWN)
         return pltpu.make_async_copy(w_down_any.at[span], w_down_ref.at[j], sems.at[16 + j])
 
-    for j in range(SEQ_WAYS):
-        up_copy(j).start()
-        down_copy(j).start()
+    up_copy(0).start()
+    down_copy(0).start()
     for copy in first:
         copy.wait()
+    up_copy(1).start()
+    down_copy(1).start()
     y_rows = jnp.concatenate([super_ref[...], glob_ref[...].astype(F32)], axis=0)
     for k in range(SEQ_WAYS):
         wide = jnp.concatenate([att_refs[k], glob_att_refs[k]], axis=0)
@@ -1002,6 +988,11 @@
     back_sum[...] = jnp.zeros((CHUNK, D), F32)
 
     def units(j, carry):
+        @pl.when(j + 2 < SEQ_WAYS)
+        def _():
+            up_copy(j + 2).start()
+            down_copy(j + 2).start()
+
         up_copy(j).wait()
         hidden, slope = gelu_parts(nn(normed, w_up_ref[j]) + bias_ref[pl.ds(j, 1)])
         down_copy(j).wait()
@@ -1438,18 +1429,16 @@
     me = lax.axis_index("seq")
     grp = lax.axis_index("grp")
     x, z_low, z_high = grp % 2, (grp // 2) % 2, grp // 4
-    (coded,) = call(
-        code_kernel,
-        [tokens, neighbours.T, token_ranks, membership.reshape(1, TOK)],
-        [((TOK, CODED), BF)],
-        [((TOK, D), BF), ((NEIGH, TOK), jnp.int32), ((2, TOK), jnp.int32), ((1, TOK), jnp.int32),
-         pltpu.SemaphoreType.DMA((4,))],
-        apart=4, room=60,
-    )
-    beside, across = reach_seq(coded)
-    cot_tokens, across = tie(cot_tokens, across)
-    tok_blocks = [coded, beside, across, lax.ppermute(across, "seq", CORE_SWAP)]
-    cot_beside, cot_across = reach_seq(cot_tokens)
+    beside, across = reach_seq(tokens)
+    (ints,) = call(
+        ints_kernel, [neighbours.T, token_ranks, membership.reshape(1, TOK)], [((16, TOK), jnp.int32)],
+        room=60,
+    )
+    int_beside, int_across = reach_seq(ints)
+    int_blocks = [ints, int_beside, int_across, lax.ppermute(int_across, "seq", CORE_SWAP)]
+    cot_tokens, across, int_blocks[3] = tie(cot_tokens, across, int_blocks[3])
+    cot_across = lax.ppermute(cot_tokens, "seq", Y_SWAP)
+    tok_blocks = [tokens, beside, across, lax.ppermute(across, "seq", CORE_SWAP)]
     rich_query, rich_key = rich_query.T, rich_key.T
 
     weights_shape = (D, D), BF
@@ -1468,17 +1457,18 @@
         prob,
     ) = call(
         attend_kernel,
-        [*tok_blocks, global_tokens, gain_one, shift_one, rich_query, rich_key, w_graph, w_query,
+        [*tok_blocks, *int_blocks, global_tokens, gain_one, shift_one, rich_query, rich_key, w_graph, w_query,
          w_key, w_value],
         [((HALF, 2 * OWN), BF), ((OWN_HEADS, GLOBALS, 640), F32),
          ((OWN_HEADS, GLOBALS, HEAD_DIM), F32), ((16, ROWS), F32), kept_agg, *stored[1:]],
         [*stored, ((PAD, D), BF), weights_shape, ((3, D, 256), BF), *heads_scratch,
          ((TOK, WIN), F32), ((OWN_HEADS, ALL, HEAD_DIM), BF), ((ALL, OWN), BF),
          ((ROWS, 128), F32), pltpu.SemaphoreType.DMA((9,)), pltpu.SemaphoreType.DMA((SEQ_WAYS,))],
-        apart=4, outs_apart=6,
-    )
-    both, cot_beside, cot_across = tie(both, cot_beside, cot_across)
+        apart=4, outs_apart=6, room=56,
+    )
+    both, cot_across, cot_tokens = tie(both, cot_across, cot_tokens)
     att_blocks = gather_seq(both)
+    cot_beside = lax.ppermute(cot_tokens, "seq", CORE_SWAP)
     cot_blocks = [cot_tokens, cot_beside, cot_across, lax.ppermute(cot_across, "seq", CORE_SWAP)]
     out_tokens, back = call(
         own_feed_kernel,
@@ -1562,14 +1552,13 @@
     )
     hold("proj", proj_kept)
     proj_came = swap_x(proj_sent)
+    up_came = swap_near(halve("up", up_came, z_low))
     down_came = swap_far(halve("down", down_came, z_high))
-    up_came = swap_near(halve("up", up_came, z_low))
     across = hold("across", due(across))
     diagonal = lax.ppermute(across, "seq", CORE_SWAP)
+    up_came = swap_far(halve("up", up_came, z_high))
     down_came = swap_far(total("down", down_came))
-    up_came = swap_far(halve("up", up_came, z_high))
     proj_came = swap_near(halve("proj", proj_came, z_low))
-
     grad_global, graph_kept, graph_sent, d_own, d_pre = call(
         norm_kernel,
         [d_qkv, beside, held["across"], diagonal, global_tokens, d_proj, gain_one, due(vec_two), d_bias_up,
@@ -1599,12 +1588,12 @@
     proj_sum = total("proj", proj_came)
     proj_core = turn_core(proj_sum[0, :, : 3 * OWN].reshape(SEQ_WAYS, PIECE, 3 * OWN))
     down_came = swap_x(join("down", down_came))
-    graph_came = swap_near(halve("graph", graph_came, z_low))
     proj_core = due(proj_core)
     proj_mine = held["proj"][0, :, : 3 * OWN].reshape(SEQ_WAYS, PIECE, 3 * OWN)
     proj_far = lax.ppermute(turn_y(proj_mine, proj_core), "seq", Y_SWAP)
     hold("proj_core", proj_core)
     up_came = swap_near(join("up", up_came))
+    graph_came = swap_near(halve("graph", graph_came, z_low))
     proj_turned = turned(proj_mine, held["proj_core"], due(proj_far))
     proj_turned = jnp.concatenate([proj_turned, held["proj"][0, :, 3 * OWN :]], axis=1)[None]
     proj_came = swap_far(hold("proj", proj_turned))
@@ -1616,9 +1605,9 @@
     hold("g_down", g_down)
     graph_came = swap_near(join("graph", graph_came))
     proj_came = swap_x(join("proj", proj_came))
+    graph_came = swap_x(join("graph", graph_came))
     (g_up,) = call(up_out_kernel, [held["up"], due(up_came)], [((OWN, FF), F32)])
     hold("g_up", g_up)
-    graph_came = swap_x(join("graph", graph_came))
     g_query, g_key, g_value, g_out = call(
         project_out_kernel,
         [held["proj"], due(proj_came)],
@@ -1636,7 +1625,10 @@
          *[((HEAD_DIM // SEQ_WAYS, 4 * HEADS), F32)] * 2],
         [((GRP_WAYS, 16, HEAD_DIM), F32)],
     )
-    grad_tokens, g_down, g_up, g_query = (held[key] for key in ("tokens", "g_down", "g_up", "g_query"))
+    hold("g_graph", g_graph)
+    grad_tokens, g_down, g_up, g_query, g_graph = (
+        held[key] for key in ("tokens", "g_down", "g_up", "g_query", "g_graph")
+    )
     return (
         out_tokens, out_global, grad_tokens, grad_global,
         g_graph, g_gain_one, g_shift_one, g_query, g_key, g_value, g_rich_q, g_rich_k,

time: 190 us -> 184 us (0.968)
  waiting for transfers between devices: 59.2 us -> 53.1 us
  local copies, waits for them, and re-layouts: 5.89 us -> 3.58 us
  starting transfers between devices: 44.4 us -> 46.5 us
    ppermute x8, waiting for transfers between devices: 23.4 us -> 16.4 us  [swap_near(): return lax.ppermute(sent, 'grp', Z_NEAR)]
    ppermute x8, waiting for transfers between devices: 13.9 us -> 7.94 us  [swap_x(): return lax.ppermute(sent, 'grp', X_SWAP)]
    ppermute x1, waiting for transfers between devices: 0.49 us -> 3.55 us  [split_heads(): proj_far = lax.ppermute(turn_y(proj_mine, proj_core), 'seq', Y_SWAP)]
    ppermute x1 -> x4, starting transfers between devices: 0.01 us -> 2.41 us  [the longest x1 1.74 us: split_heads(): cot_across = lax.ppermute(cot_tokens, 'seq', Y_SWAP)]
    ppermute x8, starting transfers between devices: 11.8 us -> 13.8 us  [swap_far(): return lax.ppermute(sent, 'grp', Z_FAR)]
    unnamed x56 -> x66, local copies, waits for them, and re-layouts: 3.94 us -> 3 us
  transfers between devices with their start and end apart: 43 -> 46, of which waited for: 17 -> 20; matrix products, arithmetic and copies ran while one was open for 2% -> 1% of each run, Pallas kernels for 39% -> 42%
where the time goes in v1:
time: 184 us; the launch traced here: 183 us
  Pallas kernels  77.9 us (42%)
  waiting for transfers between devices  53.1 us (29%)
  starting transfers between devices  46.5 us (25%)
  local copies, waits for them, and re-layouts  3.58 us (2%)
    pallas_call x13, Pallas kernels, call(): pl.pallas_call(kernel, out_shape=[jax.ShapeDtypeStruct(shape, kind) for s...  77.9 us
    ppermute x8, waiting for transfers between devices, swap_near(): return lax.ppermute(sent, 'grp', Z_NEAR)  16.4 us
    ppermute x5, waiting for transfers between devices, reach_seq(): lax.ppermute(block, 'seq', Y_SWAP)  14.7 us
    ppermute x8, starting transfers between devices, swap_far(): return lax.ppermute(sent, 'grp', Z_FAR)  13.8 us
    ppermute x8, starting transfers between devices, swap_near(): return lax.ppermute(sent, 'grp', Z_NEAR)  11.7 us
    ppermute x8, waiting for transfers between devices, swap_far(): return lax.ppermute(sent, 'grp', Z_FAR)  8.86 us
    ppermute x8, starting transfers between devices, swap_x(): return lax.ppermute(sent, 'grp', X_SWAP)  8.16 us
    ppermute x8, waiting for transfers between devices, swap_x(): return lax.ppermute(sent, 'grp', X_SWAP)  7.94 us
  transfers between devices with their start and end apart: 46, of which 20 were waited for; matrix products, arithmetic and copies ran while one was open for 1% of the time, Pallas kernels for 42%

profile of v1, /device:TPU:0, one launch (start us, length us, event | category | flops | bytes accessed | tf_op | source)
XLA Modules:
  0.0 183.5 jit_solution(18088641685076965567)
XLA Ops:
  0.7 3.0 %collective-permute-start.1 = (bf16[128,768]{1,0:T(8,128)(2,1)}, bf16[128,768]{1,0:T(8,128)(2,1)S(1)}, u32[]{:S(2)}, u32[]{:S(2)}) collective-permute-start(bf16[128,768]{1,0:T(8,128)(2,1)} %tok_a.1), channel_id=1, source_target_pairs={{0,2},{2,0},{1,3},{3,1},{4,6},{6,4},{5,7},{7,5},{8,10},{10,8},{9,1... | collective-permute-start | bytes 589832 | tf_op jit(solution)/shard_map/ppermute | solution.py:633
  3.7 1.4 shard_map.357.int_a
  5.1 3.9 %collective-permute-done.2.int_c = s32[16,128]{1,0:T(8,128)S(1)} collective-permute-done((s32[16,128]{1,0:T(8,128)}, s32[16,128]{1,0:T(8,128)S(1)}, u32[]{:S(2)}, u32[]{:S(2)}) %collective-permute-start.2) | collective-permute-done | bytes 8224 | tf_op jit(solution)/shard_map/ppermute | solution.py:633
  10.7 1.7 collective-permute-start.6
  13.3 18.9 %shard_map.358 = (bf16[288,384]{1,0:T(8,128)(2,1)}, f32[3,64,640]{2,1,0:T(8,128)}, f32[3,64,64]{2,1,0:T(8,128)}, f32[16,512]{1,0:T(8,128)}, bf16[512,256]{1,0:T(...) custom-call(bf16[128,768]{1,0:T(8,128)(2,1)} %tok_a.1, ...), custom_call_target="tpu_custom_call" | custom-call | flops 60000002048 | tf_op jit(solution)/shard_map/pallas_call | solution.py:1413
  32.2 1.2 collective-permute-start.8
  33.4 6.2 %collective-permute-done.8.att_c = bf16[288,384]{1,0:T(8,128)(2,1)S(1)} collective-permute-done((bf16[288,384]{1,0:T(8,128)(2,1)}, bf16[288,384]{1,0:T(8,128)(2,1)S(1)}, u32[]{:S(2)}, u32[]{:S(2)}) %collective-permute-start.8) | collective-permute-done | bytes 221216 | tf_op jit(solution)/shard_map/ppermute | solution.py:633
  42.1 9.8 %shard_map.359 = (bf16[128,768]{1,0:T(8,128)(2,1)}, bf16[176,768]{1,0:T(8,128)(2,1)S(1)}) custom-call(bf16[288,384]{1,0:T(8,128)(2,1)S(1)} %copy-done.2, bf16[288,384]{1,0:T(8,128)(2,1)S(1)} %collective-permute-done.7.att_b, bf16[288,384]{1,0:T(8,128)(2,1)S(1)} %collective-permute-done.8.att_c, bf16[288,384]{1,0:T(8,128)(2,1)S(1)} %collective-permute-done.9.att_d, ...), custom_call_target="tpu_custom_call" | custom-call | flops 60000002048 | tf_op jit(solution)/shard_map/pallas_call | solution.py:1413
  51.9 1.6 collective-permute-start.13
  53.5 6.7 %shard_map.360 = (bf16[4,96,768]{2,1,0:T(8,128)(2,1)S(1)}, bf16[4,96,768]{2,1,0:T(8,128)(2,1)S(1)}, bf16[576,768]{1,0:T(8,128)(2,1)S(1)}, f32[576,768]{1,0:T(8,128)}, bf16[576,768]{1,0:T(8,128)(2,1)}) custom-call(bf16[288,384]{1,0:T(8,128)(2,1)S(1)} %copy-done.2, bf16[288,384]{1,0:T(8,128)(2,1)S(1)} %collective-permute-done.7.att_b, ...), custom_call_target="tpu_custom_call" | custom-call | flops 60000002048 | tf_op jit(solution)/shard_map/pallas_call | solution.py:1413
  60.2 1.5 collective-permute-start.15
  62.0 1.2 copy-done.15
  63.2 4.7 %shard_map.361 = (bf16[4,96,768]{2,1,0:T(8,128)(2,1)S(1)}, bf16[4,96,768]{2,1,0:T(8,128)(2,1)S(1)}, f32[1,768]{1,0:T(1,128)S(1)}) custom-call(bf16[576,768]{1,0:T(8,128)(2,1)S(1)} %get-tuple-element.156.normed_ref, f32[576,768]{1,0:T(8,128)} %get-tuple-element.157.slope_ref, bf16[576,768]{1,0:T(8,128)(2,1)S(1)} %copy-done.15, bf16[3072,768]{1,0:T(8,128)(2,1)} %w_down_any.3), custom_call_target="tpu_custom_call" | custom-call | flops 60000002048 | tf_op jit(solution)/shard_map/pallas_call | solution.py:1413
  68.5 15.3 %shard_map.362 = (bf16[576,768]{1,0:T(8,128)(2,1)S(1)}, bf16[576,640]{1,0:T(8,128)(2,1)S(1)}, f32[8,768]{1,0:T(8,128)S(1)}, bf16[64,768]{1,0:T(8,128)(2,1)}) custom-call(bf16[176,768]{1,0:T(8,128)(2,1)S(1)} %get-tuple-element.147.back_a, bf16[176,768]{1,0:T(8,128)(2,1)S(1)} %collective-permute-done.10.back_b, ...), custom_call_target="tpu_custom_call" | custom-call | flops 60000002048 | tf_op jit(solution)/shard_map/pallas_call | solution.py:1413
  83.8 1.0 collective-permute-start.20
  85.1 1.6 collective-permute-start.16
  86.7 1.5 shard_map.363
  88.2 1.1 collective-permute-start.24
  89.5 1.0 collective-permute-start.19
  90.5 4.5 %collective-permute-done.16 = bf16[2,96,768]{2,1,0:T(8,128)(2,1)S(1)} collective-permute-done((bf16[2,96,768]{2,1,0:T(8,128)(2,1)S(1)}, bf16[2,96,768]{2,1,0:T(8,128)(2,1)S(1)}, u32[]{:S(2)}, u32[]{:S(2)}) %collective-permute-start.16) | collective-permute-done | bytes 294944 | tf_op jit(solution)/shard_map/ppermute | solution.py:664
  95.0 2.7 %collective-permute-start.18 = (bf16[1,96,768]{2,1,0:T(8,128)(2,1)S(1)}, bf16[1,96,768]{2,1,0:T(8,128)(2,1)S(1)}, u32[]{:S(2)}, u32[]{:S(2)}) collective-permute-start(bf16[1,96,768]{2,1,0:T(8,128)(2,1)S(1)} %get-tuple-element.267), channel_id=1, source_target_pairs={{0,16},{4,20},{8,24},{12,28},{16,0},{20,4},{24,8},{28,12},{1,17},{... | collective-permute-start | bytes 442376 | tf_op jit(solution)/shard_map/ppermute | solution.py:668
  97.7 4.6 %collective-permute-done.20.dqkv_c = bf16[576,640]{1,0:T(8,128)(2,1)S(1)} collective-permute-done((bf16[576,640]{1,0:T(8,128)(2,1)S(1)}, bf16[576,640]{1,0:T(8,128)(2,1)S(1)}, u32[]{:S(2)}, u32[]{:S(2)}) %collective-permute-start.20) | collective-permute-done | bytes 737312 | tf_op jit(solution)/shard_map/ppermute | solution.py:633
  102.3 1.7 collective-permute-done.19
  104.2 2.5 %collective-permute-start.26 = (bf16[1,96,768]{2,1,0:T(8,128)(2,1)S(1)}, bf16[1,96,768]{2,1,0:T(8,128)(2,1)S(1)}, u32[]{:S(2)}, u32[]{:S(2)}) collective-permute-start(bf16[1,96,768]{2,1,0:T(8,128)(2,1)S(1)} %add_convert_fusion.9), channel_id=1, source_target_pairs={{0,16},{4,20},{8,24},{12,28},{16,0},{20,4},{24,8},{28,12},{1,17},{... | collective-permute-start | bytes 442376 | tf_op jit(solution)/shard_map/ppermute | solution.py:668
  107.5 2.5 %collective-permute-start.27 = (bf16[2,96,768]{2,1,0:T(8,128)(2,1)S(1)}, bf16[2,96,768]{2,1,0:T(8,128)(2,1)S(1)}, u32[]{:S(2)}, u32[]{:S(2)}) collective-permute-start(bf16[2,96,768]{2,1,0:T(8,128)(2,1)S(1)} %get-tuple-element.257), channel_id=1, source_target_pairs={{0,8},{4,12},{8,0},{12,4},{16,24},{20,28},{24,16},{28,20},{1,9},{5... | collective-permute-start | bytes 884744 | tf_op jit(solution)/shard_map/ppermute | solution.py:664
  110.0 10.0 %shard_map.364 = (f32[64,768]{1,0:T(8,128)}, bf16[4,32,768]{2,1,0:T(8,128)(2,1)S(1)}, bf16[4,32,768]{2,1,0:T(8,128)(2,1)S(1)}, f32[128,768]{1,0:T(8,128)S(1)}, bf16[512,768]{1,0:T(8,128)(2,1)}) custom-call(bf16[576,640]{1,0:T(8,128)(2,1)S(1)} %get-tuple-element.168.d_qkv_ref.dqkv_a, bf16[576,640]{1,0:T(8,128)(2,1)S(1)} %collective-permute-done.22.dqkv_b, ...), custom_call_target="tpu_custom_call" | custom-call | flops 60000002048 | tf_op jit(solution)/shard_map/pallas_call | solution.py:1413
  120.9 2.4 %collective-permute-start.30 = (bf16[1,96,768]{2,1,0:T(8,128)(2,1)S(1)}, bf16[1,96,768]{2,1,0:T(8,128)(2,1)S(1)}, u32[]{:S(2)}, u32[]{:S(2)}) collective-permute-start(bf16[1,96,768]{2,1,0:T(8,128)(2,1)S(1)} %get-tuple-element.263), channel_id=1, source_target_pairs={{0,16},{4,20},{8,24},{12,28},{16,0},{20,4},{24,8},{28,12},{1,17},{... | collective-permute-start | bytes 442376 | tf_op jit(solution)/shard_map/ppermute | solution.py:668
  123.3 2.5 %collective-permute-start.33 = (bf16[2,96,768]{2,1,0:T(8,128)(2,1)S(1)}, bf16[2,96,768]{2,1,0:T(8,128)(2,1)S(1)}, u32[]{:S(2)}, u32[]{:S(2)}) collective-permute-start(bf16[2,96,768]{2,1,0:T(8,128)(2,1)S(1)} %constant_dynamic-update-slice_fusion), channel_id=1, source_target_pairs={{0,8},{4,12},{8,0},{12,4},{16,24},{20,28},{24,16},{28,20},{1,9},{5... | collective-permute-start | bytes 884744 | tf_op jit(solution)/shard_map/ppermute | solution.py:664
  125.8 1.0 collective-permute-start.29
  126.9 1.6 collective-permute-start.28
  128.5 3.5 %shard_map.365 = f32[128,768]{1,0:T(8,128)} custom-call(f32[128,768]{1,0:T(8,128)S(1)} %get-tuple-element.201.d_own_ref, bf16[512,768]{1,0:T(8,128)(2,1)S(1)} %copy-done.17, f32[16,512]{1,0:T(8,128)S(1)} %copy-done.21, bf16[768,768]{1,0:T(8,128)(2,1)S(1)} %copy-done.1), custom_call_target="tpu_custom_call" | custom-call | flops 60000002048 | tf_op jit(solution)/shard_map/pallas_call | solution.py:1413
  132.3 2.3 %collective-permute-done.33 = bf16[2,96,768]{2,1,0:T(8,128)(2,1)S(1)} collective-permute-done((bf16[2,96,768]{2,1,0:T(8,128)(2,1)S(1)}, bf16[2,96,768]{2,1,0:T(8,128)(2,1)S(1)}, u32[]{:S(2)}, u32[]{:S(2)}) %collective-permute-start.33) | collective-permute-done | bytes 294944 | tf_op jit(solution)/shard_map/ppermute | solution.py:664
  134.6 2.4 %collective-permute-start.39 = (bf16[4,96,768]{2,1,0:T(8,128)(2,1)S(1)}, bf16[4,96,768]{2,1,0:T(8,128)(2,1)S(1)}, u32[]{:S(2)}, u32[]{:S(2)}) collective-permute-start(bf16[4,96,768]{2,1,0:T(8,128)(2,1)S(1)} %constant_dynamic-update-slice_fusion.2.held), channel_id=1, source_target_pairs={{0,4},{4,0},{8,12},{12,8},{16,20},{20,16},{24,28},{28,24},{1,5},{5... | collective-permute-start | bytes 1769480 | tf_op jit(solution)/shard_map/ppermute | solution.py:660
  137.1 4.2 %collective-permute-done.31 = bf16[1,96,768]{2,1,0:T(8,128)(2,1)S(1)} collective-permute-done((bf16[1,96,768]{2,1,0:T(8,128)(2,1)S(1)}, bf16[1,96,768]{2,1,0:T(8,128)(2,1)S(1)}, u32[]{:S(2)}, u32[]{:S(2)}) %collective-permute-start.31) | collective-permute-done | bytes 147488 | tf_op jit(solution)/shard_map/ppermute | solution.py:668
  142.2 3.6 %collective-permute-done.35 = bf16[2,24,576]{2,1,0:T(8,128)(2,1)S(1)} collective-permute-done((bf16[2,24,576]{2,1,0:T(8,128)(2,1)S(1)}, bf16[2,24,576]{2,1,0:T(8,128)(2,1)S(1)}, u32[]{:S(2)}, u32[]{:S(2)}) %collective-permute-start.35) | collective-permute-done | bytes 55328 | tf_op jit(solution)/shard_map/ppermute | solution.py:1593
  145.9 1.0 collective-permute-start.37
  146.9 1.2 collective-permute-start.40
  148.1 4.9 %collective-permute-done.34 = bf16[2,96,768]{2,1,0:T(8,128)(2,1)S(1)} collective-permute-done((bf16[2,96,768]{2,1,0:T(8,128)(2,1)S(1)}, bf16[2,96,768]{2,1,0:T(8,128)(2,1)S(1)}, u32[]{:S(2)}, u32[]{:S(2)}) %collective-permute-start.34) | collective-permute-done | bytes 294944 | tf_op jit(solution)/shard_map/ppermute | solution.py:664
  154.8 1.5 collective-permute-start.41
  156.4 3.6 %collective-permute-done.41 = bf16[1,32,768]{2,1,0:T(8,128)(2,1)S(1)} collective-permute-done((bf16[1,32,768]{2,1,0:T(8,128)(2,1)S(1)}, bf16[1,32,768]{2,1,0:T(8,128)(2,1)S(1)}, u32[]{:S(2)}, u32[]{:S(2)}) %collective-permute-start.41) | collective-permute-done | bytes 49184 | tf_op jit(solution)/shard_map/ppermute | solution.py:668
  160.0 3.0 %collective-permute-start.42 = (bf16[1,32,768]{2,1,0:T(8,128)(2,1)S(1)}, bf16[1,32,768]{2,1,0:T(8,128)(2,1)S(1)}, u32[]{:S(2)}, u32[]{:S(2)}) collective-permute-start(bf16[1,32,768]{2,1,0:T(8,128)(2,1)S(1)} %add_convert_fusion.11), channel_id=1, source_target_pairs={{0,16},{4,20},{8,24},{12,28},{16,0},{20,4},{24,8},{28,12},{1,17},{... | collective-permute-start | bytes 147464 | tf_op jit(solution)/shard_map/ppermute | solution.py:668
  163.1 1.6 shard_map.366
  165.2 2.6 %collective-permute-start.43 = (bf16[2,32,768]{2,1,0:T(8,128)(2,1)S(1)}, bf16[2,32,768]{2,1,0:T(8,128)(2,1)S(1)}, u32[]{:S(2)}, u32[]{:S(2)}) collective-permute-start(bf16[2,32,768]{2,1,0:T(8,128)(2,1)S(1)} %constant_dynamic-update-slice_fusion.10), channel_id=1, source_target_pairs={{0,8},{4,12},{8,0},{12,4},{16,24},{20,28},{24,16},{28,20},{1,9},{5... | collective-permute-start | bytes 294920 | tf_op jit(solution)/shard_map/ppermute | solution.py:664
  168.3 2.2 %collective-permute-done.43 = bf16[2,32,768]{2,1,0:T(8,128)(2,1)S(1)} collective-permute-done((bf16[2,32,768]{2,1,0:T(8,128)(2,1)S(1)}, bf16[2,32,768]{2,1,0:T(8,128)(2,1)S(1)}, u32[]{:S(2)}, u32[]{:S(2)}) %collective-permute-start.43) | collective-permute-done | bytes 98336 | tf_op jit(solution)/shard_map/ppermute | solution.py:664
  170.9 1.6 shard_map.367
  172.5 7.8 %collective-permute-done.45.came = bf16[4,96,768]{2,1,0:T(8,128)(2,1)S(1)} collective-permute-done((bf16[4,96,768]{2,1,0:T(8,128)(2,1)S(1)}, bf16[4,96,768]{2,1,0:T(8,128)(2,1)S(1)}, u32[]{:S(2)}, u32[]{:S(2)}) %collective-permute-start.45) | collective-permute-done | bytes 589856 | tf_op jit(solution)/shard_map/ppermute | solution.py:660
  180.3 2.0 %shard_map.368 = (f32[192,768]{1,0:T(8,128)}, f32[192,768]{1,0:T(8,128)}, f32[192,768]{1,0:T(8,128)}, f32[192,768]{1,0:T(8,128)}) custom-call(bf16[4,96,768]{2,1,0:T(8,128)(2,1)S(1)} %constant_dynamic-update-slice_fusion.12.held, bf16[4,96,768]{2,1,0:T(8,128)(2,1)S(1)} %collective-permute-done.45.came), custom_call_target="tpu_custom_call" | custom-call | flops 60000002048 | tf_op jit(solution)/shard_map/pallas_call | solution.py:1413
  182.4 1.1 shard_map.369
  (169 shorter events, 12.7 us)
Async XLA Ops:
  0.7 9.5 %collective-permute-start.1 = (bf16[128,768]{1,0:T(8,128)(2,1)}, bf16[128,768]{1,0:T(8,128)(2,1)S(1)}, u32[]{:S(2)}, u32[]{:S(2)}) collective-permute-start(bf16[128,768]{1,0:T(8,128)(2,1)} %tok_a.1), channel_id=1, source_target_pairs={{0,2},{2,0},{1,3},{3,1},{4,6},{6,4},{5,7},{7,5},{8,10},{10,8},{9,1... | collective-permute-start | bytes 589832 | tf_op jit(solution)/shard_map/ppermute | solution.py:633
  5.0 3.9 %collective-permute-start.2 = (s32[16,128]{1,0:T(8,128)}, s32[16,128]{1,0:T(8,128)S(1)}, u32[]{:S(2)}, u32[]{:S(2)}) collective-permute-start(s32[16,128]{1,0:T(8,128)} %shard_map.357.int_a), channel_id=1, source_target_pairs={{0,2},{2,0},{1,3},{3,1},{4,6},{6,4},{5,7},{7,5},{8,10},{10,8},{9,1... | collective-permute-start | bytes 24584 | tf_op jit(solution)/shard_map/ppermute | solution.py:633
  9.0 1.2 collective-permute-start.3
  9.0 3.5 %collective-permute-start = (bf16[128,768]{1,0:T(8,128)(2,1)S(1)}, bf16[128,768]{1,0:T(8,128)(2,1)S(1)}, u32[]{:S(2)}, u32[]{:S(2)}) collective-permute-start(bf16[128,768]{1,0:T(8,128)(2,1)S(1)} %copy-done.22), channel_id=1, source_target_pairs={{0,1},{1,0},{2,3},{3,2},{4,5},{5,4},{6,7},{7,6},{8,9},{9,8},{10,11... | collective-permute-start | bytes 589832 | tf_op jit(solution)/shard_map/ppermute | solution.py:633
  10.2 2.3 %collective-permute-start.4 = (bf16[128,768]{1,0:T(8,128)(2,1)S(1)}, bf16[128,768]{1,0:T(8,128)(2,1)S(1)}, u32[]{:S(2)}, u32[]{:S(2)}) collective-permute-start(bf16[128,768]{1,0:T(8,128)(2,1)S(1)} %collective-permute-done.1.tok_c), channel_id=1, source_target_pairs={{0,1},{1,0},{2,3},{3,2},{4,5},{5,4},{6,7},{7,6},{8,9},{9,8},{10,11... | collective-permute-start | bytes 589832 | tf_op jit(solution)/shard_map/ppermute | solution.py:1441
  10.3 2.1 %collective-permute-start.5 = (s32[16,128]{1,0:T(8,128)}, s32[16,128]{1,0:T(8,128)S(1)}, u32[]{:S(2)}, u32[]{:S(2)}) collective-permute-start(s32[16,128]{1,0:T(8,128)} %shard_map.357.int_a), channel_id=1, source_target_pairs={{0,1},{1,0},{2,3},{3,2},{4,5},{5,4},{6,7},{7,6},{8,9},{9,8},{10,11... | collective-permute-start | bytes 24584 | tf_op jit(solution)/shard_map/ppermute | solution.py:633
  10.7 21.5 %collective-permute-start.6 = (bf16[128,768]{1,0:T(8,128)(2,1)S(1)}, bf16[128,768]{1,0:T(8,128)(2,1)S(1)}, u32[]{:S(2)}, u32[]{:S(2)}) collective-permute-start(bf16[128,768]{1,0:T(8,128)(2,1)S(1)} %copy-done.4), channel_id=1, source_target_pairs={{0,2},{2,0},{1,3},{3,1},{4,6},{6,4},{5,7},{7,5},{8,10},{10,8},{9,1... | collective-permute-start | bytes 589832 | tf_op jit(solution)/shard_map/ppermute | solution.py:1440
  13.2 27.9 %copy-start.10 = (f32[768]{0:T(1024)S(1)}, f32[768]{0:T(1024)}, u32[]{:S(2)}) copy-start(f32[768]{0:T(1024)} %bias_down_ref.1) | copy-start | bytes 9220
  13.3 27.9 %copy-start.11 = (f32[768]{0:T(1024)S(1)}, f32[768]{0:T(1024)}, u32[]{:S(2)}) copy-start(f32[768]{0:T(1024)} %gain_ref.5) | copy-start | bytes 9220
  32.2 7.4 %collective-permute-start.8 = (bf16[288,384]{1,0:T(8,128)(2,1)}, bf16[288,384]{1,0:T(8,128)(2,1)S(1)}, u32[]{:S(2)}, u32[]{:S(2)}) collective-permute-start(bf16[288,384]{1,0:T(8,128)(2,1)} %get-tuple-element.142.att_a.attn_ref), channel_id=1, source_target_pairs={{0,2},{2,0},{1,3},{3,1},{4,6},{6,4},{5,7},{7,5},{8,10},{10,8},{9,1... | collective-permute-start | bytes 663560 | tf_op jit(solution)/shard_map/ppermute | solution.py:633
  33.4 6.7 %collective-permute-start.7 = (bf16[288,384]{1,0:T(8,128)(2,1)}, bf16[288,384]{1,0:T(8,128)(2,1)S(1)}, u32[]{:S(2)}, u32[]{:S(2)}) collective-permute-start(bf16[288,384]{1,0:T(8,128)(2,1)} %get-tuple-element.142.att_a.attn_ref), channel_id=1, source_target_pairs={{0,1},{1,0},{2,3},{3,2},{4,5},{5,4},{6,7},{7,6},{8,9},{9,8},{10,11... | collective-permute-start | bytes 663560 | tf_op jit(solution)/shard_map/ppermute | solution.py:633
  39.6 1.5 collective-permute-start.9
  39.6 13.9 %collective-permute-start.11 = (bf16[128,768]{1,0:T(8,128)(2,1)S(1)}, bf16[128,768]{1,0:T(8,128)(2,1)S(1)}, u32[]{:S(2)}, u32[]{:S(2)}) collective-permute-start(bf16[128,768]{1,0:T(8,128)(2,1)S(1)} %copy-done.4), channel_id=1, source_target_pairs={{0,1},{1,0},{2,3},{3,2},{4,5},{5,4},{6,7},{7,6},{8,9},{9,8},{10,11... | collective-permute-start | bytes 589832 | tf_op jit(solution)/shard_map/ppermute | solution.py:1471
  40.1 13.4 %collective-permute-start.12 = (bf16[128,768]{1,0:T(8,128)(2,1)S(1)}, bf16[128,768]{1,0:T(8,128)(2,1)S(1)}, u32[]{:S(2)}, u32[]{:S(2)}) collective-permute-start(bf16[128,768]{1,0:T(8,128)(2,1)S(1)} %collective-permute-done.6.cot_c), channel_id=1, source_target_pairs={{0,1},{1,0},{2,3},{3,2},{4,5},{5,4},{6,7},{7,6},{8,9},{9,8},{10,11... | collective-permute-start | bytes 589832 | tf_op jit(solution)/shard_map/ppermute | solution.py:1472
  51.9 9.9 %collective-permute-start.13 = (bf16[176,768]{1,0:T(8,128)(2,1)S(1)}, bf16[176,768]{1,0:T(8,128)(2,1)S(1)}, u32[]{:S(2)}, u32[]{:S(2)}) collective-permute-start(bf16[176,768]{1,0:T(8,128)(2,1)S(1)} %get-tuple-element.147.back_a), channel_id=1, source_target_pairs={{0,2},{2,0},{1,3},{3,1},{4,6},{6,4},{5,7},{7,5},{8,10},{10,8},{9,1... | collective-permute-start | bytes 811016 | tf_op jit(solution)/shard_map/ppermute | solution.py:633
  53.5 14.9 %collective-permute-start.10 = (bf16[176,768]{1,0:T(8,128)(2,1)S(1)}, bf16[176,768]{1,0:T(8,128)(2,1)S(1)}, u32[]{:S(2)}, u32[]{:S(2)}) collective-permute-start(bf16[176,768]{1,0:T(8,128)(2,1)S(1)} %get-tuple-element.147.back_a), channel_id=1, source_target_pairs={{0,1},{1,0},{2,3},{3,2},{4,5},{5,4},{6,7},{7,6},{8,9},{9,8},{10,11... | collective-permute-start | bytes 811016 | tf_op jit(solution)/shard_map/ppermute | solution.py:633
  60.2 24.6 %collective-permute-start.15 = (bf16[4,96,768]{2,1,0:T(8,128)(2,1)S(1)}, bf16[4,96,768]{2,1,0:T(8,128)(2,1)S(1)}, u32[]{:S(2)}, u32[]{:S(2)}) collective-permute-start(bf16[4,96,768]{2,1,0:T(8,128)(2,1)S(1)} %get-tuple-element.167), channel_id=1, source_target_pairs={{0,4},{4,0},{8,12},{12,8},{16,20},{20,16},{24,28},{28,24},{1,5},{5... | collective-permute-start | bytes 1769480 | tf_op jit(solution)/shard_map/ppermute | solution.py:660
  61.8 6.7 %collective-permute-start.14 = (bf16[176,768]{1,0:T(8,128)(2,1)S(1)}, bf16[176,768]{1,0:T(8,128)(2,1)S(1)}, u32[]{:S(2)}, u32[]{:S(2)}) collective-permute-start(bf16[176,768]{1,0:T(8,128)(2,1)S(1)} %collective-permute-done.13.back_c), channel_id=1, source_target_pairs={{0,1},{1,0},{2,3},{3,2},{4,5},{5,4},{6,7},{7,6},{8,9},{9,8},{10,11... | collective-permute-start | bytes 811016 | tf_op jit(solution)/shard_map/ppermute | solution.py:1497
  67.8 21.5 %collective-permute-start.17 = (bf16[4,96,768]{2,1,0:T(8,128)(2,1)S(1)}, bf16[4,96,768]{2,1,0:T(8,128)(2,1)S(1)}, u32[]{:S(2)}, u32[]{:S(2)}) collective-permute-start(bf16[4,96,768]{2,1,0:T(8,128)(2,1)S(1)} %get-tuple-element.172), channel_id=1, source_target_pairs={{0,4},{4,0},{8,12},{12,8},{16,20},{20,16},{24,28},{28,24},{1,5},{5... | collective-permute-start | bytes 1769480 | tf_op jit(solution)/shard_map/ppermute | solution.py:660
  83.8 18.5 %collective-permute-start.20 = (bf16[576,640]{1,0:T(8,128)(2,1)S(1)}, bf16[576,640]{1,0:T(8,128)(2,1)S(1)}, u32[]{:S(2)}, u32[]{:S(2)}) collective-permute-start(bf16[576,640]{1,0:T(8,128)(2,1)S(1)} %get-tuple-element.168.d_qkv_ref.dqkv_a), channel_id=1, source_target_pairs={{0,2},{2,0},{1,3},{3,1},{4,6},{6,4},{5,7},{7,5},{8,10},{10,8},{9,1... | collective-permute-start | bytes 2211848 | tf_op jit(solution)/shard_map/ppermute | solution.py:633
  84.9 25.1 %collective-permute-start.22 = (bf16[576,640]{1,0:T(8,128)(2,1)S(1)}, bf16[576,640]{1,0:T(8,128)(2,1)S(1)}, u32[]{:S(2)}, u32[]{:S(2)}) collective-permute-start(bf16[576,640]{1,0:T(8,128)(2,1)S(1)} %get-tuple-element.168.d_qkv_ref.dqkv_a), channel_id=1, source_target_pairs={{0,1},{1,0},{2,3},{3,2},{4,5},{5,4},{6,7},{7,6},{8,9},{9,8},{10,11... | collective-permute-start | bytes 2211848 | tf_op jit(solution)/shard_map/ppermute | solution.py:633
  85.1 9.9 %collective-permute-start.16 = (bf16[2,96,768]{2,1,0:T(8,128)(2,1)S(1)}, bf16[2,96,768]{2,1,0:T(8,128)(2,1)S(1)}, u32[]{:S(2)}, u32[]{:S(2)}) collective-permute-start(bf16[2,96,768]{2,1,0:T(8,128)(2,1)S(1)} %get-tuple-element.261), channel_id=1, source_target_pairs={{0,8},{4,12},{8,0},{12,4},{16,24},{20,28},{24,16},{28,20},{1,9},{5... | collective-permute-start | bytes 884744 | tf_op jit(solution)/shard_map/ppermute | solution.py:664
  88.2 18.5 %collective-permute-start.24 = (bf16[4,96,768]{2,1,0:T(8,128)(2,1)S(1)}, bf16[4,96,768]{2,1,0:T(8,128)(2,1)S(1)}, u32[]{:S(2)}, u32[]{:S(2)}) collective-permute-start(bf16[4,96,768]{2,1,0:T(8,128)(2,1)S(1)} %get-tuple-element.185), channel_id=1, source_target_pairs={{0,4},{4,0},{8,12},{12,8},{16,20},{20,16},{24,28},{28,24},{1,5},{5... | collective-permute-start | bytes 1769480 | tf_op jit(solution)/shard_map/ppermute | solution.py:660
  89.5 14.5 %collective-permute-start.19 = (bf16[2,96,768]{2,1,0:T(8,128)(2,1)S(1)}, bf16[2,96,768]{2,1,0:T(8,128)(2,1)S(1)}, u32[]{:S(2)}, u32[]{:S(2)}) collective-permute-start(bf16[2,96,768]{2,1,0:T(8,128)(2,1)S(1)} %get-tuple-element.260), channel_id=1, source_target_pairs={{0,8},{4,12},{8,0},{12,4},{16,24},{20,28},{24,16},{28,20},{1,9},{5... | collective-permute-start | bytes 884744 | tf_op jit(solution)/shard_map/ppermute | solution.py:664
  95.0 9.1 %collective-permute-start.18 = (bf16[1,96,768]{2,1,0:T(8,128)(2,1)S(1)}, bf16[1,96,768]{2,1,0:T(8,128)(2,1)S(1)}, u32[]{:S(2)}, u32[]{:S(2)}) collective-permute-start(bf16[1,96,768]{2,1,0:T(8,128)(2,1)S(1)} %get-tuple-element.267), channel_id=1, source_target_pairs={{0,16},{4,20},{8,24},{12,28},{16,0},{20,4},{24,8},{28,12},{1,17},{... | collective-permute-start | bytes 442376 | tf_op jit(solution)/shard_map/ppermute | solution.py:668
  102.3 7.7 %collective-permute-start.23 = (bf16[576,640]{1,0:T(8,128)(2,1)S(1)}, bf16[576,640]{1,0:T(8,128)(2,1)S(1)}, u32[]{:S(2)}, u32[]{:S(2)}) collective-permute-start(bf16[576,640]{1,0:T(8,128)(2,1)S(1)} %collective-permute-done.20.dqkv_c), channel_id=1, source_target_pairs={{0,1},{1,0},{2,3},{3,2},{4,5},{5,4},{6,7},{7,6},{8,9},{9,8},{10,11... | collective-permute-start | bytes 2211848 | tf_op jit(solution)/shard_map/ppermute | solution.py:1558
  104.2 16.5 %collective-permute-start.26 = (bf16[1,96,768]{2,1,0:T(8,128)(2,1)S(1)}, bf16[1,96,768]{2,1,0:T(8,128)(2,1)S(1)}, u32[]{:S(2)}, u32[]{:S(2)}) collective-permute-start(bf16[1,96,768]{2,1,0:T(8,128)(2,1)S(1)} %add_convert_fusion.9), channel_id=1, source_target_pairs={{0,16},{4,20},{8,24},{12,28},{16,0},{20,4},{24,8},{28,12},{1,17},{... | collective-permute-start | bytes 442376 | tf_op jit(solution)/shard_map/ppermute | solution.py:668
  106.9 13.3 %collective-permute-start.21 = (bf16[1,96,768]{2,1,0:T(8,128)(2,1)S(1)}, bf16[1,96,768]{2,1,0:T(8,128)(2,1)S(1)}, u32[]{:S(2)}, u32[]{:S(2)}) collective-permute-start(bf16[1,96,768]{2,1,0:T(8,128)(2,1)S(1)} %get-tuple-element.266), channel_id=1, source_target_pairs={{0,16},{4,20},{8,24},{12,28},{16,0},{20,4},{24,8},{28,12},{1,17},{... | collective-permute-start | bytes 442376 | tf_op jit(solution)/shard_map/ppermute | solution.py:668
  107.5 13.1 %collective-permute-start.27 = (bf16[2,96,768]{2,1,0:T(8,128)(2,1)S(1)}, bf16[2,96,768]{2,1,0:T(8,128)(2,1)S(1)}, u32[]{:S(2)}, u32[]{:S(2)}) collective-permute-start(bf16[2,96,768]{2,1,0:T(8,128)(2,1)S(1)} %get-tuple-element.257), channel_id=1, source_target_pairs={{0,8},{4,12},{8,0},{12,4},{16,24},{20,28},{24,16},{28,20},{1,9},{5... | collective-permute-start | bytes 884744 | tf_op jit(solution)/shard_map/ppermute | solution.py:664
  120.8 6.1 %collective-permute-start.25 = (bf16[2,24,768]{2,1,0:T(8,128)(2,1)S(1)}, bf16[2,24,768]{2,1,0:T(8,128)(2,1)S(1)}, u32[]{:S(2)}, u32[]{:S(2)}) collective-permute-start(bf16[2,24,768]{2,1,0:T(8,128)(2,1)S(1)} %pad_maximum_fusion), channel_id=1, source_target_pairs={{0,1},{1,0},{2,3},{3,2},{4,5},{5,4},{6,7},{7,6},{8,9},{9,8},{10,11... | collective-permute-start | bytes 221192 | tf_op jit(solution)/shard_map/ppermute | solution.py:643
  120.9 11.3 %collective-permute-start.30 = (bf16[1,96,768]{2,1,0:T(8,128)(2,1)S(1)}, bf16[1,96,768]{2,1,0:T(8,128)(2,1)S(1)}, u32[]{:S(2)}, u32[]{:S(2)}) collective-permute-start(bf16[1,96,768]{2,1,0:T(8,128)(2,1)S(1)} %get-tuple-element.263), channel_id=1, source_target_pairs={{0,16},{4,20},{8,24},{12,28},{16,0},{20,4},{24,8},{28,12},{1,17},{... | collective-permute-start | bytes 442376 | tf_op jit(solution)/shard_map/ppermute | solution.py:668
  123.3 11.3 %collective-permute-start.33 = (bf16[2,96,768]{2,1,0:T(8,128)(2,1)S(1)}, bf16[2,96,768]{2,1,0:T(8,128)(2,1)S(1)}, u32[]{:S(2)}, u32[]{:S(2)}) collective-permute-start(bf16[2,96,768]{2,1,0:T(8,128)(2,1)S(1)} %constant_dynamic-update-slice_fusion), channel_id=1, source_target_pairs={{0,8},{4,12},{8,0},{12,4},{16,24},{20,28},{24,16},{28,20},{1,9},{5... | collective-permute-start | bytes 884744 | tf_op jit(solution)/shard_map/ppermute | solution.py:664
  125.8 15.6 %collective-permute-start.29 = (bf16[4,32,768]{2,1,0:T(8,128)(2,1)S(1)}, bf16[4,32,768]{2,1,0:T(8,128)(2,1)S(1)}, u32[]{:S(2)}, u32[]{:S(2)}) collective-permute-start(bf16[4,32,768]{2,1,0:T(8,128)(2,1)S(1)} %get-tuple-element.205), channel_id=1, source_target_pairs={{0,4},{4,0},{8,12},{12,8},{16,20},{20,16},{24,28},{28,24},{1,5},{5... | collective-permute-start | bytes 589832 | tf_op jit(solution)/shard_map/ppermute | solution.py:660
  126.9 5.1 %collective-permute-start.28 = (bf16[2,24,768]{2,1,0:T(8,128)(2,1)S(1)}, bf16[2,24,768]{2,1,0:T(8,128)(2,1)S(1)}, u32[]{:S(2)}, u32[]{:S(2)}) collective-permute-start(bf16[2,24,768]{2,1,0:T(8,128)(2,1)S(1)} %pad_maximum_fusion.1), channel_id=1, source_target_pairs={{0,2},{2,0},{1,3},{3,1},{4,6},{6,4},{5,7},{7,5},{8,10},{10,8},{9,1... | collective-permute-start | bytes 221192 | tf_op jit(solution)/shard_map/ppermute | solution.py:1580
  132.0 9.2 %collective-permute-start.31 = (bf16[1,96,768]{2,1,0:T(8,128)(2,1)S(1)}, bf16[1,96,768]{2,1,0:T(8,128)(2,1)S(1)}, u32[]{:S(2)}, u32[]{:S(2)}) collective-permute-start(bf16[1,96,768]{2,1,0:T(8,128)(2,1)S(1)} %maximum_bitcast_fusion), channel_id=1, source_target_pairs={{0,16},{4,20},{8,24},{12,28},{16,0},{20,4},{24,8},{28,12},{1,17},{... | collective-permute-start | bytes 442376 | tf_op jit(solution)/shard_map/ppermute | solution.py:668
  132.2 4.8 %collective-permute-start.32 = (bf16[2,24,576]{2,1,0:T(8,128)(2,1)S(1)}, bf16[2,24,576]{2,1,0:T(8,128)(2,1)S(1)}, u32[]{:S(2)}, u32[]{:S(2)}) collective-permute-start(bf16[2,24,576]{2,1,0:T(8,128)(2,1)S(1)} %pad_maximum_fusion.2), channel_id=1, source_target_pairs={{0,1},{1,0},{2,3},{3,2},{4,5},{5,4},{6,7},{7,6},{8,9},{9,8},{10,11... | collective-permute-start | bytes 165896 | tf_op jit(solution)/shard_map/ppermute | solution.py:643
  134.6 28.4 %collective-permute-start.39 = (bf16[4,96,768]{2,1,0:T(8,128)(2,1)S(1)}, bf16[4,96,768]{2,1,0:T(8,128)(2,1)S(1)}, u32[]{:S(2)}, u32[]{:S(2)}) collective-permute-start(bf16[4,96,768]{2,1,0:T(8,128)(2,1)S(1)} %constant_dynamic-update-slice_fusion.2.held), channel_id=1, source_target_pairs={{0,4},{4,0},{8,12},{12,8},{16,20},{20,16},{24,28},{28,24},{1,5},{5... | collective-permute-start | bytes 1769480 | tf_op jit(solution)/shard_map/ppermute | solution.py:660
  141.3 11.7 %collective-permute-start.34 = (bf16[2,96,768]{2,1,0:T(8,128)(2,1)S(1)}, bf16[2,96,768]{2,1,0:T(8,128)(2,1)S(1)}, u32[]{:S(2)}, u32[]{:S(2)}) collective-permute-start(bf16[2,96,768]{2,1,0:T(8,128)(2,1)S(1)} %constant_dynamic-update-slice_fusion.4), channel_id=1, source_target_pairs={{0,8},{4,12},{8,0},{12,4},{16,24},{20,28},{24,16},{28,20},{1,9},{5... | collective-permute-start | bytes 884744 | tf_op jit(solution)/shard_map/ppermute | solution.py:664
  141.5 4.3 %collective-permute-start.35 = (bf16[2,24,576]{2,1,0:T(8,128)(2,1)S(1)}, bf16[2,24,576]{2,1,0:T(8,128)(2,1)S(1)}, u32[]{:S(2)}, u32[]{:S(2)}) collective-permute-start(bf16[2,24,576]{2,1,0:T(8,128)(2,1)S(1)} %pad_maximum_fusion.3), channel_id=1, source_target_pairs={{0,2},{2,0},{1,3},{3,1},{4,6},{6,4},{5,7},{7,5},{8,10},{10,8},{9,1... | collective-permute-start | bytes 165896 | tf_op jit(solution)/shard_map/ppermute | solution.py:1593
  145.9 8.1 %collective-permute-start.37 = (bf16[1,96,768]{2,1,0:T(8,128)(2,1)S(1)}, bf16[1,96,768]{2,1,0:T(8,128)(2,1)S(1)}, u32[]{:S(2)}, u32[]{:S(2)}) collective-permute-start(bf16[1,96,768]{2,1,0:T(8,128)(2,1)S(1)} %maximum_bitcast_fusion.1), channel_id=1, source_target_pairs={{0,16},{4,20},{8,24},{12,28},{16,0},{20,4},{24,8},{28,12},{1,17},{... | collective-permute-start | bytes 442376 | tf_op jit(solution)/shard_map/ppermute | solution.py:668
  146.9 7.9 %collective-permute-start.40 = (bf16[2,32,768]{2,1,0:T(8,128)(2,1)S(1)}, bf16[2,32,768]{2,1,0:T(8,128)(2,1)S(1)}, u32[]{:S(2)}, u32[]{:S(2)}) collective-permute-start(bf16[2,32,768]{2,1,0:T(8,128)(2,1)S(1)} %get-tuple-element.269), channel_id=1, source_target_pairs={{0,8},{4,12},{8,0},{12,4},{16,24},{20,28},{24,16},{28,20},{1,9},{5... | collective-permute-start | bytes 294920 | tf_op jit(solution)/shard_map/ppermute | solution.py:664
  153.0 17.9 %collective-permute-start.36 = (bf16[4,96,768]{2,1,0:T(8,128)(2,1)S(1)}, bf16[4,96,768]{2,1,0:T(8,128)(2,1)S(1)}, u32[]{:S(2)}, u32[]{:S(2)}) collective-permute-start(bf16[4,96,768]{2,1,0:T(8,128)(2,1)S(1)} %constant_dynamic-update-slice_fusion.6.held), channel_id=1, source_target_pairs={{0,4},{4,0},{8,12},{12,8},{16,20},{20,16},{24,28},{28,24},{1,5},{5... | collective-permute-start | bytes 1769480 | tf_op jit(solution)/shard_map/ppermute | solution.py:660
  154.0 13.9 %collective-permute-start.38 = (bf16[2,96,768]{2,1,0:T(8,128)(2,1)S(1)}, bf16[2,96,768]{2,1,0:T(8,128)(2,1)S(1)}, u32[]{:S(2)}, u32[]{:S(2)}) collective-permute-start(bf16[2,96,768]{2,1,0:T(8,128)(2,1)S(1)} %constant_dynamic-update-slice_fusion.8), channel_id=1, source_target_pairs={{0,8},{4,12},{8,0},{12,4},{16,24},{20,28},{24,16},{28,20},{1,9},{5... | collective-permute-start | bytes 884744 | tf_op jit(solution)/shard_map/ppermute | solution.py:664
  154.8 5.2 %collective-permute-start.41 = (bf16[1,32,768]{2,1,0:T(8,128)(2,1)S(1)}, bf16[1,32,768]{2,1,0:T(8,128)(2,1)S(1)}, u32[]{:S(2)}, u32[]{:S(2)}) collective-permute-start(bf16[1,32,768]{2,1,0:T(8,128)(2,1)S(1)} %get-tuple-element.280), channel_id=1, source_target_pairs={{0,16},{4,20},{8,24},{12,28},{16,0},{20,4},{24,8},{28,12},{1,17},{... | collective-permute-start | bytes 147464 | tf_op jit(solution)/shard_map/ppermute | solution.py:668
  160.0 5.2 %collective-permute-start.42 = (bf16[1,32,768]{2,1,0:T(8,128)(2,1)S(1)}, bf16[1,32,768]{2,1,0:T(8,128)(2,1)S(1)}, u32[]{:S(2)}, u32[]{:S(2)}) collective-permute-start(bf16[1,32,768]{2,1,0:T(8,128)(2,1)S(1)} %add_convert_fusion.11), channel_id=1, source_target_pairs={{0,16},{4,20},{8,24},{12,28},{16,0},{20,4},{24,8},{28,12},{1,17},{... | collective-permute-start | bytes 147464 | tf_op jit(solution)/shard_map/ppermute | solution.py:668
  165.2 5.2 %collective-permute-start.43 = (bf16[2,32,768]{2,1,0:T(8,128)(2,1)S(1)}, bf16[2,32,768]{2,1,0:T(8,128)(2,1)S(1)}, u32[]{:S(2)}, u32[]{:S(2)}) collective-permute-start(bf16[2,32,768]{2,1,0:T(8,128)(2,1)S(1)} %constant_dynamic-update-slice_fusion.10), channel_id=1, source_target_pairs={{0,8},{4,12},{8,0},{12,4},{16,24},{20,28},{24,16},{28,20},{1,9},{5... | collective-permute-start | bytes 294920 | tf_op jit(solution)/shard_map/ppermute | solution.py:664
  167.9 12.4 %collective-permute-start.45 = (bf16[4,96,768]{2,1,0:T(8,128)(2,1)S(1)}, bf16[4,96,768]{2,1,0:T(8,128)(2,1)S(1)}, u32[]{:S(2)}, u32[]{:S(2)}) collective-permute-start(bf16[4,96,768]{2,1,0:T(8,128)(2,1)S(1)} %constant_dynamic-update-slice_fusion.12.held), channel_id=1, source_target_pairs={{0,4},{4,0},{8,12},{12,8},{16,20},{20,16},{24,28},{28,24},{1,5},{5... | collective-permute-start | bytes 1769480 | tf_op jit(solution)/shard_map/ppermute | solution.py:660
  170.5 11.9 %collective-permute-start.44 = (bf16[4,32,768]{2,1,0:T(8,128)(2,1)S(1)}, bf16[4,32,768]{2,1,0:T(8,128)(2,1)S(1)}, u32[]{:S(2)}, u32[]{:S(2)}) collective-permute-start(bf16[4,32,768]{2,1,0:T(8,128)(2,1)S(1)} %constant_dynamic-update-slice_fusion.14.held), channel_id=1, source_target_pairs={{0,4},{4,0},{8,12},{12,8},{16,20},{20,16},{24,28},{28,24},{1,5},{5... | collective-permute-start | bytes 589832 | tf_op jit(solution)/shard_map/ppermute | solution.py:660
  (27 other events, 222.2 us)

commit v2 on v1

--- a/solution.py
+++ b/solution.py
@@ -827,7 +827,7 @@
         rich_left[h] = rich_columns(rich_q, me, h).astype(BF)
         return carry
 
-    lax.fori_loop(0, OWN_HEADS, prepare, 0)
+    lax.fori_loop(0, OWN_HEADS, prepare, 0, unroll=True)
 
     def prob_copy(b):
         rows = pl.ds(pl.multiple_of(b * TOK, TOK), TOK)
@@ -909,7 +909,7 @@
         heads_out[h, ROWS:] = mixed.astype(BF)
         return carry
 
-    lax.fori_loop(0, OWN_HEADS, glob_head, 0)
+    lax.fori_loop(0, OWN_HEADS, glob_head, 0, unroll=True)
     for h in range(OWN_HEADS):
         attn_ref[:, h * HEAD_DIM : (h + 1) * HEAD_DIM] = heads_out[h]
     for half in range(2):
@@ -1152,7 +1152,7 @@
         key_rich[h] = nt(rich_kt[h].astype(BF), keys[h])
         return carry
 
-    lax.fori_loop(0, OWN_HEADS, prepare, 0)
+    lax.fori_loop(0, OWN_HEADS, prepare, 0, unroll=True)
     d_keys[...] = jnp.zeros((OWN_HEADS, PAD, HEAD_DIM), F32)
     d_values[...] = jnp.zeros((OWN_HEADS, PAD, HEAD_DIM), F32)
     d_key_rich[...] = jnp.zeros((OWN_HEADS, 8, PAD), F32)
@@ -1246,7 +1246,7 @@
         )
         return carry
 
-    lax.fori_loop(0, OWN_HEADS, glob_head, 0)
+    lax.fori_loop(0, OWN_HEADS, glob_head, 0, unroll=True)
     for i in range(3 * OWN_HEADS):
         d_qkv_ref[:, i * HEAD_DIM : (i + 1) * HEAD_DIM] = parts[i]
     rich[RICH:] = jnp.zeros((32 - RICH, HEAD_DIM), F32)
@@ -1275,9 +1275,9 @@
     total = None
     for i, weight in enumerate((w_query_ref, w_key_ref, w_value_ref)):
         weight_copies[i].wait()
-        for p in range(SEQ_WAYS):
-            term = nt(d_qkv[p, :, OWN * i : OWN * (i + 1)], weight[:, OWN * p : OWN * (p + 1)])
-            total = term if total is None else total + term
+        columns = [d_qkv[p, :, OWN * i : OWN * (i + 1)] for p in range(SEQ_WAYS)]
+        term = nt(jnp.concatenate(columns, axis=1), weight[...])
+        total = term if total is None else total + term
     d_norm[...] = total
     for copy in row_copies:
         copy.wait()

time: 184 us -> 182 us (0.989)
  Pallas kernels: 77.9 us -> 75.1 us
    pallas_call x13, Pallas kernels: 77.9 us -> 75.1 us  [call(): pl.pallas_call(kernel, out_shape=[jax.ShapeDtypeStruct(shape, kind) for s...]
  transfers between devices with their start and end apart: 46 -> 46, of which waited for: 20 -> 20; matrix products, arithmetic and copies ran while one was open for 1% -> 1% of each run, Pallas kernels for 42% -> 41%
where the time goes in v2:
time: 182 us
  Pallas kernels  75.1 us (41%)
  waiting for transfers between devices  54.1 us (30%)
  starting transfers between devices  46.8 us (26%)
  local copies, waits for them, and re-layouts  3.58 us (2%)
    pallas_call x13, Pallas kernels, call(): pl.pallas_call(kernel, out_shape=[jax.ShapeDtypeStruct(shape, kind) for s...  75.1 us
    ppermute x8, waiting for transfers between devices, swap_near(): return lax.ppermute(sent, 'grp', Z_NEAR)  16.1 us
    ppermute x5, waiting for transfers between devices, reach_seq(): lax.ppermute(block, 'seq', Y_SWAP)  14.7 us
    ppermute x8, starting transfers between devices, swap_far(): return lax.ppermute(sent, 'grp', Z_FAR)  13.7 us
    ppermute x8, starting transfers between devices, swap_near(): return lax.ppermute(sent, 'grp', Z_NEAR)  12.1 us
    ppermute x8, waiting for transfers between devices, swap_far(): return lax.ppermute(sent, 'grp', Z_FAR)  10.1 us
    ppermute x8, starting transfers between devices, swap_x(): return lax.ppermute(sent, 'grp', X_SWAP)  8.14 us
    ppermute x8, waiting for transfers between devices, swap_x(): return lax.ppermute(sent, 'grp', X_SWAP)  7.97 us
  transfers between devices with their start and end apart: 46, of which 20 were waited for; matrix products, arithmetic and copies ran while one was open for 1% of the time, Pallas kernels for 41%

profile of v2, /device:TPU:0, one launch (start us, length us, event | category | flops | bytes accessed | tf_op | source)
XLA Modules:
  0.0 181.9 jit_solution(12280947719131151980)
XLA Ops:
  0.7 3.0 %collective-permute-start.1 = (bf16[128,768]{1,0:T(8,128)(2,1)}, bf16[128,768]{1,0:T(8,128)(2,1)S(1)}, u32[]{:S(2)}, u32[]{:S(2)}) collective-permute-start(bf16[128,768]{1,0:T(8,128)(2,1)} %tok_a.1), channel_id=1, source_target_pairs={{0,2},{2,0},{1,3},{3,1},{4,6},{6,4},{5,7},{7,5},{8,10},{10,8},{9,1... | collective-permute-start | bytes 589832 | tf_op jit(solution)/shard_map/ppermute | solution.py:633
  3.7 1.4 shard_map.357.int_a
  5.1 3.9 %collective-permute-done.2.int_c = s32[16,128]{1,0:T(8,128)S(1)} collective-permute-done((s32[16,128]{1,0:T(8,128)}, s32[16,128]{1,0:T(8,128)S(1)}, u32[]{:S(2)}, u32[]{:S(2)}) %collective-permute-start.2) | collective-permute-done | bytes 8224 | tf_op jit(solution)/shard_map/ppermute | solution.py:633
  10.7 1.7 collective-permute-start.6
  13.3 17.7 %shard_map.358 = (bf16[288,384]{1,0:T(8,128)(2,1)}, f32[3,64,640]{2,1,0:T(8,128)}, f32[3,64,64]{2,1,0:T(8,128)}, f32[16,512]{1,0:T(8,128)}, bf16[512,256]{1,0:T(...) custom-call(bf16[128,768]{1,0:T(8,128)(2,1)} %tok_a.1, ...), custom_call_target="tpu_custom_call" | custom-call | flops 60000002048 | tf_op jit(solution)/shard_map/pallas_call | solution.py:1413
  31.0 1.2 collective-permute-start.8
  32.2 6.2 %collective-permute-done.8.att_c = bf16[288,384]{1,0:T(8,128)(2,1)S(1)} collective-permute-done((bf16[288,384]{1,0:T(8,128)(2,1)}, bf16[288,384]{1,0:T(8,128)(2,1)S(1)}, u32[]{:S(2)}, u32[]{:S(2)}) %collective-permute-start.8) | collective-permute-done | bytes 221216 | tf_op jit(solution)/shard_map/ppermute | solution.py:633
  40.9 9.8 %shard_map.359 = (bf16[128,768]{1,0:T(8,128)(2,1)}, bf16[176,768]{1,0:T(8,128)(2,1)S(1)}) custom-call(bf16[288,384]{1,0:T(8,128)(2,1)S(1)} %copy-done.2, bf16[288,384]{1,0:T(8,128)(2,1)S(1)} %collective-permute-done.7.att_b, bf16[288,384]{1,0:T(8,128)(2,1)S(1)} %collective-permute-done.8.att_c, bf16[288,384]{1,0:T(8,128)(2,1)S(1)} %collective-permute-done.9.att_d, ...), custom_call_target="tpu_custom_call" | custom-call | flops 60000002048 | tf_op jit(solution)/shard_map/pallas_call | solution.py:1413
  50.6 1.6 collective-permute-start.13
  52.3 6.7 %shard_map.360 = (bf16[4,96,768]{2,1,0:T(8,128)(2,1)S(1)}, bf16[4,96,768]{2,1,0:T(8,128)(2,1)S(1)}, bf16[576,768]{1,0:T(8,128)(2,1)S(1)}, f32[576,768]{1,0:T(8,128)}, bf16[576,768]{1,0:T(8,128)(2,1)}) custom-call(bf16[288,384]{1,0:T(8,128)(2,1)S(1)} %copy-done.2, bf16[288,384]{1,0:T(8,128)(2,1)S(1)} %collective-permute-done.7.att_b, ...), custom_call_target="tpu_custom_call" | custom-call | flops 60000002048 | tf_op jit(solution)/shard_map/pallas_call | solution.py:1413
  59.0 1.6 collective-permute-start.15
  60.7 1.2 copy-done.15
  61.9 4.7 %shard_map.361 = (bf16[4,96,768]{2,1,0:T(8,128)(2,1)S(1)}, bf16[4,96,768]{2,1,0:T(8,128)(2,1)S(1)}, f32[1,768]{1,0:T(1,128)S(1)}) custom-call(bf16[576,768]{1,0:T(8,128)(2,1)S(1)} %get-tuple-element.156.normed_ref, f32[576,768]{1,0:T(8,128)} %get-tuple-element.157.slope_ref, bf16[576,768]{1,0:T(8,128)(2,1)S(1)} %copy-done.15, bf16[3072,768]{1,0:T(8,128)(2,1)} %w_down_any.3), custom_call_target="tpu_custom_call" | custom-call | flops 60000002048 | tf_op jit(solution)/shard_map/pallas_call | solution.py:1413
  67.3 15.0 %shard_map.362 = (bf16[576,768]{1,0:T(8,128)(2,1)S(1)}, bf16[576,640]{1,0:T(8,128)(2,1)S(1)}, f32[8,768]{1,0:T(8,128)S(1)}, bf16[64,768]{1,0:T(8,128)(2,1)}) custom-call(bf16[176,768]{1,0:T(8,128)(2,1)S(1)} %get-tuple-element.147.back_a, bf16[176,768]{1,0:T(8,128)(2,1)S(1)} %collective-permute-done.10.back_b, ...), custom_call_target="tpu_custom_call" | custom-call | flops 60000002048 | tf_op jit(solution)/shard_map/pallas_call | solution.py:1413
  82.3 1.1 collective-permute-start.20
  83.5 1.6 collective-permute-start.16
  85.2 1.5 shard_map.363
  86.7 1.1 collective-permute-start.24
  88.0 1.3 collective-permute-start.19
  89.2 4.2 %collective-permute-done.16 = bf16[2,96,768]{2,1,0:T(8,128)(2,1)S(1)} collective-permute-done((bf16[2,96,768]{2,1,0:T(8,128)(2,1)S(1)}, bf16[2,96,768]{2,1,0:T(8,128)(2,1)S(1)}, u32[]{:S(2)}, u32[]{:S(2)}) %collective-permute-start.16) | collective-permute-done | bytes 294944 | tf_op jit(solution)/shard_map/ppermute | solution.py:664
  93.5 2.6 %collective-permute-start.18 = (bf16[1,96,768]{2,1,0:T(8,128)(2,1)S(1)}, bf16[1,96,768]{2,1,0:T(8,128)(2,1)S(1)}, u32[]{:S(2)}, u32[]{:S(2)}) collective-permute-start(bf16[1,96,768]{2,1,0:T(8,128)(2,1)S(1)} %get-tuple-element.267), channel_id=1, source_target_pairs={{0,16},{4,20},{8,24},{12,28},{16,0},{20,4},{24,8},{28,12},{1,17},{... | collective-permute-start | bytes 442376 | tf_op jit(solution)/shard_map/ppermute | solution.py:668
  96.2 4.6 %collective-permute-done.20.dqkv_c = bf16[576,640]{1,0:T(8,128)(2,1)S(1)} collective-permute-done((bf16[576,640]{1,0:T(8,128)(2,1)S(1)}, bf16[576,640]{1,0:T(8,128)(2,1)S(1)}, u32[]{:S(2)}, u32[]{:S(2)}) %collective-permute-start.20) | collective-permute-done | bytes 737312 | tf_op jit(solution)/shard_map/ppermute | solution.py:633
  100.8 1.7 collective-permute-done.19
  102.7 2.5 %collective-permute-start.26 = (bf16[1,96,768]{2,1,0:T(8,128)(2,1)S(1)}, bf16[1,96,768]{2,1,0:T(8,128)(2,1)S(1)}, u32[]{:S(2)}, u32[]{:S(2)}) collective-permute-start(bf16[1,96,768]{2,1,0:T(8,128)(2,1)S(1)} %add_convert_fusion.9), channel_id=1, source_target_pairs={{0,16},{4,20},{8,24},{12,28},{16,0},{20,4},{24,8},{28,12},{1,17},{... | collective-permute-start | bytes 442376 | tf_op jit(solution)/shard_map/ppermute | solution.py:668
  105.9 2.5 %collective-permute-start.27 = (bf16[2,96,768]{2,1,0:T(8,128)(2,1)S(1)}, bf16[2,96,768]{2,1,0:T(8,128)(2,1)S(1)}, u32[]{:S(2)}, u32[]{:S(2)}) collective-permute-start(bf16[2,96,768]{2,1,0:T(8,128)(2,1)S(1)} %get-tuple-element.257), channel_id=1, source_target_pairs={{0,8},{4,12},{8,0},{12,4},{16,24},{20,28},{24,16},{28,20},{1,9},{5... | collective-permute-start | bytes 884744 | tf_op jit(solution)/shard_map/ppermute | solution.py:664
  108.4 8.8 %shard_map.364 = (f32[64,768]{1,0:T(8,128)}, bf16[4,32,768]{2,1,0:T(8,128)(2,1)S(1)}, bf16[4,32,768]{2,1,0:T(8,128)(2,1)S(1)}, f32[128,768]{1,0:T(8,128)S(1)}, bf16[512,768]{1,0:T(8,128)(2,1)}) custom-call(bf16[576,640]{1,0:T(8,128)(2,1)S(1)} %get-tuple-element.168.d_qkv_ref.dqkv_a, bf16[576,640]{1,0:T(8,128)(2,1)S(1)} %collective-permute-done.22.dqkv_b, ...), custom_call_target="tpu_custom_call" | custom-call | flops 60000002048 | tf_op jit(solution)/shard_map/pallas_call | solution.py:1413
  117.2 1.5 collective-permute-done.21
  119.3 2.4 %collective-permute-start.30 = (bf16[1,96,768]{2,1,0:T(8,128)(2,1)S(1)}, bf16[1,96,768]{2,1,0:T(8,128)(2,1)S(1)}, u32[]{:S(2)}, u32[]{:S(2)}) collective-permute-start(bf16[1,96,768]{2,1,0:T(8,128)(2,1)S(1)} %get-tuple-element.263), channel_id=1, source_target_pairs={{0,16},{4,20},{8,24},{12,28},{16,0},{20,4},{24,8},{28,12},{1,17},{... | collective-permute-start | bytes 442376 | tf_op jit(solution)/shard_map/ppermute | solution.py:668
  121.8 2.5 %collective-permute-start.33 = (bf16[2,96,768]{2,1,0:T(8,128)(2,1)S(1)}, bf16[2,96,768]{2,1,0:T(8,128)(2,1)S(1)}, u32[]{:S(2)}, u32[]{:S(2)}) collective-permute-start(bf16[2,96,768]{2,1,0:T(8,128)(2,1)S(1)} %constant_dynamic-update-slice_fusion), channel_id=1, source_target_pairs={{0,8},{4,12},{8,0},{12,4},{16,24},{20,28},{24,16},{28,20},{1,9},{5... | collective-permute-start | bytes 884744 | tf_op jit(solution)/shard_map/ppermute | solution.py:664
  124.3 1.0 collective-permute-start.29
  125.3 1.6 collective-permute-start.28
  126.9 3.5 %shard_map.365 = f32[128,768]{1,0:T(8,128)} custom-call(f32[128,768]{1,0:T(8,128)S(1)} %get-tuple-element.201.d_own_ref, bf16[512,768]{1,0:T(8,128)(2,1)S(1)} %copy-done.17, f32[16,512]{1,0:T(8,128)S(1)} %copy-done.21, bf16[768,768]{1,0:T(8,128)(2,1)S(1)} %copy-done.1), custom_call_target="tpu_custom_call" | custom-call | flops 60000002048 | tf_op jit(solution)/shard_map/pallas_call | solution.py:1413
  130.8 2.3 %collective-permute-done.33 = bf16[2,96,768]{2,1,0:T(8,128)(2,1)S(1)} collective-permute-done((bf16[2,96,768]{2,1,0:T(8,128)(2,1)S(1)}, bf16[2,96,768]{2,1,0:T(8,128)(2,1)S(1)}, u32[]{:S(2)}, u32[]{:S(2)}) %collective-permute-start.33) | collective-permute-done | bytes 294944 | tf_op jit(solution)/shard_map/ppermute | solution.py:664
  133.1 2.4 %collective-permute-start.39 = (bf16[4,96,768]{2,1,0:T(8,128)(2,1)S(1)}, bf16[4,96,768]{2,1,0:T(8,128)(2,1)S(1)}, u32[]{:S(2)}, u32[]{:S(2)}) collective-permute-start(bf16[4,96,768]{2,1,0:T(8,128)(2,1)S(1)} %constant_dynamic-update-slice_fusion.2.held), channel_id=1, source_target_pairs={{0,4},{4,0},{8,12},{12,8},{16,20},{20,16},{24,28},{28,24},{1,5},{5... | collective-permute-start | bytes 1769480 | tf_op jit(solution)/shard_map/ppermute | solution.py:660
  135.5 4.2 %collective-permute-done.31 = bf16[1,96,768]{2,1,0:T(8,128)(2,1)S(1)} collective-permute-done((bf16[1,96,768]{2,1,0:T(8,128)(2,1)S(1)}, bf16[1,96,768]{2,1,0:T(8,128)(2,1)S(1)}, u32[]{:S(2)}, u32[]{:S(2)}) %collective-permute-start.31) | collective-permute-done | bytes 147488 | tf_op jit(solution)/shard_map/ppermute | solution.py:668
  140.7 3.6 %collective-permute-done.35 = bf16[2,24,576]{2,1,0:T(8,128)(2,1)S(1)} collective-permute-done((bf16[2,24,576]{2,1,0:T(8,128)(2,1)S(1)}, bf16[2,24,576]{2,1,0:T(8,128)(2,1)S(1)}, u32[]{:S(2)}, u32[]{:S(2)}) %collective-permute-start.35) | collective-permute-done | bytes 55328 | tf_op jit(solution)/shard_map/ppermute | solution.py:1593
  145.3 1.2 collective-permute-start.40
  146.5 4.9 %collective-permute-done.34 = bf16[2,96,768]{2,1,0:T(8,128)(2,1)S(1)} collective-permute-done((bf16[2,96,768]{2,1,0:T(8,128)(2,1)S(1)}, bf16[2,96,768]{2,1,0:T(8,128)(2,1)S(1)}, u32[]{:S(2)}, u32[]{:S(2)}) %collective-permute-start.34) | collective-permute-done | bytes 294944 | tf_op jit(solution)/shard_map/ppermute | solution.py:664
  153.3 1.5 collective-permute-start.41
  154.8 3.6 %collective-permute-done.41 = bf16[1,32,768]{2,1,0:T(8,128)(2,1)S(1)} collective-permute-done((bf16[1,32,768]{2,1,0:T(8,128)(2,1)S(1)}, bf16[1,32,768]{2,1,0:T(8,128)(2,1)S(1)}, u32[]{:S(2)}, u32[]{:S(2)}) %collective-permute-start.41) | collective-permute-done | bytes 49184 | tf_op jit(solution)/shard_map/ppermute | solution.py:668
  158.5 3.0 %collective-permute-start.42 = (bf16[1,32,768]{2,1,0:T(8,128)(2,1)S(1)}, bf16[1,32,768]{2,1,0:T(8,128)(2,1)S(1)}, u32[]{:S(2)}, u32[]{:S(2)}) collective-permute-start(bf16[1,32,768]{2,1,0:T(8,128)(2,1)S(1)} %add_convert_fusion.11), channel_id=1, source_target_pairs={{0,16},{4,20},{8,24},{12,28},{16,0},{20,4},{24,8},{28,12},{1,17},{... | collective-permute-start | bytes 147464 | tf_op jit(solution)/shard_map/ppermute | solution.py:668
  161.5 1.6 shard_map.366
  163.7 2.6 %collective-permute-start.43 = (bf16[2,32,768]{2,1,0:T(8,128)(2,1)S(1)}, bf16[2,32,768]{2,1,0:T(8,128)(2,1)S(1)}, u32[]{:S(2)}, u32[]{:S(2)}) collective-permute-start(bf16[2,32,768]{2,1,0:T(8,128)(2,1)S(1)} %constant_dynamic-update-slice_fusion.10), channel_id=1, source_target_pairs={{0,8},{4,12},{8,0},{12,4},{16,24},{20,28},{24,16},{28,20},{1,9},{5... | collective-permute-start | bytes 294920 | tf_op jit(solution)/shard_map/ppermute | solution.py:664
  166.8 2.1 %collective-permute-done.43 = bf16[2,32,768]{2,1,0:T(8,128)(2,1)S(1)} collective-permute-done((bf16[2,32,768]{2,1,0:T(8,128)(2,1)S(1)}, bf16[2,32,768]{2,1,0:T(8,128)(2,1)S(1)}, u32[]{:S(2)}, u32[]{:S(2)}) %collective-permute-start.43) | collective-permute-done | bytes 98336 | tf_op jit(solution)/shard_map/ppermute | solution.py:664
  169.3 1.6 shard_map.367
  170.9 7.9 %collective-permute-done.45.came = bf16[4,96,768]{2,1,0:T(8,128)(2,1)S(1)} collective-permute-done((bf16[4,96,768]{2,1,0:T(8,128)(2,1)S(1)}, bf16[4,96,768]{2,1,0:T(8,128)(2,1)S(1)}, u32[]{:S(2)}, u32[]{:S(2)}) %collective-permute-start.45) | collective-permute-done | bytes 589856 | tf_op jit(solution)/shard_map/ppermute | solution.py:660
  178.8 2.0 %shard_map.368 = (f32[192,768]{1,0:T(8,128)}, f32[192,768]{1,0:T(8,128)}, f32[192,768]{1,0:T(8,128)}, f32[192,768]{1,0:T(8,128)}) custom-call(bf16[4,96,768]{2,1,0:T(8,128)(2,1)S(1)} %constant_dynamic-update-slice_fusion.12.held, bf16[4,96,768]{2,1,0:T(8,128)(2,1)S(1)} %collective-permute-done.45.came), custom_call_target="tpu_custom_call" | custom-call | flops 60000002048 | tf_op jit(solution)/shard_map/pallas_call | solution.py:1413
  180.9 1.1 shard_map.369
  (169 shorter events, 13.5 us)
Async XLA Ops:
  0.7 9.5 %collective-permute-start.1 = (bf16[128,768]{1,0:T(8,128)(2,1)}, bf16[128,768]{1,0:T(8,128)(2,1)S(1)}, u32[]{:S(2)}, u32[]{:S(2)}) collective-permute-start(bf16[128,768]{1,0:T(8,128)(2,1)} %tok_a.1), channel_id=1, source_target_pairs={{0,2},{2,0},{1,3},{3,1},{4,6},{6,4},{5,7},{7,5},{8,10},{10,8},{9,1... | collective-permute-start | bytes 589832 | tf_op jit(solution)/shard_map/ppermute | solution.py:633
  5.0 3.9 %collective-permute-start.2 = (s32[16,128]{1,0:T(8,128)}, s32[16,128]{1,0:T(8,128)S(1)}, u32[]{:S(2)}, u32[]{:S(2)}) collective-permute-start(s32[16,128]{1,0:T(8,128)} %shard_map.357.int_a), channel_id=1, source_target_pairs={{0,2},{2,0},{1,3},{3,1},{4,6},{6,4},{5,7},{7,5},{8,10},{10,8},{9,1... | collective-permute-start | bytes 24584 | tf_op jit(solution)/shard_map/ppermute | solution.py:633
  9.0 1.2 collective-permute-start.3
  9.0 3.5 %collective-permute-start = (bf16[128,768]{1,0:T(8,128)(2,1)S(1)}, bf16[128,768]{1,0:T(8,128)(2,1)S(1)}, u32[]{:S(2)}, u32[]{:S(2)}) collective-permute-start(bf16[128,768]{1,0:T(8,128)(2,1)S(1)} %copy-done.22), channel_id=1, source_target_pairs={{0,1},{1,0},{2,3},{3,2},{4,5},{5,4},{6,7},{7,6},{8,9},{9,8},{10,11... | collective-permute-start | bytes 589832 | tf_op jit(solution)/shard_map/ppermute | solution.py:633
  10.2 2.3 %collective-permute-start.4 = (bf16[128,768]{1,0:T(8,128)(2,1)S(1)}, bf16[128,768]{1,0:T(8,128)(2,1)S(1)}, u32[]{:S(2)}, u32[]{:S(2)}) collective-permute-start(bf16[128,768]{1,0:T(8,128)(2,1)S(1)} %collective-permute-done.1.tok_c), channel_id=1, source_target_pairs={{0,1},{1,0},{2,3},{3,2},{4,5},{5,4},{6,7},{7,6},{8,9},{9,8},{10,11... | collective-permute-start | bytes 589832 | tf_op jit(solution)/shard_map/ppermute | solution.py:1441
  10.3 2.1 %collective-permute-start.5 = (s32[16,128]{1,0:T(8,128)}, s32[16,128]{1,0:T(8,128)S(1)}, u32[]{:S(2)}, u32[]{:S(2)}) collective-permute-start(s32[16,128]{1,0:T(8,128)} %shard_map.357.int_a), channel_id=1, source_target_pairs={{0,1},{1,0},{2,3},{3,2},{4,5},{5,4},{6,7},{7,6},{8,9},{9,8},{10,11... | collective-permute-start | bytes 24584 | tf_op jit(solution)/shard_map/ppermute | solution.py:633
  10.7 20.2 %collective-permute-start.6 = (bf16[128,768]{1,0:T(8,128)(2,1)S(1)}, bf16[128,768]{1,0:T(8,128)(2,1)S(1)}, u32[]{:S(2)}, u32[]{:S(2)}) collective-permute-start(bf16[128,768]{1,0:T(8,128)(2,1)S(1)} %copy-done.4), channel_id=1, source_target_pairs={{0,2},{2,0},{1,3},{3,1},{4,6},{6,4},{5,7},{7,5},{8,10},{10,8},{9,1... | collective-permute-start | bytes 589832 | tf_op jit(solution)/shard_map/ppermute | solution.py:1440
  13.2 26.7 %copy-start.10 = (f32[768]{0:T(1024)S(1)}, f32[768]{0:T(1024)}, u32[]{:S(2)}) copy-start(f32[768]{0:T(1024)} %bias_down_ref.1) | copy-start | bytes 9220
  13.3 26.7 %copy-start.11 = (f32[768]{0:T(1024)S(1)}, f32[768]{0:T(1024)}, u32[]{:S(2)}) copy-start(f32[768]{0:T(1024)} %gain_ref.5) | copy-start | bytes 9220
  31.0 7.4 %collective-permute-start.8 = (bf16[288,384]{1,0:T(8,128)(2,1)}, bf16[288,384]{1,0:T(8,128)(2,1)S(1)}, u32[]{:S(2)}, u32[]{:S(2)}) collective-permute-start(bf16[288,384]{1,0:T(8,128)(2,1)} %get-tuple-element.142.att_a.attn_ref), channel_id=1, source_target_pairs={{0,2},{2,0},{1,3},{3,1},{4,6},{6,4},{5,7},{7,5},{8,10},{10,8},{9,1... | collective-permute-start | bytes 663560 | tf_op jit(solution)/shard_map/ppermute | solution.py:633
  32.2 6.7 %collective-permute-start.7 = (bf16[288,384]{1,0:T(8,128)(2,1)}, bf16[288,384]{1,0:T(8,128)(2,1)S(1)}, u32[]{:S(2)}, u32[]{:S(2)}) collective-permute-start(bf16[288,384]{1,0:T(8,128)(2,1)} %get-tuple-element.142.att_a.attn_ref), channel_id=1, source_target_pairs={{0,1},{1,0},{2,3},{3,2},{4,5},{5,4},{6,7},{7,6},{8,9},{9,8},{10,11... | collective-permute-start | bytes 663560 | tf_op jit(solution)/shard_map/ppermute | solution.py:633
  38.4 1.5 collective-permute-start.9
  38.4 13.9 %collective-permute-start.11 = (bf16[128,768]{1,0:T(8,128)(2,1)S(1)}, bf16[128,768]{1,0:T(8,128)(2,1)S(1)}, u32[]{:S(2)}, u32[]{:S(2)}) collective-permute-start(bf16[128,768]{1,0:T(8,128)(2,1)S(1)} %copy-done.4), channel_id=1, source_target_pairs={{0,1},{1,0},{2,3},{3,2},{4,5},{5,4},{6,7},{7,6},{8,9},{9,8},{10,11... | collective-permute-start | bytes 589832 | tf_op jit(solution)/shard_map/ppermute | solution.py:1471
  38.9 13.4 %collective-permute-start.12 = (bf16[128,768]{1,0:T(8,128)(2,1)S(1)}, bf16[128,768]{1,0:T(8,128)(2,1)S(1)}, u32[]{:S(2)}, u32[]{:S(2)}) collective-permute-start(bf16[128,768]{1,0:T(8,128)(2,1)S(1)} %collective-permute-done.6.cot_c), channel_id=1, source_target_pairs={{0,1},{1,0},{2,3},{3,2},{4,5},{5,4},{6,7},{7,6},{8,9},{9,8},{10,11... | collective-permute-start | bytes 589832 | tf_op jit(solution)/shard_map/ppermute | solution.py:1472
  50.6 9.9 %collective-permute-start.13 = (bf16[176,768]{1,0:T(8,128)(2,1)S(1)}, bf16[176,768]{1,0:T(8,128)(2,1)S(1)}, u32[]{:S(2)}, u32[]{:S(2)}) collective-permute-start(bf16[176,768]{1,0:T(8,128)(2,1)S(1)} %get-tuple-element.147.back_a), channel_id=1, source_target_pairs={{0,2},{2,0},{1,3},{3,1},{4,6},{6,4},{5,7},{7,5},{8,10},{10,8},{9,1... | collective-permute-start | bytes 811016 | tf_op jit(solution)/shard_map/ppermute | solution.py:633
  52.3 14.9 %collective-permute-start.10 = (bf16[176,768]{1,0:T(8,128)(2,1)S(1)}, bf16[176,768]{1,0:T(8,128)(2,1)S(1)}, u32[]{:S(2)}, u32[]{:S(2)}) collective-permute-start(bf16[176,768]{1,0:T(8,128)(2,1)S(1)} %get-tuple-element.147.back_a), channel_id=1, source_target_pairs={{0,1},{1,0},{2,3},{3,2},{4,5},{5,4},{6,7},{7,6},{8,9},{9,8},{10,11... | collective-permute-start | bytes 811016 | tf_op jit(solution)/shard_map/ppermute | solution.py:633
  59.0 24.3 %collective-permute-start.15 = (bf16[4,96,768]{2,1,0:T(8,128)(2,1)S(1)}, bf16[4,96,768]{2,1,0:T(8,128)(2,1)S(1)}, u32[]{:S(2)}, u32[]{:S(2)}) collective-permute-start(bf16[4,96,768]{2,1,0:T(8,128)(2,1)S(1)} %get-tuple-element.167), channel_id=1, source_target_pairs={{0,4},{4,0},{8,12},{12,8},{16,20},{20,16},{24,28},{28,24},{1,5},{5... | collective-permute-start | bytes 1769480 | tf_op jit(solution)/shard_map/ppermute | solution.py:660
  60.5 6.7 %collective-permute-start.14 = (bf16[176,768]{1,0:T(8,128)(2,1)S(1)}, bf16[176,768]{1,0:T(8,128)(2,1)S(1)}, u32[]{:S(2)}, u32[]{:S(2)}) collective-permute-start(bf16[176,768]{1,0:T(8,128)(2,1)S(1)} %collective-permute-done.13.back_c), channel_id=1, source_target_pairs={{0,1},{1,0},{2,3},{3,2},{4,5},{5,4},{6,7},{7,6},{8,9},{9,8},{10,11... | collective-permute-start | bytes 811016 | tf_op jit(solution)/shard_map/ppermute | solution.py:1497
  66.6 21.1 %collective-permute-start.17 = (bf16[4,96,768]{2,1,0:T(8,128)(2,1)S(1)}, bf16[4,96,768]{2,1,0:T(8,128)(2,1)S(1)}, u32[]{:S(2)}, u32[]{:S(2)}) collective-permute-start(bf16[4,96,768]{2,1,0:T(8,128)(2,1)S(1)} %get-tuple-element.172), channel_id=1, source_target_pairs={{0,4},{4,0},{8,12},{12,8},{16,20},{20,16},{24,28},{28,24},{1,5},{5... | collective-permute-start | bytes 1769480 | tf_op jit(solution)/shard_map/ppermute | solution.py:660
  82.3 18.5 %collective-permute-start.20 = (bf16[576,640]{1,0:T(8,128)(2,1)S(1)}, bf16[576,640]{1,0:T(8,128)(2,1)S(1)}, u32[]{:S(2)}, u32[]{:S(2)}) collective-permute-start(bf16[576,640]{1,0:T(8,128)(2,1)S(1)} %get-tuple-element.168.d_qkv_ref.dqkv_a), channel_id=1, source_target_pairs={{0,2},{2,0},{1,3},{3,1},{4,6},{6,4},{5,7},{7,5},{8,10},{10,8},{9,1... | collective-permute-start | bytes 2211848 | tf_op jit(solution)/shard_map/ppermute | solution.py:633
  83.3 25.1 %collective-permute-start.22 = (bf16[576,640]{1,0:T(8,128)(2,1)S(1)}, bf16[576,640]{1,0:T(8,128)(2,1)S(1)}, u32[]{:S(2)}, u32[]{:S(2)}) collective-permute-start(bf16[576,640]{1,0:T(8,128)(2,1)S(1)} %get-tuple-element.168.d_qkv_ref.dqkv_a), channel_id=1, source_target_pairs={{0,1},{1,0},{2,3},{3,2},{4,5},{5,4},{6,7},{7,6},{8,9},{9,8},{10,11... | collective-permute-start | bytes 2211848 | tf_op jit(solution)/shard_map/ppermute | solution.py:633
  83.5 9.9 %collective-permute-start.16 = (bf16[2,96,768]{2,1,0:T(8,128)(2,1)S(1)}, bf16[2,96,768]{2,1,0:T(8,128)(2,1)S(1)}, u32[]{:S(2)}, u32[]{:S(2)}) collective-permute-start(bf16[2,96,768]{2,1,0:T(8,128)(2,1)S(1)} %get-tuple-element.261), channel_id=1, source_target_pairs={{0,8},{4,12},{8,0},{12,4},{16,24},{20,28},{24,16},{28,20},{1,9},{5... | collective-permute-start | bytes 884744 | tf_op jit(solution)/shard_map/ppermute | solution.py:664
  86.7 18.5 %collective-permute-start.24 = (bf16[4,96,768]{2,1,0:T(8,128)(2,1)S(1)}, bf16[4,96,768]{2,1,0:T(8,128)(2,1)S(1)}, u32[]{:S(2)}, u32[]{:S(2)}) collective-permute-start(bf16[4,96,768]{2,1,0:T(8,128)(2,1)S(1)} %get-tuple-element.185), channel_id=1, source_target_pairs={{0,4},{4,0},{8,12},{12,8},{16,20},{20,16},{24,28},{28,24},{1,5},{5... | collective-permute-start | bytes 1769480 | tf_op jit(solution)/shard_map/ppermute | solution.py:660
  88.0 14.5 %collective-permute-start.19 = (bf16[2,96,768]{2,1,0:T(8,128)(2,1)S(1)}, bf16[2,96,768]{2,1,0:T(8,128)(2,1)S(1)}, u32[]{:S(2)}, u32[]{:S(2)}) collective-permute-start(bf16[2,96,768]{2,1,0:T(8,128)(2,1)S(1)} %get-tuple-element.260), channel_id=1, source_target_pairs={{0,8},{4,12},{8,0},{12,4},{16,24},{20,28},{24,16},{28,20},{1,9},{5... | collective-permute-start | bytes 884744 | tf_op jit(solution)/shard_map/ppermute | solution.py:664
  93.5 9.1 %collective-permute-start.18 = (bf16[1,96,768]{2,1,0:T(8,128)(2,1)S(1)}, bf16[1,96,768]{2,1,0:T(8,128)(2,1)S(1)}, u32[]{:S(2)}, u32[]{:S(2)}) collective-permute-start(bf16[1,96,768]{2,1,0:T(8,128)(2,1)S(1)} %get-tuple-element.267), channel_id=1, source_target_pairs={{0,16},{4,20},{8,24},{12,28},{16,0},{20,4},{24,8},{28,12},{1,17},{... | collective-permute-start | bytes 442376 | tf_op jit(solution)/shard_map/ppermute | solution.py:668
  100.7 7.7 %collective-permute-start.23 = (bf16[576,640]{1,0:T(8,128)(2,1)S(1)}, bf16[576,640]{1,0:T(8,128)(2,1)S(1)}, u32[]{:S(2)}, u32[]{:S(2)}) collective-permute-start(bf16[576,640]{1,0:T(8,128)(2,1)S(1)} %collective-permute-done.20.dqkv_c), channel_id=1, source_target_pairs={{0,1},{1,0},{2,3},{3,2},{4,5},{5,4},{6,7},{7,6},{8,9},{9,8},{10,11... | collective-permute-start | bytes 2211848 | tf_op jit(solution)/shard_map/ppermute | solution.py:1558
  102.7 16.5 %collective-permute-start.26 = (bf16[1,96,768]{2,1,0:T(8,128)(2,1)S(1)}, bf16[1,96,768]{2,1,0:T(8,128)(2,1)S(1)}, u32[]{:S(2)}, u32[]{:S(2)}) collective-permute-start(bf16[1,96,768]{2,1,0:T(8,128)(2,1)S(1)} %add_convert_fusion.9), channel_id=1, source_target_pairs={{0,16},{4,20},{8,24},{12,28},{16,0},{20,4},{24,8},{28,12},{1,17},{... | collective-permute-start | bytes 442376 | tf_op jit(solution)/shard_map/ppermute | solution.py:668
  105.4 13.3 %collective-permute-start.21 = (bf16[1,96,768]{2,1,0:T(8,128)(2,1)S(1)}, bf16[1,96,768]{2,1,0:T(8,128)(2,1)S(1)}, u32[]{:S(2)}, u32[]{:S(2)}) collective-permute-start(bf16[1,96,768]{2,1,0:T(8,128)(2,1)S(1)} %get-tuple-element.266), channel_id=1, source_target_pairs={{0,16},{4,20},{8,24},{12,28},{16,0},{20,4},{24,8},{28,12},{1,17},{... | collective-permute-start | bytes 442376 | tf_op jit(solution)/shard_map/ppermute | solution.py:668
  105.9 13.1 %collective-permute-start.27 = (bf16[2,96,768]{2,1,0:T(8,128)(2,1)S(1)}, bf16[2,96,768]{2,1,0:T(8,128)(2,1)S(1)}, u32[]{:S(2)}, u32[]{:S(2)}) collective-permute-start(bf16[2,96,768]{2,1,0:T(8,128)(2,1)S(1)} %get-tuple-element.257), channel_id=1, source_target_pairs={{0,8},{4,12},{8,0},{12,4},{16,24},{20,28},{24,16},{28,20},{1,9},{5... | collective-permute-start | bytes 884744 | tf_op jit(solution)/shard_map/ppermute | solution.py:664
  119.2 6.1 %collective-permute-start.25 = (bf16[2,24,768]{2,1,0:T(8,128)(2,1)S(1)}, bf16[2,24,768]{2,1,0:T(8,128)(2,1)S(1)}, u32[]{:S(2)}, u32[]{:S(2)}) collective-permute-start(bf16[2,24,768]{2,1,0:T(8,128)(2,1)S(1)} %pad_maximum_fusion), channel_id=1, source_target_pairs={{0,1},{1,0},{2,3},{3,2},{4,5},{5,4},{6,7},{7,6},{8,9},{9,8},{10,11... | collective-permute-start | bytes 221192 | tf_op jit(solution)/shard_map/ppermute | solution.py:643
  119.3 11.3 %collective-permute-start.30 = (bf16[1,96,768]{2,1,0:T(8,128)(2,1)S(1)}, bf16[1,96,768]{2,1,0:T(8,128)(2,1)S(1)}, u32[]{:S(2)}, u32[]{:S(2)}) collective-permute-start(bf16[1,96,768]{2,1,0:T(8,128)(2,1)S(1)} %get-tuple-element.263), channel_id=1, source_target_pairs={{0,16},{4,20},{8,24},{12,28},{16,0},{20,4},{24,8},{28,12},{1,17},{... | collective-permute-start | bytes 442376 | tf_op jit(solution)/shard_map/ppermute | solution.py:668
  121.8 11.3 %collective-permute-start.33 = (bf16[2,96,768]{2,1,0:T(8,128)(2,1)S(1)}, bf16[2,96,768]{2,1,0:T(8,128)(2,1)S(1)}, u32[]{:S(2)}, u32[]{:S(2)}) collective-permute-start(bf16[2,96,768]{2,1,0:T(8,128)(2,1)S(1)} %constant_dynamic-update-slice_fusion), channel_id=1, source_target_pairs={{0,8},{4,12},{8,0},{12,4},{16,24},{20,28},{24,16},{28,20},{1,9},{5... | collective-permute-start | bytes 884744 | tf_op jit(solution)/shard_map/ppermute | solution.py:664
  124.3 15.6 %collective-permute-start.29 = (bf16[4,32,768]{2,1,0:T(8,128)(2,1)S(1)}, bf16[4,32,768]{2,1,0:T(8,128)(2,1)S(1)}, u32[]{:S(2)}, u32[]{:S(2)}) collective-permute-start(bf16[4,32,768]{2,1,0:T(8,128)(2,1)S(1)} %get-tuple-element.205), channel_id=1, source_target_pairs={{0,4},{4,0},{8,12},{12,8},{16,20},{20,16},{24,28},{28,24},{1,5},{5... | collective-permute-start | bytes 589832 | tf_op jit(solution)/shard_map/ppermute | solution.py:660
  125.3 5.1 %collective-permute-start.28 = (bf16[2,24,768]{2,1,0:T(8,128)(2,1)S(1)}, bf16[2,24,768]{2,1,0:T(8,128)(2,1)S(1)}, u32[]{:S(2)}, u32[]{:S(2)}) collective-permute-start(bf16[2,24,768]{2,1,0:T(8,128)(2,1)S(1)} %pad_maximum_fusion.1), channel_id=1, source_target_pairs={{0,2},{2,0},{1,3},{3,1},{4,6},{6,4},{5,7},{7,5},{8,10},{10,8},{9,1... | collective-permute-start | bytes 221192 | tf_op jit(solution)/shard_map/ppermute | solution.py:1580
  130.5 9.2 %collective-permute-start.31 = (bf16[1,96,768]{2,1,0:T(8,128)(2,1)S(1)}, bf16[1,96,768]{2,1,0:T(8,128)(2,1)S(1)}, u32[]{:S(2)}, u32[]{:S(2)}) collective-permute-start(bf16[1,96,768]{2,1,0:T(8,128)(2,1)S(1)} %maximum_bitcast_fusion), channel_id=1, source_target_pairs={{0,16},{4,20},{8,24},{12,28},{16,0},{20,4},{24,8},{28,12},{1,17},{... | collective-permute-start | bytes 442376 | tf_op jit(solution)/shard_map/ppermute | solution.py:668
  130.7 4.8 %collective-permute-start.32 = (bf16[2,24,576]{2,1,0:T(8,128)(2,1)S(1)}, bf16[2,24,576]{2,1,0:T(8,128)(2,1)S(1)}, u32[]{:S(2)}, u32[]{:S(2)}) collective-permute-start(bf16[2,24,576]{2,1,0:T(8,128)(2,1)S(1)} %pad_maximum_fusion.2), channel_id=1, source_target_pairs={{0,1},{1,0},{2,3},{3,2},{4,5},{5,4},{6,7},{7,6},{8,9},{9,8},{10,11... | collective-permute-start | bytes 165896 | tf_op jit(solution)/shard_map/ppermute | solution.py:643
  133.1 28.4 %collective-permute-start.39 = (bf16[4,96,768]{2,1,0:T(8,128)(2,1)S(1)}, bf16[4,96,768]{2,1,0:T(8,128)(2,1)S(1)}, u32[]{:S(2)}, u32[]{:S(2)}) collective-permute-start(bf16[4,96,768]{2,1,0:T(8,128)(2,1)S(1)} %constant_dynamic-update-slice_fusion.2.held), channel_id=1, source_target_pairs={{0,4},{4,0},{8,12},{12,8},{16,20},{20,16},{24,28},{28,24},{1,5},{5... | collective-permute-start | bytes 1769480 | tf_op jit(solution)/shard_map/ppermute | solution.py:660
  139.7 11.7 %collective-permute-start.34 = (bf16[2,96,768]{2,1,0:T(8,128)(2,1)S(1)}, bf16[2,96,768]{2,1,0:T(8,128)(2,1)S(1)}, u32[]{:S(2)}, u32[]{:S(2)}) collective-permute-start(bf16[2,96,768]{2,1,0:T(8,128)(2,1)S(1)} %constant_dynamic-update-slice_fusion.4), channel_id=1, source_target_pairs={{0,8},{4,12},{8,0},{12,4},{16,24},{20,28},{24,16},{28,20},{1,9},{5... | collective-permute-start | bytes 884744 | tf_op jit(solution)/shard_map/ppermute | solution.py:664
  139.9 4.3 %collective-permute-start.35 = (bf16[2,24,576]{2,1,0:T(8,128)(2,1)S(1)}, bf16[2,24,576]{2,1,0:T(8,128)(2,1)S(1)}, u32[]{:S(2)}, u32[]{:S(2)}) collective-permute-start(bf16[2,24,576]{2,1,0:T(8,128)(2,1)S(1)} %pad_maximum_fusion.3), channel_id=1, source_target_pairs={{0,2},{2,0},{1,3},{3,1},{4,6},{6,4},{5,7},{7,5},{8,10},{10,8},{9,1... | collective-permute-start | bytes 165896 | tf_op jit(solution)/shard_map/ppermute | solution.py:1593
  144.3 8.1 %collective-permute-start.37 = (bf16[1,96,768]{2,1,0:T(8,128)(2,1)S(1)}, bf16[1,96,768]{2,1,0:T(8,128)(2,1)S(1)}, u32[]{:S(2)}, u32[]{:S(2)}) collective-permute-start(bf16[1,96,768]{2,1,0:T(8,128)(2,1)S(1)} %maximum_bitcast_fusion.1), channel_id=1, source_target_pairs={{0,16},{4,20},{8,24},{12,28},{16,0},{20,4},{24,8},{28,12},{1,17},{... | collective-permute-start | bytes 442376 | tf_op jit(solution)/shard_map/ppermute | solution.py:668
  145.3 7.9 %collective-permute-start.40 = (bf16[2,32,768]{2,1,0:T(8,128)(2,1)S(1)}, bf16[2,32,768]{2,1,0:T(8,128)(2,1)S(1)}, u32[]{:S(2)}, u32[]{:S(2)}) collective-permute-start(bf16[2,32,768]{2,1,0:T(8,128)(2,1)S(1)} %get-tuple-element.269), channel_id=1, source_target_pairs={{0,8},{4,12},{8,0},{12,4},{16,24},{20,28},{24,16},{28,20},{1,9},{5... | collective-permute-start | bytes 294920 | tf_op jit(solution)/shard_map/ppermute | solution.py:664
  151.5 17.8 %collective-permute-start.36 = (bf16[4,96,768]{2,1,0:T(8,128)(2,1)S(1)}, bf16[4,96,768]{2,1,0:T(8,128)(2,1)S(1)}, u32[]{:S(2)}, u32[]{:S(2)}) collective-permute-start(bf16[4,96,768]{2,1,0:T(8,128)(2,1)S(1)} %constant_dynamic-update-slice_fusion.6.held), channel_id=1, source_target_pairs={{0,4},{4,0},{8,12},{12,8},{16,20},{20,16},{24,28},{28,24},{1,5},{5... | collective-permute-start | bytes 1769480 | tf_op jit(solution)/shard_map/ppermute | solution.py:660
  152.4 13.8 %collective-permute-start.38 = (bf16[2,96,768]{2,1,0:T(8,128)(2,1)S(1)}, bf16[2,96,768]{2,1,0:T(8,128)(2,1)S(1)}, u32[]{:S(2)}, u32[]{:S(2)}) collective-permute-start(bf16[2,96,768]{2,1,0:T(8,128)(2,1)S(1)} %constant_dynamic-update-slice_fusion.8), channel_id=1, source_target_pairs={{0,8},{4,12},{8,0},{12,4},{16,24},{20,28},{24,16},{28,20},{1,9},{5... | collective-permute-start | bytes 884744 | tf_op jit(solution)/shard_map/ppermute | solution.py:664
  153.3 5.2 %collective-permute-start.41 = (bf16[1,32,768]{2,1,0:T(8,128)(2,1)S(1)}, bf16[1,32,768]{2,1,0:T(8,128)(2,1)S(1)}, u32[]{:S(2)}, u32[]{:S(2)}) collective-permute-start(bf16[1,32,768]{2,1,0:T(8,128)(2,1)S(1)} %get-tuple-element.280), channel_id=1, source_target_pairs={{0,16},{4,20},{8,24},{12,28},{16,0},{20,4},{24,8},{28,12},{1,17},{... | collective-permute-start | bytes 147464 | tf_op jit(solution)/shard_map/ppermute | solution.py:668
  158.5 5.2 %collective-permute-start.42 = (bf16[1,32,768]{2,1,0:T(8,128)(2,1)S(1)}, bf16[1,32,768]{2,1,0:T(8,128)(2,1)S(1)}, u32[]{:S(2)}, u32[]{:S(2)}) collective-permute-start(bf16[1,32,768]{2,1,0:T(8,128)(2,1)S(1)} %add_convert_fusion.11), channel_id=1, source_target_pairs={{0,16},{4,20},{8,24},{12,28},{16,0},{20,4},{24,8},{28,12},{1,17},{... | collective-permute-start | bytes 147464 | tf_op jit(solution)/shard_map/ppermute | solution.py:668
  163.7 5.2 %collective-permute-start.43 = (bf16[2,32,768]{2,1,0:T(8,128)(2,1)S(1)}, bf16[2,32,768]{2,1,0:T(8,128)(2,1)S(1)}, u32[]{:S(2)}, u32[]{:S(2)}) collective-permute-start(bf16[2,32,768]{2,1,0:T(8,128)(2,1)S(1)} %constant_dynamic-update-slice_fusion.10), channel_id=1, source_target_pairs={{0,8},{4,12},{8,0},{12,4},{16,24},{20,28},{24,16},{28,20},{1,9},{5... | collective-permute-start | bytes 294920 | tf_op jit(solution)/shard_map/ppermute | solution.py:664
  166.3 12.5 %collective-permute-start.45 = (bf16[4,96,768]{2,1,0:T(8,128)(2,1)S(1)}, bf16[4,96,768]{2,1,0:T(8,128)(2,1)S(1)}, u32[]{:S(2)}, u32[]{:S(2)}) collective-permute-start(bf16[4,96,768]{2,1,0:T(8,128)(2,1)S(1)} %constant_dynamic-update-slice_fusion.12.held), channel_id=1, source_target_pairs={{0,4},{4,0},{8,12},{12,8},{16,20},{20,16},{24,28},{28,24},{1,5},{5... | collective-permute-start | bytes 1769480 | tf_op jit(solution)/shard_map/ppermute | solution.py:660
  168.9 12.0 %collective-permute-start.44 = (bf16[4,32,768]{2,1,0:T(8,128)(2,1)S(1)}, bf16[4,32,768]{2,1,0:T(8,128)(2,1)S(1)}, u32[]{:S(2)}, u32[]{:S(2)}) collective-permute-start(bf16[4,32,768]{2,1,0:T(8,128)(2,1)S(1)} %constant_dynamic-update-slice_fusion.14.held), channel_id=1, source_target_pairs={{0,4},{4,0},{8,12},{12,8},{16,20},{20,16},{24,28},{28,24},{1,5},{5... | collective-permute-start | bytes 589832 | tf_op jit(solution)/shard_map/ppermute | solution.py:660
  (27 other events, 216.0 us)

commit v3 on v2

--- a/solution.py
+++ b/solution.py
@@ -1057,7 +1057,7 @@
         normed_ref[rows] = normed
         hidden, slope = gelu_parts(nn(normed, w_up_ref[...]) + bias)
         hidden_ref[rows] = hidden.astype(BF)
-        slope_ref[rows] = slope
+        slope_ref[rows] = slope.astype(BF)
     grad[...] = tn(hidden_ref[...], cot_ref[...])
     share_out(lambda g: grad[BAND * g : BAND * (g + 1)].astype(BF), x, X_PAIRS, kept_ref, sent_ref)
 
@@ -1073,7 +1073,7 @@
     d_bias = jnp.zeros((1, FF_OWN), F32)
     for half in range(2):
         rows = slice(HALF * half, HALF * (half + 1))
-        d_pre = (nt(cot_ref[rows], w_down_ref[...]) * slope_ref[rows]).astype(BF)
+        d_pre = (nt(cot_ref[rows], w_down_ref[...]) * slope_ref[rows].astype(F32)).astype(BF)
         d_pre_ref[rows] = d_pre
         d_bias = d_bias + jnp.sum(d_pre.astype(F32), axis=0, keepdims=True)
     d_bias_ref[...] = d_bias
@@ -1487,7 +1487,7 @@
         feed_rows_kernel,
         [*att_blocks, *cot_blocks, cot_global, global_tokens, late_gain, shift_two,
          bias_up, super_rows, w_out, w_up],
-        [((4, BAND, D), BF), ((4, BAND, D), BF), ((ALL, D), BF), ((ALL, FF_OWN), F32), ((ALL, D), BF)],
+        [((4, BAND, D), BF), ((4, BAND, D), BF), ((ALL, D), BF), ((ALL, FF_OWN), BF), ((ALL, D), BF)],
         [((ROWS, D), F32), weights_shape, ((D, FF_OWN), BF), ((ALL, FF_OWN), BF), ((D, D), F32),
          pltpu.SemaphoreType.DMA((3,))],
         apart=3,

time: 182 us -> 182 us (level)
    unnamed x66 -> x68, local copies, waits for them, and re-layouts: 3 us -> 4.17 us
  transfers between devices with their start and end apart: 46 -> 46, of which waited for: 20 -> 20; matrix products, arithmetic and copies ran while one was open for 1% -> 1% of each run, Pallas kernels for 41% -> 40%
where the time goes in v3:
time: 182 us; the launch traced here: 181 us
  Pallas kernels  73.3 us (40%)
  waiting for transfers between devices  54.4 us (30%)
  starting transfers between devices  46.6 us (26%)
  local copies, waits for them, and re-layouts  4.74 us (3%)
    pallas_call x13, Pallas kernels, call(): pl.pallas_call(kernel, out_shape=[jax.ShapeDtypeStruct(shape, kind) for s...  73.3 us
    ppermute x8, waiting for transfers between devices, swap_near(): return lax.ppermute(sent, 'grp', Z_NEAR)  16.8 us
    ppermute x5, waiting for transfers between devices, reach_seq(): lax.ppermute(block, 'seq', Y_SWAP)  14.4 us
    ppermute x8, starting transfers between devices, swap_far(): return lax.ppermute(sent, 'grp', Z_FAR)  13.1 us
    ppermute x8, starting transfers between devices, swap_near(): return lax.ppermute(sent, 'grp', Z_NEAR)  12 us
    ppermute x8, waiting for transfers between devices, swap_far(): return lax.ppermute(sent, 'grp', Z_FAR)  10.5 us
    ppermute x8, starting transfers between devices, swap_x(): return lax.ppermute(sent, 'grp', X_SWAP)  8.36 us
    ppermute x8, waiting for transfers between devices, swap_x(): return lax.ppermute(sent, 'grp', X_SWAP)  7.42 us
  transfers between devices with their start and end apart: 46, of which 20 were waited for; matrix products, arithmetic and copies ran while one was open for 1% of the time, Pallas kernels for 40%

profile of v3, /device:TPU:0, one launch (start us, length us, event | category | flops | bytes accessed | tf_op | source)
XLA Modules:
  0.0 181.4 jit_solution(336344625389654633)
XLA Ops:
  0.7 3.0 %collective-permute-start.1 = (bf16[128,768]{1,0:T(8,128)(2,1)}, bf16[128,768]{1,0:T(8,128)(2,1)S(1)}, u32[]{:S(2)}, u32[]{:S(2)}) collective-permute-start(bf16[128,768]{1,0:T(8,128)(2,1)} %tok_a.1), channel_id=1, source_target_pairs={{0,2},{2,0},{1,3},{3,1},{4,6},{6,4},{5,7},{7,5},{8,10},{10,8},{9,1... | collective-permute-start | bytes 589832 | tf_op jit(solution)/shard_map/ppermute | solution.py:633
  3.7 1.4 shard_map.357.int_a
  5.1 3.9 %collective-permute-done.2.int_c = s32[16,128]{1,0:T(8,128)S(1)} collective-permute-done((s32[16,128]{1,0:T(8,128)}, s32[16,128]{1,0:T(8,128)S(1)}, u32[]{:S(2)}, u32[]{:S(2)}) %collective-permute-start.2) | collective-permute-done | bytes 8224 | tf_op jit(solution)/shard_map/ppermute | solution.py:633
  10.7 1.7 collective-permute-start.6
  13.3 17.7 %shard_map.358 = (bf16[288,384]{1,0:T(8,128)(2,1)}, f32[3,64,640]{2,1,0:T(8,128)}, f32[3,64,64]{2,1,0:T(8,128)}, f32[16,512]{1,0:T(8,128)}, bf16[512,256]{1,0:T(...) custom-call(bf16[128,768]{1,0:T(8,128)(2,1)} %tok_a.1, ...), custom_call_target="tpu_custom_call" | custom-call | flops 60000002048 | tf_op jit(solution)/shard_map/pallas_call | solution.py:1413
  31.0 1.2 collective-permute-start.8
  32.2 6.2 %collective-permute-done.8.att_c = bf16[288,384]{1,0:T(8,128)(2,1)S(1)} collective-permute-done((bf16[288,384]{1,0:T(8,128)(2,1)}, bf16[288,384]{1,0:T(8,128)(2,1)S(1)}, u32[]{:S(2)}, u32[]{:S(2)}) %collective-permute-start.8) | collective-permute-done | bytes 221216 | tf_op jit(solution)/shard_map/ppermute | solution.py:633
  40.9 9.8 %shard_map.359 = (bf16[128,768]{1,0:T(8,128)(2,1)}, bf16[176,768]{1,0:T(8,128)(2,1)S(1)}) custom-call(bf16[288,384]{1,0:T(8,128)(2,1)S(1)} %copy-done.2, bf16[288,384]{1,0:T(8,128)(2,1)S(1)} %collective-permute-done.7.att_b, bf16[288,384]{1,0:T(8,128)(2,1)S(1)} %collective-permute-done.8.att_c, bf16[288,384]{1,0:T(8,128)(2,1)S(1)} %collective-permute-done.9.att_d, ...), custom_call_target="tpu_custom_call" | custom-call | flops 60000002048 | tf_op jit(solution)/shard_map/pallas_call | solution.py:1413
  50.6 1.6 collective-permute-start.13
  52.3 6.4 %shard_map.360 = (bf16[4,96,768]{2,1,0:T(8,128)(2,1)S(1)}, bf16[4,96,768]{2,1,0:T(8,128)(2,1)S(1)}, bf16[576,768]{1,0:T(8,128)(2,1)S(1)}, bf16[576,768]{1,0:T(8,128)(2,1)}, bf16[576,768]{1,0:T(8,128)(2,1)}) custom-call(bf16[288,384]{1,0:T(8,128)(2,1)S(1)} %copy-done.2, bf16[288,384]{1,0:T(8,128)(2,1)S(1)} %collective-permute-done.7.att_b, ...), custom_call_target="tpu_custom_call" | custom-call | flops 60000002048 | tf_op jit(solution)/shard_map/pallas_call | solution.py:1413
  58.7 1.6 collective-permute-start.15
  60.5 1.2 copy-done.15
  61.6 1.2 copy-done.16
  62.8 3.2 %shard_map.361 = (bf16[4,96,768]{2,1,0:T(8,128)(2,1)S(1)}, bf16[4,96,768]{2,1,0:T(8,128)(2,1)S(1)}, f32[1,768]{1,0:T(1,128)S(1)}) custom-call(bf16[576,768]{1,0:T(8,128)(2,1)S(1)} %get-tuple-element.156.normed_ref, bf16[576,768]{1,0:T(8,128)(2,1)S(1)} %copy-done.15, bf16[576,768]{1,0:T(8,128)(2,1)S(1)} %copy-done.16, bf16[3072,768]{1,0:T(8,128)(2,1)} %w_down_any.3), custom_call_target="tpu_custom_call" | custom-call | flops 60000002048 | tf_op jit(solution)/shard_map/pallas_call | solution.py:1413
  66.7 15.0 %shard_map.362 = (bf16[576,768]{1,0:T(8,128)(2,1)S(1)}, bf16[576,640]{1,0:T(8,128)(2,1)S(1)}, f32[8,768]{1,0:T(8,128)S(1)}, bf16[64,768]{1,0:T(8,128)(2,1)}) custom-call(bf16[176,768]{1,0:T(8,128)(2,1)S(1)} %get-tuple-element.147.back_a, bf16[176,768]{1,0:T(8,128)(2,1)S(1)} %collective-permute-done.10.back_b, ...), custom_call_target="tpu_custom_call" | custom-call | flops 60000002048 | tf_op jit(solution)/shard_map/pallas_call | solution.py:1413
  81.7 1.3 collective-permute-start.20
  83.2 1.6 collective-permute-start.16
  84.9 1.5 shard_map.363
  87.4 1.6 collective-permute-start.19
  89.0 4.1 %collective-permute-done.16 = bf16[2,96,768]{2,1,0:T(8,128)(2,1)S(1)} collective-permute-done((bf16[2,96,768]{2,1,0:T(8,128)(2,1)S(1)}, bf16[2,96,768]{2,1,0:T(8,128)(2,1)S(1)}, u32[]{:S(2)}, u32[]{:S(2)}) %collective-permute-start.16) | collective-permute-done | bytes 294944 | tf_op jit(solution)/shard_map/ppermute | solution.py:664
  93.2 2.6 %collective-permute-start.18 = (bf16[1,96,768]{2,1,0:T(8,128)(2,1)S(1)}, bf16[1,96,768]{2,1,0:T(8,128)(2,1)S(1)}, u32[]{:S(2)}, u32[]{:S(2)}) collective-permute-start(bf16[1,96,768]{2,1,0:T(8,128)(2,1)S(1)} %get-tuple-element.267), channel_id=1, source_target_pairs={{0,16},{4,20},{8,24},{12,28},{16,0},{20,4},{24,8},{28,12},{1,17},{... | collective-permute-start | bytes 442376 | tf_op jit(solution)/shard_map/ppermute | solution.py:668
  95.8 4.3 %collective-permute-done.20.dqkv_c = bf16[576,640]{1,0:T(8,128)(2,1)S(1)} collective-permute-done((bf16[576,640]{1,0:T(8,128)(2,1)S(1)}, bf16[576,640]{1,0:T(8,128)(2,1)S(1)}, u32[]{:S(2)}, u32[]{:S(2)}) %collective-permute-start.20) | collective-permute-done | bytes 737312 | tf_op jit(solution)/shard_map/ppermute | solution.py:633
  100.2 2.0 %collective-permute-done.19 = bf16[2,96,768]{2,1,0:T(8,128)(2,1)S(1)} collective-permute-done((bf16[2,96,768]{2,1,0:T(8,128)(2,1)S(1)}, bf16[2,96,768]{2,1,0:T(8,128)(2,1)S(1)}, u32[]{:S(2)}, u32[]{:S(2)}) %collective-permute-start.19) | collective-permute-done | bytes 294944 | tf_op jit(solution)/shard_map/ppermute | solution.py:664
  102.3 2.5 %collective-permute-start.26 = (bf16[1,96,768]{2,1,0:T(8,128)(2,1)S(1)}, bf16[1,96,768]{2,1,0:T(8,128)(2,1)S(1)}, u32[]{:S(2)}, u32[]{:S(2)}) collective-permute-start(bf16[1,96,768]{2,1,0:T(8,128)(2,1)S(1)} %add_convert_fusion.9), channel_id=1, source_target_pairs={{0,16},{4,20},{8,24},{12,28},{16,0},{20,4},{24,8},{28,12},{1,17},{... | collective-permute-start | bytes 442376 | tf_op jit(solution)/shard_map/ppermute | solution.py:668
  105.6 2.5 %collective-permute-start.27 = (bf16[2,96,768]{2,1,0:T(8,128)(2,1)S(1)}, bf16[2,96,768]{2,1,0:T(8,128)(2,1)S(1)}, u32[]{:S(2)}, u32[]{:S(2)}) collective-permute-start(bf16[2,96,768]{2,1,0:T(8,128)(2,1)S(1)} %get-tuple-element.257), channel_id=1, source_target_pairs={{0,8},{4,12},{8,0},{12,4},{16,24},{20,28},{24,16},{28,20},{1,9},{5... | collective-permute-start | bytes 884744 | tf_op jit(solution)/shard_map/ppermute | solution.py:664
  108.1 8.8 %shard_map.364 = (f32[64,768]{1,0:T(8,128)}, bf16[4,32,768]{2,1,0:T(8,128)(2,1)S(1)}, bf16[4,32,768]{2,1,0:T(8,128)(2,1)S(1)}, f32[128,768]{1,0:T(8,128)S(1)}, bf16[512,768]{1,0:T(8,128)(2,1)}) custom-call(bf16[576,640]{1,0:T(8,128)(2,1)S(1)} %get-tuple-element.168.d_qkv_ref.dqkv_a, bf16[576,640]{1,0:T(8,128)(2,1)S(1)} %collective-permute-done.22.dqkv_b, ...), custom_call_target="tpu_custom_call" | custom-call | flops 60000002048 | tf_op jit(solution)/shard_map/pallas_call | solution.py:1413
  116.9 1.5 collective-permute-done.21
  119.0 2.4 %collective-permute-start.30 = (bf16[1,96,768]{2,1,0:T(8,128)(2,1)S(1)}, bf16[1,96,768]{2,1,0:T(8,128)(2,1)S(1)}, u32[]{:S(2)}, u32[]{:S(2)}) collective-permute-start(bf16[1,96,768]{2,1,0:T(8,128)(2,1)S(1)} %get-tuple-element.263), channel_id=1, source_target_pairs={{0,16},{4,20},{8,24},{12,28},{16,0},{20,4},{24,8},{28,12},{1,17},{... | collective-permute-start | bytes 442376 | tf_op jit(solution)/shard_map/ppermute | solution.py:668
  121.4 2.5 %collective-permute-start.33 = (bf16[2,96,768]{2,1,0:T(8,128)(2,1)S(1)}, bf16[2,96,768]{2,1,0:T(8,128)(2,1)S(1)}, u32[]{:S(2)}, u32[]{:S(2)}) collective-permute-start(bf16[2,96,768]{2,1,0:T(8,128)(2,1)S(1)} %constant_dynamic-update-slice_fusion), channel_id=1, source_target_pairs={{0,8},{4,12},{8,0},{12,4},{16,24},{20,28},{24,16},{28,20},{1,9},{5... | collective-permute-start | bytes 884744 | tf_op jit(solution)/shard_map/ppermute | solution.py:664
  124.7 1.6 collective-permute-start.28
  126.3 3.5 %shard_map.365 = f32[128,768]{1,0:T(8,128)} custom-call(f32[128,768]{1,0:T(8,128)S(1)} %get-tuple-element.201.d_own_ref, bf16[512,768]{1,0:T(8,128)(2,1)S(1)} %copy-done.18, f32[16,512]{1,0:T(8,128)S(1)} %copy-done.22, bf16[768,768]{1,0:T(8,128)(2,1)S(1)} %copy-done.1), custom_call_target="tpu_custom_call" | custom-call | flops 60000002048 | tf_op jit(solution)/shard_map/pallas_call | solution.py:1413
  130.2 2.5 %collective-permute-done.33 = bf16[2,96,768]{2,1,0:T(8,128)(2,1)S(1)} collective-permute-done((bf16[2,96,768]{2,1,0:T(8,128)(2,1)S(1)}, bf16[2,96,768]{2,1,0:T(8,128)(2,1)S(1)}, u32[]{:S(2)}, u32[]{:S(2)}) %collective-permute-start.33) | collective-permute-done | bytes 294944 | tf_op jit(solution)/shard_map/ppermute | solution.py:664
  132.8 2.2 %collective-permute-start.39 = (bf16[4,96,768]{2,1,0:T(8,128)(2,1)S(1)}, bf16[4,96,768]{2,1,0:T(8,128)(2,1)S(1)}, u32[]{:S(2)}, u32[]{:S(2)}) collective-permute-start(bf16[4,96,768]{2,1,0:T(8,128)(2,1)S(1)} %constant_dynamic-update-slice_fusion.2.held), channel_id=1, source_target_pairs={{0,4},{4,0},{8,12},{12,8},{16,20},{20,16},{24,28},{28,24},{1,5},{5... | collective-permute-start | bytes 1769480 | tf_op jit(solution)/shard_map/ppermute | solution.py:660
  134.9 4.2 %collective-permute-done.31 = bf16[1,96,768]{2,1,0:T(8,128)(2,1)S(1)} collective-permute-done((bf16[1,96,768]{2,1,0:T(8,128)(2,1)S(1)}, bf16[1,96,768]{2,1,0:T(8,128)(2,1)S(1)}, u32[]{:S(2)}, u32[]{:S(2)}) %collective-permute-start.31) | collective-permute-done | bytes 147488 | tf_op jit(solution)/shard_map/ppermute | solution.py:668
  140.1 3.6 %collective-permute-done.35 = bf16[2,24,576]{2,1,0:T(8,128)(2,1)S(1)} collective-permute-done((bf16[2,24,576]{2,1,0:T(8,128)(2,1)S(1)}, bf16[2,24,576]{2,1,0:T(8,128)(2,1)S(1)}, u32[]{:S(2)}, u32[]{:S(2)}) %collective-permute-start.35) | collective-permute-done | bytes 55328 | tf_op jit(solution)/shard_map/ppermute | solution.py:1593
  144.7 1.2 collective-permute-start.40
  145.9 4.9 %collective-permute-done.34 = bf16[2,96,768]{2,1,0:T(8,128)(2,1)S(1)} collective-permute-done((bf16[2,96,768]{2,1,0:T(8,128)(2,1)S(1)}, bf16[2,96,768]{2,1,0:T(8,128)(2,1)S(1)}, u32[]{:S(2)}, u32[]{:S(2)}) %collective-permute-start.34) | collective-permute-done | bytes 294944 | tf_op jit(solution)/shard_map/ppermute | solution.py:664
  153.0 1.5 collective-permute-start.41
  154.6 3.6 %collective-permute-done.41 = bf16[1,32,768]{2,1,0:T(8,128)(2,1)S(1)} collective-permute-done((bf16[1,32,768]{2,1,0:T(8,128)(2,1)S(1)}, bf16[1,32,768]{2,1,0:T(8,128)(2,1)S(1)}, u32[]{:S(2)}, u32[]{:S(2)}) %collective-permute-start.41) | collective-permute-done | bytes 49184 | tf_op jit(solution)/shard_map/ppermute | solution.py:668
  158.2 2.5 %collective-permute-start.42 = (bf16[1,32,768]{2,1,0:T(8,128)(2,1)S(1)}, bf16[1,32,768]{2,1,0:T(8,128)(2,1)S(1)}, u32[]{:S(2)}, u32[]{:S(2)}) collective-permute-start(bf16[1,32,768]{2,1,0:T(8,128)(2,1)S(1)} %add_convert_fusion.11), channel_id=1, source_target_pairs={{0,16},{4,20},{8,24},{12,28},{16,0},{20,4},{24,8},{28,12},{1,17},{... | collective-permute-start | bytes 147464 | tf_op jit(solution)/shard_map/ppermute | solution.py:668
  160.7 1.6 shard_map.366
  162.3 1.1 collective-permute-done.42
  163.4 2.1 %collective-permute-start.43 = (bf16[2,32,768]{2,1,0:T(8,128)(2,1)S(1)}, bf16[2,32,768]{2,1,0:T(8,128)(2,1)S(1)}, u32[]{:S(2)}, u32[]{:S(2)}) collective-permute-start(bf16[2,32,768]{2,1,0:T(8,128)(2,1)S(1)} %constant_dynamic-update-slice_fusion.10), channel_id=1, source_target_pairs={{0,8},{4,12},{8,0},{12,4},{16,24},{20,28},{24,16},{28,20},{1,9},{5... | collective-permute-start | bytes 294920 | tf_op jit(solution)/shard_map/ppermute | solution.py:664
  166.2 1.9 %collective-permute-done.43 = bf16[2,32,768]{2,1,0:T(8,128)(2,1)S(1)} collective-permute-done((bf16[2,32,768]{2,1,0:T(8,128)(2,1)S(1)}, bf16[2,32,768]{2,1,0:T(8,128)(2,1)S(1)}, u32[]{:S(2)}, u32[]{:S(2)}) %collective-permute-start.43) | collective-permute-done | bytes 98336 | tf_op jit(solution)/shard_map/ppermute | solution.py:664
  168.1 1.3 collective-permute-start.44
  169.4 1.6 shard_map.367
  170.9 7.3 %collective-permute-done.45.came = bf16[4,96,768]{2,1,0:T(8,128)(2,1)S(1)} collective-permute-done((bf16[4,96,768]{2,1,0:T(8,128)(2,1)S(1)}, bf16[4,96,768]{2,1,0:T(8,128)(2,1)S(1)}, u32[]{:S(2)}, u32[]{:S(2)}) %collective-permute-start.45) | collective-permute-done | bytes 589856 | tf_op jit(solution)/shard_map/ppermute | solution.py:660
  178.3 2.0 %shard_map.368 = (f32[192,768]{1,0:T(8,128)}, f32[192,768]{1,0:T(8,128)}, f32[192,768]{1,0:T(8,128)}, f32[192,768]{1,0:T(8,128)}) custom-call(bf16[4,96,768]{2,1,0:T(8,128)(2,1)S(1)} %constant_dynamic-update-slice_fusion.12.held, bf16[4,96,768]{2,1,0:T(8,128)(2,1)S(1)} %collective-permute-done.45.came), custom_call_target="tpu_custom_call" | custom-call | flops 60000002048 | tf_op jit(solution)/shard_map/pallas_call | solution.py:1413
  (171 shorter events, 15.6 us)
Async XLA Ops:
  0.7 9.5 %collective-permute-start.1 = (bf16[128,768]{1,0:T(8,128)(2,1)}, bf16[128,768]{1,0:T(8,128)(2,1)S(1)}, u32[]{:S(2)}, u32[]{:S(2)}) collective-permute-start(bf16[128,768]{1,0:T(8,128)(2,1)} %tok_a.1), channel_id=1, source_target_pairs={{0,2},{2,0},{1,3},{3,1},{4,6},{6,4},{5,7},{7,5},{8,10},{10,8},{9,1... | collective-permute-start | bytes 589832 | tf_op jit(solution)/shard_map/ppermute | solution.py:633
  5.0 3.9 %collective-permute-start.2 = (s32[16,128]{1,0:T(8,128)}, s32[16,128]{1,0:T(8,128)S(1)}, u32[]{:S(2)}, u32[]{:S(2)}) collective-permute-start(s32[16,128]{1,0:T(8,128)} %shard_map.357.int_a), channel_id=1, source_target_pairs={{0,2},{2,0},{1,3},{3,1},{4,6},{6,4},{5,7},{7,5},{8,10},{10,8},{9,1... | collective-permute-start | bytes 24584 | tf_op jit(solution)/shard_map/ppermute | solution.py:633
  9.0 1.2 collective-permute-start.3
  9.0 3.5 %collective-permute-start = (bf16[128,768]{1,0:T(8,128)(2,1)S(1)}, bf16[128,768]{1,0:T(8,128)(2,1)S(1)}, u32[]{:S(2)}, u32[]{:S(2)}) collective-permute-start(bf16[128,768]{1,0:T(8,128)(2,1)S(1)} %copy-done.23), channel_id=1, source_target_pairs={{0,1},{1,0},{2,3},{3,2},{4,5},{5,4},{6,7},{7,6},{8,9},{9,8},{10,11... | collective-permute-start | bytes 589832 | tf_op jit(solution)/shard_map/ppermute | solution.py:633
  10.2 2.3 %collective-permute-start.4 = (bf16[128,768]{1,0:T(8,128)(2,1)S(1)}, bf16[128,768]{1,0:T(8,128)(2,1)S(1)}, u32[]{:S(2)}, u32[]{:S(2)}) collective-permute-start(bf16[128,768]{1,0:T(8,128)(2,1)S(1)} %collective-permute-done.1.tok_c), channel_id=1, source_target_pairs={{0,1},{1,0},{2,3},{3,2},{4,5},{5,4},{6,7},{7,6},{8,9},{9,8},{10,11... | collective-permute-start | bytes 589832 | tf_op jit(solution)/shard_map/ppermute | solution.py:1441
  10.3 2.1 %collective-permute-start.5 = (s32[16,128]{1,0:T(8,128)}, s32[16,128]{1,0:T(8,128)S(1)}, u32[]{:S(2)}, u32[]{:S(2)}) collective-permute-start(s32[16,128]{1,0:T(8,128)} %shard_map.357.int_a), channel_id=1, source_target_pairs={{0,1},{1,0},{2,3},{3,2},{4,5},{5,4},{6,7},{7,6},{8,9},{9,8},{10,11... | collective-permute-start | bytes 24584 | tf_op jit(solution)/shard_map/ppermute | solution.py:633
  10.7 20.2 %collective-permute-start.6 = (bf16[128,768]{1,0:T(8,128)(2,1)S(1)}, bf16[128,768]{1,0:T(8,128)(2,1)S(1)}, u32[]{:S(2)}, u32[]{:S(2)}) collective-permute-start(bf16[128,768]{1,0:T(8,128)(2,1)S(1)} %copy-done.4), channel_id=1, source_target_pairs={{0,2},{2,0},{1,3},{3,1},{4,6},{6,4},{5,7},{7,5},{8,10},{10,8},{9,1... | collective-permute-start | bytes 589832 | tf_op jit(solution)/shard_map/ppermute | solution.py:1440
  13.2 26.7 %copy-start.10 = (f32[768]{0:T(1024)S(1)}, f32[768]{0:T(1024)}, u32[]{:S(2)}) copy-start(f32[768]{0:T(1024)} %bias_down_ref.1) | copy-start | bytes 9220
  13.3 26.7 %copy-start.11 = (f32[768]{0:T(1024)S(1)}, f32[768]{0:T(1024)}, u32[]{:S(2)}) copy-start(f32[768]{0:T(1024)} %gain_ref.5) | copy-start | bytes 9220
  31.0 7.4 %collective-permute-start.8 = (bf16[288,384]{1,0:T(8,128)(2,1)}, bf16[288,384]{1,0:T(8,128)(2,1)S(1)}, u32[]{:S(2)}, u32[]{:S(2)}) collective-permute-start(bf16[288,384]{1,0:T(8,128)(2,1)} %get-tuple-element.142.att_a.attn_ref), channel_id=1, source_target_pairs={{0,2},{2,0},{1,3},{3,1},{4,6},{6,4},{5,7},{7,5},{8,10},{10,8},{9,1... | collective-permute-start | bytes 663560 | tf_op jit(solution)/shard_map/ppermute | solution.py:633
  32.2 6.7 %collective-permute-start.7 = (bf16[288,384]{1,0:T(8,128)(2,1)}, bf16[288,384]{1,0:T(8,128)(2,1)S(1)}, u32[]{:S(2)}, u32[]{:S(2)}) collective-permute-start(bf16[288,384]{1,0:T(8,128)(2,1)} %get-tuple-element.142.att_a.attn_ref), channel_id=1, source_target_pairs={{0,1},{1,0},{2,3},{3,2},{4,5},{5,4},{6,7},{7,6},{8,9},{9,8},{10,11... | collective-permute-start | bytes 663560 | tf_op jit(solution)/shard_map/ppermute | solution.py:633
  38.4 1.5 collective-permute-start.9
  38.4 13.9 %collective-permute-start.11 = (bf16[128,768]{1,0:T(8,128)(2,1)S(1)}, bf16[128,768]{1,0:T(8,128)(2,1)S(1)}, u32[]{:S(2)}, u32[]{:S(2)}) collective-permute-start(bf16[128,768]{1,0:T(8,128)(2,1)S(1)} %copy-done.4), channel_id=1, source_target_pairs={{0,1},{1,0},{2,3},{3,2},{4,5},{5,4},{6,7},{7,6},{8,9},{9,8},{10,11... | collective-permute-start | bytes 589832 | tf_op jit(solution)/shard_map/ppermute | solution.py:1471
  38.9 13.4 %collective-permute-start.12 = (bf16[128,768]{1,0:T(8,128)(2,1)S(1)}, bf16[128,768]{1,0:T(8,128)(2,1)S(1)}, u32[]{:S(2)}, u32[]{:S(2)}) collective-permute-start(bf16[128,768]{1,0:T(8,128)(2,1)S(1)} %collective-permute-done.6.cot_c), channel_id=1, source_target_pairs={{0,1},{1,0},{2,3},{3,2},{4,5},{5,4},{6,7},{7,6},{8,9},{9,8},{10,11... | collective-permute-start | bytes 589832 | tf_op jit(solution)/shard_map/ppermute | solution.py:1472
  50.6 9.6 %collective-permute-start.13 = (bf16[176,768]{1,0:T(8,128)(2,1)S(1)}, bf16[176,768]{1,0:T(8,128)(2,1)S(1)}, u32[]{:S(2)}, u32[]{:S(2)}) collective-permute-start(bf16[176,768]{1,0:T(8,128)(2,1)S(1)} %get-tuple-element.147.back_a), channel_id=1, source_target_pairs={{0,2},{2,0},{1,3},{3,1},{4,6},{6,4},{5,7},{7,5},{8,10},{10,8},{9,1... | collective-permute-start | bytes 811016 | tf_op jit(solution)/shard_map/ppermute | solution.py:633
  52.3 14.4 %collective-permute-start.10 = (bf16[176,768]{1,0:T(8,128)(2,1)S(1)}, bf16[176,768]{1,0:T(8,128)(2,1)S(1)}, u32[]{:S(2)}, u32[]{:S(2)}) collective-permute-start(bf16[176,768]{1,0:T(8,128)(2,1)S(1)} %get-tuple-element.147.back_a), channel_id=1, source_target_pairs={{0,1},{1,0},{2,3},{3,2},{4,5},{5,4},{6,7},{7,6},{8,9},{9,8},{10,11... | collective-permute-start | bytes 811016 | tf_op jit(solution)/shard_map/ppermute | solution.py:633
  58.7 24.3 %collective-permute-start.15 = (bf16[4,96,768]{2,1,0:T(8,128)(2,1)S(1)}, bf16[4,96,768]{2,1,0:T(8,128)(2,1)S(1)}, u32[]{:S(2)}, u32[]{:S(2)}) collective-permute-start(bf16[4,96,768]{2,1,0:T(8,128)(2,1)S(1)} %get-tuple-element.167), channel_id=1, source_target_pairs={{0,4},{4,0},{8,12},{12,8},{16,20},{20,16},{24,28},{28,24},{1,5},{5... | collective-permute-start | bytes 1769480 | tf_op jit(solution)/shard_map/ppermute | solution.py:660
  60.3 6.4 %collective-permute-start.14 = (bf16[176,768]{1,0:T(8,128)(2,1)S(1)}, bf16[176,768]{1,0:T(8,128)(2,1)S(1)}, u32[]{:S(2)}, u32[]{:S(2)}) collective-permute-start(bf16[176,768]{1,0:T(8,128)(2,1)S(1)} %collective-permute-done.13.back_c), channel_id=1, source_target_pairs={{0,1},{1,0},{2,3},{3,2},{4,5},{5,4},{6,7},{7,6},{8,9},{9,8},{10,11... | collective-permute-start | bytes 811016 | tf_op jit(solution)/shard_map/ppermute | solution.py:1497
  66.0 21.1 %collective-permute-start.17 = (bf16[4,96,768]{2,1,0:T(8,128)(2,1)S(1)}, bf16[4,96,768]{2,1,0:T(8,128)(2,1)S(1)}, u32[]{:S(2)}, u32[]{:S(2)}) collective-permute-start(bf16[4,96,768]{2,1,0:T(8,128)(2,1)S(1)} %get-tuple-element.172), channel_id=1, source_target_pairs={{0,4},{4,0},{8,12},{12,8},{16,20},{20,16},{24,28},{28,24},{1,5},{5... | collective-permute-start | bytes 1769480 | tf_op jit(solution)/shard_map/ppermute | solution.py:660
  81.7 18.5 %collective-permute-start.20 = (bf16[576,640]{1,0:T(8,128)(2,1)S(1)}, bf16[576,640]{1,0:T(8,128)(2,1)S(1)}, u32[]{:S(2)}, u32[]{:S(2)}) collective-permute-start(bf16[576,640]{1,0:T(8,128)(2,1)S(1)} %get-tuple-element.168.d_qkv_ref.dqkv_a), channel_id=1, source_target_pairs={{0,2},{2,0},{1,3},{3,1},{4,6},{6,4},{5,7},{7,5},{8,10},{10,8},{9,1... | collective-permute-start | bytes 2211848 | tf_op jit(solution)/shard_map/ppermute | solution.py:633
  83.0 25.1 %collective-permute-start.22 = (bf16[576,640]{1,0:T(8,128)(2,1)S(1)}, bf16[576,640]{1,0:T(8,128)(2,1)S(1)}, u32[]{:S(2)}, u32[]{:S(2)}) collective-permute-start(bf16[576,640]{1,0:T(8,128)(2,1)S(1)} %get-tuple-element.168.d_qkv_ref.dqkv_a), channel_id=1, source_target_pairs={{0,1},{1,0},{2,3},{3,2},{4,5},{5,4},{6,7},{7,6},{8,9},{9,8},{10,11... | collective-permute-start | bytes 2211848 | tf_op jit(solution)/shard_map/ppermute | solution.py:633
  83.2 9.9 %collective-permute-start.16 = (bf16[2,96,768]{2,1,0:T(8,128)(2,1)S(1)}, bf16[2,96,768]{2,1,0:T(8,128)(2,1)S(1)}, u32[]{:S(2)}, u32[]{:S(2)}) collective-permute-start(bf16[2,96,768]{2,1,0:T(8,128)(2,1)S(1)} %get-tuple-element.261), channel_id=1, source_target_pairs={{0,8},{4,12},{8,0},{12,4},{16,24},{20,28},{24,16},{28,20},{1,9},{5... | collective-permute-start | bytes 884744 | tf_op jit(solution)/shard_map/ppermute | solution.py:664
  86.4 18.5 %collective-permute-start.24 = (bf16[4,96,768]{2,1,0:T(8,128)(2,1)S(1)}, bf16[4,96,768]{2,1,0:T(8,128)(2,1)S(1)}, u32[]{:S(2)}, u32[]{:S(2)}) collective-permute-start(bf16[4,96,768]{2,1,0:T(8,128)(2,1)S(1)} %get-tuple-element.185), channel_id=1, source_target_pairs={{0,4},{4,0},{8,12},{12,8},{16,20},{20,16},{24,28},{28,24},{1,5},{5... | collective-permute-start | bytes 1769480 | tf_op jit(solution)/shard_map/ppermute | solution.py:660
  87.4 14.8 %collective-permute-start.19 = (bf16[2,96,768]{2,1,0:T(8,128)(2,1)S(1)}, bf16[2,96,768]{2,1,0:T(8,128)(2,1)S(1)}, u32[]{:S(2)}, u32[]{:S(2)}) collective-permute-start(bf16[2,96,768]{2,1,0:T(8,128)(2,1)S(1)} %get-tuple-element.260), channel_id=1, source_target_pairs={{0,8},{4,12},{8,0},{12,4},{16,24},{20,28},{24,16},{28,20},{1,9},{5... | collective-permute-start | bytes 884744 | tf_op jit(solution)/shard_map/ppermute | solution.py:664
  93.2 9.1 %collective-permute-start.18 = (bf16[1,96,768]{2,1,0:T(8,128)(2,1)S(1)}, bf16[1,96,768]{2,1,0:T(8,128)(2,1)S(1)}, u32[]{:S(2)}, u32[]{:S(2)}) collective-permute-start(bf16[1,96,768]{2,1,0:T(8,128)(2,1)S(1)} %get-tuple-element.267), channel_id=1, source_target_pairs={{0,16},{4,20},{8,24},{12,28},{16,0},{20,4},{24,8},{28,12},{1,17},{... | collective-permute-start | bytes 442376 | tf_op jit(solution)/shard_map/ppermute | solution.py:668
  100.2 8.0 %collective-permute-start.23 = (bf16[576,640]{1,0:T(8,128)(2,1)S(1)}, bf16[576,640]{1,0:T(8,128)(2,1)S(1)}, u32[]{:S(2)}, u32[]{:S(2)}) collective-permute-start(bf16[576,640]{1,0:T(8,128)(2,1)S(1)} %collective-permute-done.20.dqkv_c), channel_id=1, source_target_pairs={{0,1},{1,0},{2,3},{3,2},{4,5},{5,4},{6,7},{7,6},{8,9},{9,8},{10,11... | collective-permute-start | bytes 2211848 | tf_op jit(solution)/shard_map/ppermute | solution.py:1558
  102.3 16.5 %collective-permute-start.26 = (bf16[1,96,768]{2,1,0:T(8,128)(2,1)S(1)}, bf16[1,96,768]{2,1,0:T(8,128)(2,1)S(1)}, u32[]{:S(2)}, u32[]{:S(2)}) collective-permute-start(bf16[1,96,768]{2,1,0:T(8,128)(2,1)S(1)} %add_convert_fusion.9), channel_id=1, source_target_pairs={{0,16},{4,20},{8,24},{12,28},{16,0},{20,4},{24,8},{28,12},{1,17},{... | collective-permute-start | bytes 442376 | tf_op jit(solution)/shard_map/ppermute | solution.py:668
  105.1 13.3 %collective-permute-start.21 = (bf16[1,96,768]{2,1,0:T(8,128)(2,1)S(1)}, bf16[1,96,768]{2,1,0:T(8,128)(2,1)S(1)}, u32[]{:S(2)}, u32[]{:S(2)}) collective-permute-start(bf16[1,96,768]{2,1,0:T(8,128)(2,1)S(1)} %get-tuple-element.266), channel_id=1, source_target_pairs={{0,16},{4,20},{8,24},{12,28},{16,0},{20,4},{24,8},{28,12},{1,17},{... | collective-permute-start | bytes 442376 | tf_op jit(solution)/shard_map/ppermute | solution.py:668
  105.6 13.1 %collective-permute-start.27 = (bf16[2,96,768]{2,1,0:T(8,128)(2,1)S(1)}, bf16[2,96,768]{2,1,0:T(8,128)(2,1)S(1)}, u32[]{:S(2)}, u32[]{:S(2)}) collective-permute-start(bf16[2,96,768]{2,1,0:T(8,128)(2,1)S(1)} %get-tuple-element.257), channel_id=1, source_target_pairs={{0,8},{4,12},{8,0},{12,4},{16,24},{20,28},{24,16},{28,20},{1,9},{5... | collective-permute-start | bytes 884744 | tf_op jit(solution)/shard_map/ppermute | solution.py:664
  118.9 5.8 %collective-permute-start.25 = (bf16[2,24,768]{2,1,0:T(8,128)(2,1)S(1)}, bf16[2,24,768]{2,1,0:T(8,128)(2,1)S(1)}, u32[]{:S(2)}, u32[]{:S(2)}) collective-permute-start(bf16[2,24,768]{2,1,0:T(8,128)(2,1)S(1)} %pad_maximum_fusion), channel_id=1, source_target_pairs={{0,1},{1,0},{2,3},{3,2},{4,5},{5,4},{6,7},{7,6},{8,9},{9,8},{10,11... | collective-permute-start | bytes 221192 | tf_op jit(solution)/shard_map/ppermute | solution.py:643
  119.0 11.0 %collective-permute-start.30 = (bf16[1,96,768]{2,1,0:T(8,128)(2,1)S(1)}, bf16[1,96,768]{2,1,0:T(8,128)(2,1)S(1)}, u32[]{:S(2)}, u32[]{:S(2)}) collective-permute-start(bf16[1,96,768]{2,1,0:T(8,128)(2,1)S(1)} %get-tuple-element.263), channel_id=1, source_target_pairs={{0,16},{4,20},{8,24},{12,28},{16,0},{20,4},{24,8},{28,12},{1,17},{... | collective-permute-start | bytes 442376 | tf_op jit(solution)/shard_map/ppermute | solution.py:668
  121.4 11.3 %collective-permute-start.33 = (bf16[2,96,768]{2,1,0:T(8,128)(2,1)S(1)}, bf16[2,96,768]{2,1,0:T(8,128)(2,1)S(1)}, u32[]{:S(2)}, u32[]{:S(2)}) collective-permute-start(bf16[2,96,768]{2,1,0:T(8,128)(2,1)S(1)} %constant_dynamic-update-slice_fusion), channel_id=1, source_target_pairs={{0,8},{4,12},{8,0},{12,4},{16,24},{20,28},{24,16},{28,20},{1,9},{5... | collective-permute-start | bytes 884744 | tf_op jit(solution)/shard_map/ppermute | solution.py:664
  124.0 15.3 %collective-permute-start.29 = (bf16[4,32,768]{2,1,0:T(8,128)(2,1)S(1)}, bf16[4,32,768]{2,1,0:T(8,128)(2,1)S(1)}, u32[]{:S(2)}, u32[]{:S(2)}) collective-permute-start(bf16[4,32,768]{2,1,0:T(8,128)(2,1)S(1)} %get-tuple-element.205), channel_id=1, source_target_pairs={{0,4},{4,0},{8,12},{12,8},{16,20},{20,16},{24,28},{28,24},{1,5},{5... | collective-permute-start | bytes 589832 | tf_op jit(solution)/shard_map/ppermute | solution.py:660
  124.7 5.1 %collective-permute-start.28 = (bf16[2,24,768]{2,1,0:T(8,128)(2,1)S(1)}, bf16[2,24,768]{2,1,0:T(8,128)(2,1)S(1)}, u32[]{:S(2)}, u32[]{:S(2)}) collective-permute-start(bf16[2,24,768]{2,1,0:T(8,128)(2,1)S(1)} %pad_maximum_fusion.1), channel_id=1, source_target_pairs={{0,2},{2,0},{1,3},{3,1},{4,6},{6,4},{5,7},{7,5},{8,10},{10,8},{9,1... | collective-permute-start | bytes 221192 | tf_op jit(solution)/shard_map/ppermute | solution.py:1580
  129.9 9.2 %collective-permute-start.31 = (bf16[1,96,768]{2,1,0:T(8,128)(2,1)S(1)}, bf16[1,96,768]{2,1,0:T(8,128)(2,1)S(1)}, u32[]{:S(2)}, u32[]{:S(2)}) collective-permute-start(bf16[1,96,768]{2,1,0:T(8,128)(2,1)S(1)} %maximum_bitcast_fusion), channel_id=1, source_target_pairs={{0,16},{4,20},{8,24},{12,28},{16,0},{20,4},{24,8},{28,12},{1,17},{... | collective-permute-start | bytes 442376 | tf_op jit(solution)/shard_map/ppermute | solution.py:668
  130.1 4.8 %collective-permute-start.32 = (bf16[2,24,576]{2,1,0:T(8,128)(2,1)S(1)}, bf16[2,24,576]{2,1,0:T(8,128)(2,1)S(1)}, u32[]{:S(2)}, u32[]{:S(2)}) collective-permute-start(bf16[2,24,576]{2,1,0:T(8,128)(2,1)S(1)} %pad_maximum_fusion.2), channel_id=1, source_target_pairs={{0,1},{1,0},{2,3},{3,2},{4,5},{5,4},{6,7},{7,6},{8,9},{9,8},{10,11... | collective-permute-start | bytes 165896 | tf_op jit(solution)/shard_map/ppermute | solution.py:643
  132.8 27.9 %collective-permute-start.39 = (bf16[4,96,768]{2,1,0:T(8,128)(2,1)S(1)}, bf16[4,96,768]{2,1,0:T(8,128)(2,1)S(1)}, u32[]{:S(2)}, u32[]{:S(2)}) collective-permute-start(bf16[4,96,768]{2,1,0:T(8,128)(2,1)S(1)} %constant_dynamic-update-slice_fusion.2.held), channel_id=1, source_target_pairs={{0,4},{4,0},{8,12},{12,8},{16,20},{20,16},{24,28},{28,24},{1,5},{5... | collective-permute-start | bytes 1769480 | tf_op jit(solution)/shard_map/ppermute | solution.py:660
  139.1 11.7 %collective-permute-start.34 = (bf16[2,96,768]{2,1,0:T(8,128)(2,1)S(1)}, bf16[2,96,768]{2,1,0:T(8,128)(2,1)S(1)}, u32[]{:S(2)}, u32[]{:S(2)}) collective-permute-start(bf16[2,96,768]{2,1,0:T(8,128)(2,1)S(1)} %constant_dynamic-update-slice_fusion.4), channel_id=1, source_target_pairs={{0,8},{4,12},{8,0},{12,4},{16,24},{20,28},{24,16},{28,20},{1,9},{5... | collective-permute-start | bytes 884744 | tf_op jit(solution)/shard_map/ppermute | solution.py:664
  139.4 4.3 %collective-permute-start.35 = (bf16[2,24,576]{2,1,0:T(8,128)(2,1)S(1)}, bf16[2,24,576]{2,1,0:T(8,128)(2,1)S(1)}, u32[]{:S(2)}, u32[]{:S(2)}) collective-permute-start(bf16[2,24,576]{2,1,0:T(8,128)(2,1)S(1)} %pad_maximum_fusion.3), channel_id=1, source_target_pairs={{0,2},{2,0},{1,3},{3,1},{4,6},{6,4},{5,7},{7,5},{8,10},{10,8},{9,1... | collective-permute-start | bytes 165896 | tf_op jit(solution)/shard_map/ppermute | solution.py:1593
  143.8 7.9 %collective-permute-start.37 = (bf16[1,96,768]{2,1,0:T(8,128)(2,1)S(1)}, bf16[1,96,768]{2,1,0:T(8,128)(2,1)S(1)}, u32[]{:S(2)}, u32[]{:S(2)}) collective-permute-start(bf16[1,96,768]{2,1,0:T(8,128)(2,1)S(1)} %maximum_bitcast_fusion.1), channel_id=1, source_target_pairs={{0,16},{4,20},{8,24},{12,28},{16,0},{20,4},{24,8},{28,12},{1,17},{... | collective-permute-start | bytes 442376 | tf_op jit(solution)/shard_map/ppermute | solution.py:668
  144.7 8.3 %collective-permute-start.40 = (bf16[2,32,768]{2,1,0:T(8,128)(2,1)S(1)}, bf16[2,32,768]{2,1,0:T(8,128)(2,1)S(1)}, u32[]{:S(2)}, u32[]{:S(2)}) collective-permute-start(bf16[2,32,768]{2,1,0:T(8,128)(2,1)S(1)} %get-tuple-element.269), channel_id=1, source_target_pairs={{0,8},{4,12},{8,0},{12,4},{16,24},{20,28},{24,16},{28,20},{1,9},{5... | collective-permute-start | bytes 294920 | tf_op jit(solution)/shard_map/ppermute | solution.py:664
  150.9 18.5 %collective-permute-start.36 = (bf16[4,96,768]{2,1,0:T(8,128)(2,1)S(1)}, bf16[4,96,768]{2,1,0:T(8,128)(2,1)S(1)}, u32[]{:S(2)}, u32[]{:S(2)}) collective-permute-start(bf16[4,96,768]{2,1,0:T(8,128)(2,1)S(1)} %constant_dynamic-update-slice_fusion.6.held), channel_id=1, source_target_pairs={{0,4},{4,0},{8,12},{12,8},{16,20},{20,16},{24,28},{28,24},{1,5},{5... | collective-permute-start | bytes 1769480 | tf_op jit(solution)/shard_map/ppermute | solution.py:660
  151.7 13.8 %collective-permute-start.38 = (bf16[2,96,768]{2,1,0:T(8,128)(2,1)S(1)}, bf16[2,96,768]{2,1,0:T(8,128)(2,1)S(1)}, u32[]{:S(2)}, u32[]{:S(2)}) collective-permute-start(bf16[2,96,768]{2,1,0:T(8,128)(2,1)S(1)} %constant_dynamic-update-slice_fusion.8), channel_id=1, source_target_pairs={{0,8},{4,12},{8,0},{12,4},{16,24},{20,28},{24,16},{28,20},{1,9},{5... | collective-permute-start | bytes 884744 | tf_op jit(solution)/shard_map/ppermute | solution.py:664
  153.0 5.2 %collective-permute-start.41 = (bf16[1,32,768]{2,1,0:T(8,128)(2,1)S(1)}, bf16[1,32,768]{2,1,0:T(8,128)(2,1)S(1)}, u32[]{:S(2)}, u32[]{:S(2)}) collective-permute-start(bf16[1,32,768]{2,1,0:T(8,128)(2,1)S(1)} %get-tuple-element.280), channel_id=1, source_target_pairs={{0,16},{4,20},{8,24},{12,28},{16,0},{20,4},{24,8},{28,12},{1,17},{... | collective-permute-start | bytes 147464 | tf_op jit(solution)/shard_map/ppermute | solution.py:668
  158.2 5.2 %collective-permute-start.42 = (bf16[1,32,768]{2,1,0:T(8,128)(2,1)S(1)}, bf16[1,32,768]{2,1,0:T(8,128)(2,1)S(1)}, u32[]{:S(2)}, u32[]{:S(2)}) collective-permute-start(bf16[1,32,768]{2,1,0:T(8,128)(2,1)S(1)} %add_convert_fusion.11), channel_id=1, source_target_pairs={{0,16},{4,20},{8,24},{12,28},{16,0},{20,4},{24,8},{28,12},{1,17},{... | collective-permute-start | bytes 147464 | tf_op jit(solution)/shard_map/ppermute | solution.py:668
  163.4 4.7 %collective-permute-start.43 = (bf16[2,32,768]{2,1,0:T(8,128)(2,1)S(1)}, bf16[2,32,768]{2,1,0:T(8,128)(2,1)S(1)}, u32[]{:S(2)}, u32[]{:S(2)}) collective-permute-start(bf16[2,32,768]{2,1,0:T(8,128)(2,1)S(1)} %constant_dynamic-update-slice_fusion.10), channel_id=1, source_target_pairs={{0,8},{4,12},{8,0},{12,4},{16,24},{20,28},{24,16},{28,20},{1,9},{5... | collective-permute-start | bytes 294920 | tf_op jit(solution)/shard_map/ppermute | solution.py:664
  165.5 12.7 %collective-permute-start.45 = (bf16[4,96,768]{2,1,0:T(8,128)(2,1)S(1)}, bf16[4,96,768]{2,1,0:T(8,128)(2,1)S(1)}, u32[]{:S(2)}, u32[]{:S(2)}) collective-permute-start(bf16[4,96,768]{2,1,0:T(8,128)(2,1)S(1)} %constant_dynamic-update-slice_fusion.12.held), channel_id=1, source_target_pairs={{0,4},{4,0},{8,12},{12,8},{16,20},{20,16},{24,28},{28,24},{1,5},{5... | collective-permute-start | bytes 1769480 | tf_op jit(solution)/shard_map/ppermute | solution.py:660
  168.1 12.3 %collective-permute-start.44 = (bf16[4,32,768]{2,1,0:T(8,128)(2,1)S(1)}, bf16[4,32,768]{2,1,0:T(8,128)(2,1)S(1)}, u32[]{:S(2)}, u32[]{:S(2)}) collective-permute-start(bf16[4,32,768]{2,1,0:T(8,128)(2,1)S(1)} %constant_dynamic-update-slice_fusion.14.held), channel_id=1, source_target_pairs={{0,4},{4,0},{8,12},{12,8},{16,20},{20,16},{24,28},{28,24},{1,5},{5... | collective-permute-start | bytes 589832 | tf_op jit(solution)/shard_map/ppermute | solution.py:660
  (28 other events, 210.0 us)
